TPU v7x, 512 devices: a whole 4x8x8 slice. The times are simulated.
512 devices in a mesh: dp: 8 (over x, y_hi), ctx: 64 (over y_lo, z, core).
Axes of the slice: x: 4, y: 8 (y_hi: 2, y_lo: 4; y = y_hi * 4 + y_lo), z: 8, core: 2. Of those that a mesh axis runs over, the one named last changes fastest.
Arguments:
- gated_input: bfloat16 [8, 49152, 1024], P('dp', 'ctx'), may hold values from -6 to 6
- upstream: bfloat16 [8, 49152, 1024], P('dp', 'ctx'), may hold values from -6 to 6
- depth_kernel: float32 [31, 1024], replicated, may hold values from -1 to 1
- carried_error: float32 [8, 1024, 1024], P('dp', 'ctx'), may hold values from -6 to 6
- right_init: float32 [1024, 64], replicated, may hold values from -6 to 6
Outputs:
- right_factor: float32 [1024, 64], replicated
- estimate: float32 [1024, 1024], P('ctx')
- updated_error: float32 [8, 1024, 1024], P('dp', 'ctx')
All inputs are finite; a program needn't handle non-finite values.
Results may differ from a plain program's by a relative error of at most 0.0019.
Values may be sent and summed in bfloat16 or wider, within the bound.
No kernel may reach another device: no remote copies, remote signals or barrier semaphores. Data moves between devices by JAX's collectives and lax.ppermute only.
A program may use at most 64 MiB of HBM per device.

v0:
```python
import math

import jax
import jax.numpy as jnp
from jax import lax
from jax.sharding import PartitionSpec as P


def extended(block, sides, width):
    for axis, dim in sides:
        count = lax.axis_size(axis)
        forward = [(i, i + 1) for i in range(count - 1)]
        backward = [(target, source) for source, target in forward]
        low = lax.ppermute(
            lax.slice_in_dim(block, block.shape[dim] - width, None, axis=dim), axis, forward
        )
        high = lax.ppermute(lax.slice_in_dim(block, 0, width, axis=dim), axis, backward)
        block = jnp.concatenate([low, block, high], axis=dim)
    return block


def local(gated_input, upstream, depth_kernel, carried_error, right_init):
    ctx_count = lax.axis_size("ctx")
    replicas = lax.axis_size("dp")
    frame_count = gated_input.shape[1]
    taps = depth_kernel.shape[0]
    rim_width = (taps - 1) // 2
    padded = extended(gated_input, (("ctx", 1),), rim_width)
    widened = padded[0].astype(jnp.float32)
    summed = jnp.zeros((frame_count, gated_input.shape[2]), jnp.float32)
    for tap_index in range(taps):
        summed = summed + depth_kernel[tap_index] * widened[tap_index : tap_index + frame_count]
    activation = (summed * jax.nn.sigmoid(summed)).astype(jnp.bfloat16)
    signal = upstream[0]
    inverse_root = 1.0 / math.sqrt(frame_count * ctx_count)
    highest = lax.Precision.HIGHEST
    gradient_rows = lax.psum_scatter(
        lax.dot_general(
            activation, signal, (((0,), (0,)), ((), ())), preferred_element_type=jnp.float32
        ),
        "ctx",
        scatter_dimension=0,
        tiled=True,
    )
    merged = gradient_rows * inverse_root + carried_error[0]
    left_local = jnp.dot(merged, right_init, precision=highest)
    left_rows = lax.psum(left_local, "dp")
    gram_matrix = lax.psum(jnp.dot(left_rows.T, left_rows, precision=highest), "ctx")
    factor = jnp.linalg.cholesky(gram_matrix)
    left_hat_rows = lax.linalg.triangular_solve(
        factor, left_rows, left_side=False, lower=True, transpose_a=True
    )
    right_term = jnp.dot(merged.T, left_hat_rows, precision=highest)
    right_factor = lax.psum(right_term, ("dp", "ctx")) / replicas
    estimate = jnp.dot(left_hat_rows, right_factor.T, precision=highest)
    updated_error = merged - estimate
    return (right_factor, estimate, updated_error[None])


def solution(mesh):
    return jax.shard_map(
        local,
        mesh=mesh,
        in_specs=(P("dp", "ctx", None), P("dp", "ctx", None), P(), P("dp", "ctx", None), P()),
        out_specs=(P(), P("ctx", None), P("dp", "ctx", None)),
        check_vma=False,
    )
```

profile of v0, /device:TPU:1, one launch (start us, length us, event | category | flops | bytes accessed | tf_op | source)
XLA Modules:
  0.0 948.6 jit_solution(5753601036791976680)
XLA Ops:
  7.2 0.9 fusion.70
  8.1 5.4 collective-permute-start
  13.5 4.7 collective-permute-start.1
  18.2 1.4 fusion.71
  19.6 1.1 fusion.72
  20.8 3.6 maximum_convert_fusion
  24.4 58.7 %fusion.61 = f32[1024,1024]{1,0:T(8,128)} fusion(bf16[1,768,1024]{2,1,0:T(8,128)(2,1)S(1)} %copy-done, f32[1,798,1024]{2,1,0:T(8,128)} %maximum_convert_fusion, f32[1024]{0:T(1024)S(1)} %bitcast.424, f32[1024]{0:T(1024)S(1)} %bitcast.425, f32[1024]{0:T(1024)S(1)} %bitcast.396, f32[1024]{0:T(1024)S(1)} %bitcast.397, f32[1024]{0:T(1024)S(1)} %bitcast.398, ...), kind=kOutput, calls=%fused_computation.94 | convolution fusion | flops 1662517248 | bytes 103411712 | tf_op jit(solution)/shard_map/dot_general | solution.py:38
  83.2 0.0 all-reduce.2.cloned.1.call-start
  83.3 283.8 %reduce-scatter.2.cloned.1.call-done = f32[16,1024]{1,0:T(8,128)} async-done(((f32[1024,1024]{1,0:T(8,128)}), f32[16,1024]{1,0:T(8,128)}) %reduce-scatter.2.cloned.1.call-update) | async-done | bytes 65552 | tf_op jit(solution)/shard_map/reduce_scatter | solution.py:37
  367.1 1.1 fusion.69
  368.2 26.6 %psum.21 = f32[16,64]{1,0:T(8,128)S(1)} all-reduce(f32[16,64]{1,0:T(8,128)S(1)} %fusion.69), channel_id=1, replica_groups=mesh['dp'=8,'ctx'=64] {'dp'}, use_global_device_ids=true, to_apply=%region_1.0 | all-reduce | flops 1024 | bytes 8192 | tf_op jit(solution)/shard_map/psum | solution.py:47
  394.9 0.2 fusion.73
  395.1 266.9 %psum.22 = f32[64,64]{0,1:T(8,128)S(1)} all-reduce(f32[64,64]{0,1:T(8,128)S(1)} %fusion.73), channel_id=1, replica_groups=mesh['dp'=8,'ctx'=64] {'ctx'}, use_global_device_ids=true, to_apply=%region_2.0 | all-reduce | flops 4096 | bytes 32768 | tf_op jit(solution)/shard_map/psum | solution.py:48
  662.0 0.1 copy.9
  662.1 5.8 cholesky.16
  667.9 0.6 compare_reduce_fusion
  668.6 0.7 fusion.63
  669.3 4.9 custom-call.6
  674.1 0.2 fusion.64
  674.3 2.0 fusion.68
  676.3 262.7 %all-reduce.2.cloned.1.call-done = f32[1024,64]{0,1:T(8,128)} async-done(((f32[1024,64]{0,1:T(8,128)}), f32[1024,64]{0,1:T(8,128)}) %all-reduce.2.cloned.1.call-update) | async-done | bytes 262160 | tf_op jit(solution)/shard_map/psum | solution.py:54
  939.0 1.0 broadcast_multiply_fusion
  940.0 0.2 fusion.74
  940.3 1.5 subtract_bitcast_fusion
  (17 shorter events, 0.2 us)
Async XLA Ops:
  7.2 17.2 %copy-start = (bf16[1,768,1024]{2,1,0:T(8,128)(2,1)S(1)}, bf16[1,768,1024]{2,1,0:T(8,128)(2,1)}, u32[]{:S(2)}) copy-start(bf16[1,768,1024]{2,1,0:T(8,128)(2,1)} %param.6) | copy-start | bytes 4718596
  7.2 359.9 %reduce-scatter.2.cloned.1.call-start = ((), (), s32[]{:S(2)}) async-start(), calls=%async_computation.1 | async-start | bytes 4259840 | tf_op jit(solution)/shard_map/reduce_scatter | solution.py:37
  8.1 12.7 %collective-permute-start = (bf16[1,15,1024]{2,1,0:T(8,128)(2,1)S(1)}, bf16[1,15,1024]{2,1,0:T(8,128)(2,1)S(1)}, u32[]{:S(2)}, u32[]{:S(2)}) collective-permute-start(bf16[1,15,1024]{2,1,0:T(8,128)(2,1)S(1)} %get-tuple-element.3), channel_id=1, source_target_pairs={{0,1},{1,2},{2,3},{3,4},{4,5},{5,6},{6,7},{7,8},{8,9},{9,10},{10,1... | collective-permute-start | bytes 92168 | tf_op jit(solution)/shard_map/ppermute | solution.py:14
  13.5 7.3 collective-permute-start.1
  83.2 283.9 %copy-start.2 = (f32[1,16,1024]{2,1,0:T(8,128)S(1)}, f32[1,16,1024]{2,1,0:T(8,128)}, u32[]{:S(2)}) copy-start(f32[1,16,1024]{2,1,0:T(8,128)} %param.8) | copy-start | bytes 196612
  83.2 283.9 %copy-start.3 = (f32[1024,64]{0,1:T(8,128)S(1)}, f32[1024,64]{0,1:T(8,128)}, u32[]{:S(2)}) copy-start(f32[1024,64]{0,1:T(8,128)} %param.9) | copy-start | bytes 786436
  83.2 855.8 %all-reduce.2.cloned.1.call-start = ((), (), s32[]{:S(2)}) async-start(), calls=%async_computation.2 | async-start | bytes 524288 | tf_op jit(solution)/shard_map/psum | solution.py:54
  940.0 1.8 copy-start.1
  940.2 1.5 copy-start.4
Sparse Core Ops, SparseCore 0:
  83.3 283.7 reduce-scatter.1
  676.4 262.5 all-reduce.1
where the time goes:
time: 949 us
  waiting for transfers between devices  547 us (58%)
  blocking collectives  294 us (31%)
  matrix products  62.5 us (7%)
  other arithmetic  18.2 us (2%)
  between operations  14.2 us (1%)
  starting transfers between devices  10.2 us (1%)
    reduce_scatter x1, waiting for transfers between devices, local(): lax.psum_scatter(lax.dot_general(activation, signal, (((0,), (0,)), ((),...  284 us
    psum x1, blocking collectives, local(): lax.psum(jnp.dot(left_rows.T, left_rows, precision=highest), 'ctx')  267 us
    psum x1, waiting for transfers between devices, local(): right_factor = lax.psum(right_term, ('dp', 'ctx')) / replicas  263 us
    dot_general x1, matrix products, local(): lax.dot_general(activation, signal, (((0,), (0,)), ((), ())), preferred_e...  58.7 us
    psum x1, blocking collectives, local(): left_rows = lax.psum(left_local, 'dp')  26.6 us
  transfers between devices with their start and end apart: 4, of which 2 were waited for; matrix products, arithmetic and copies ran while one was open for 0% of the time, Pallas kernels for 0%

commit v1 on v0

v1 whole, which is shorter than its diff:
```python
import functools
import math

import jax
import jax.numpy as jnp
from jax import lax
from jax.experimental import pallas as pl
from jax.experimental.pallas import tpu as pltpu
from jax.sharding import Mesh, PartitionSpec as P

F32 = jnp.float32
BF16 = jnp.bfloat16
HIGHEST = lax.Precision.HIGHEST
DP = ("x", "h")
CTX = ("y", "z", "c")
CHIPS = ("y", "z")
NEAR = ("x", "z")
FAR = ("h", "y", "c")
RIM = 16
BLOCK = 256
STEP = 96
PARAMS = pltpu.CompilerParams(vmem_limit_bytes=48 << 20)


def conv_kernel(core_ref, x_ref, low_ref, high_ref, taps_ref, up_ref, keep_ref, send_ref, wide_ref, act_ref):
    frames, width = x_ref.shape
    wide_ref[0:RIM] = low_ref[...].astype(F32)
    wide_ref[RIM : RIM + frames] = x_ref[...].astype(F32)
    wide_ref[RIM + frames :] = high_ref[...].astype(F32)
    for lane in range(0, width, 128):
        cols = slice(lane, lane + 128)

        def chunk(index, _):
            base = pl.multiple_of(index * STEP, STEP)
            rows = wide_ref[pl.ds(base, STEP + 2 * RIM), cols]
            total = None
            for shift in range(8):
                part = None
                for tile in range(4):
                    tap = 8 * tile + shift
                    if tap == 0:
                        continue
                    term = taps_ref[tap : tap + 1, cols] * rows[8 * tile : 8 * tile + STEP + 8]
                    part = term if part is None else part + term
                if shift:
                    part = pltpu.roll(part, STEP + 8 - shift, 0)
                part = part[:STEP]
                total = part if total is None else total + part
            half = 0.5 * total
            act_ref[pl.ds(base, STEP), cols] = (half + half * jnp.tanh(half)).astype(BF16)
            return 0

        lax.fori_loop(0, frames // STEP, chunk, 0)
    product = lax.dot_general(
        act_ref[...], up_ref[...], (((0,), (0,)), ((), ())), preferred_element_type=F32
    )
    pieces = product.reshape(width // 32, 2, 16, product.shape[1])
    first = pieces[:, 0].reshape(width // 2, -1)
    second = pieces[:, 1].reshape(width // 2, -1)

    @pl.when(core_ref[0] == 0)
    def _():
        keep_ref[...] = first
        send_ref[...] = second

    @pl.when(core_ref[0] == 1)
    def _():
        keep_ref[...] = second
        send_ref[...] = first


def conv_product(core, block, low, high, taps, signal):
    frames, channels = block.shape
    features = signal.shape[1]
    half = jax.ShapeDtypeStruct((channels // 2, features), F32)
    column = lambda rows: pl.BlockSpec((rows, BLOCK), lambda i: (0, i))
    return pl.pallas_call(
        conv_kernel,
        grid=(channels // BLOCK,),
        in_specs=[
            pl.BlockSpec(memory_space=pltpu.SMEM),
            column(frames),
            column(RIM),
            column(RIM),
            column(taps.shape[0]),
            pl.BlockSpec((frames, features), lambda i: (0, 0)),
        ],
        out_specs=[pl.BlockSpec((BLOCK // 2, features), lambda i: (i, 0))] * 2,
        out_shape=[half, half],
        scratch_shapes=[pltpu.VMEM((frames + 2 * RIM, BLOCK), F32), pltpu.VMEM((frames, BLOCK), BF16)],
        compiler_params=PARAMS,
        name="conv_product",
    )(core, block, low, high, taps, signal)


def merge_kernel(inverse_root, parts_ref, carried_ref, right_ref, merged_ref, left_ref):
    total = parts_ref[0].astype(F32)
    for index in range(1, parts_ref.shape[0]):
        total = total + parts_ref[index].astype(F32)
    merged = total * inverse_root + carried_ref[...]
    merged_ref[...] = merged
    left = lax.dot_general(
        merged, right_ref[...], (((1,), (1,)), ((), ())), precision=HIGHEST, preferred_element_type=F32
    )
    for index in range(left_ref.shape[0]):
        left_ref[index] = left


def term_kernel(parts_ref, merged_ref, left_ref, term_ref):
    left = parts_ref[0]
    for index in range(1, parts_ref.shape[0]):
        left = left + parts_ref[index]
    left_ref[...] = left
    share = left * (1.0 / parts_ref.shape[0])
    joined = jnp.concatenate([merged_ref[...], jnp.zeros_like(left), share], axis=1)
    term = lax.dot_general(
        left, joined, (((0,), (0,)), ((), ())), precision=HIGHEST, preferred_element_type=F32
    )
    for index in range(term_ref.shape[0]):
        term_ref[index] = term[2 * index : 2 * index + 2]


def total_kernel(parts_ref, total_ref):
    total = parts_ref[0]
    for index in range(1, parts_ref.shape[0]):
        total = total + parts_ref[index]
    for index in range(total_ref.shape[0]):
        total_ref[index] = total


def finish_kernel(replicas, rows_ref, left_ref, merged_ref, right_ref, estimate_ref, error_ref, wide_ref):
    rank = left_ref.shape[1]
    features = merged_ref.shape[1]
    for index in range(rows_ref.shape[0]):
        wide_ref[2 * index : 2 * index + 2] = rows_ref[index]
    row = lax.broadcasted_iota(jnp.int32, (rank, 2 * rank), 0)
    lane = lax.broadcasted_iota(jnp.int32, (rank, 2 * rank), 1)
    work = wide_ref[:, features:] + (row == lane).astype(F32)
    for step in range(rank - 1):
        column = work[:, rank + step : rank + step + 1]
        pivot_row = work[step : step + 1]
        scaled = pivot_row / pivot_row[:, rank + step : rank + step + 1]
        work = work - jnp.where(row > step, column, 0.0) * scaled
    pivots = jnp.sum(jnp.where(row + rank == lane, work, 0.0), axis=1, keepdims=True)
    inverse = (work * (1.0 / jnp.sqrt(pivots)))[:, :rank]
    dot = functools.partial(lax.dot_general, precision=HIGHEST, preferred_element_type=F32)
    right = dot(inverse, wide_ref[:, :features], (((1,), (0,)), ((), ()))) * (1.0 / replicas)
    right_ref[...] = right
    left_hat = dot(left_ref[...], inverse, (((1,), (1,)), ((), ())))
    estimate = dot(left_hat, right, (((1,), (0,)), ((), ())))
    estimate_ref[...] = estimate
    error_ref[...] = merged_ref[...] - estimate


def call(kernel, outs, *args, scratch=()):
    return pl.pallas_call(
        kernel,
        out_shape=[jax.ShapeDtypeStruct(shape, F32) for shape in outs],
        scratch_shapes=list(scratch),
        compiler_params=PARAMS,
        name=getattr(kernel, "func", kernel).__name__,
    )(*args)


def exchange(block, axes):
    return lax.all_to_all(block, axes, 0, 0, tiled=True)


def local(gated_input, upstream, depth_kernel, carried_error, right_init):
    replicas = lax.axis_size(DP)
    contexts = lax.axis_size(CTX)
    chips = lax.axis_size(CHIPS)
    near, far = lax.axis_size(NEAR), lax.axis_size(FAR)
    block = gated_input[0]
    frames, channels = block.shape
    features = upstream.shape[2]
    rank = right_init.shape[1]
    owned = channels // contexts
    forward = [(i, i + 1) for i in range(contexts - 1)]
    backward = [(target, source) for source, target in forward]
    low = lax.ppermute(block[frames - RIM :], CTX, forward)
    high = lax.ppermute(block[:RIM], CTX, backward)
    taps = jnp.pad(depth_kernel, ((1, 0), (0, 0)))
    core = lax.axis_index("c").reshape(1)
    keep, send = conv_product(core, block, low, high, taps, upstream[0])
    received = lax.ppermute(send, "c", [(0, 1), (1, 0)])
    pair_sum = (keep + received).astype(BF16)
    parts = exchange(pair_sum, CHIPS).reshape(chips, owned, features)
    inverse_root = 1.0 / math.sqrt(frames * contexts)
    merged, left_parts = call(
        functools.partial(merge_kernel, inverse_root),
        [(owned, features), (replicas, owned, rank)],
        parts,
        carried_error[0],
        right_init.T,
    )
    left_parts = exchange(left_parts, DP)
    width = features + 2 * rank
    pair = rank // near
    left, term = call(term_kernel, [(owned, rank), (near, pair, width)], left_parts, merged)
    (near_sum,) = call(total_kernel, [(far, pair, width)], exchange(term, NEAR))
    (far_sum,) = call(total_kernel, [(near, pair, width)], exchange(near_sum, FAR))
    right, estimate, error = call(
        functools.partial(finish_kernel, replicas),
        [(rank, features), (owned, features), (owned, features)],
        exchange(far_sum, NEAR),
        left,
        merged,
        scratch=[pltpu.VMEM((rank, width), F32)],
    )
    return right.T, estimate, error[None]


def solution(mesh):
    wide = Mesh(mesh.devices.reshape(4, 2, 4, 8, 2), ("x", "h", "y", "z", "c"))
    return jax.shard_map(
        local,
        mesh=wide,
        in_specs=(P(DP, CTX, None), P(DP, CTX, None), P(), P(DP, CTX, None), P()),
        out_specs=(P(), P(CTX, None), P(DP, CTX, None)),
        check_vma=False,
    )
```

time: 949 us -> 148 us (0.16)
  waiting for transfers between devices: 547 us -> 4.16 us
  blocking collectives: 294 us -> 102 us
  matrix products: 62.5 us -> 0 us
  Pallas kernels: 0 us -> 21.8 us
  other arithmetic: 18.2 us -> 1.22 us
  between operations: 14.2 us -> 0.74 us
    psum x2 -> x0, blocking collectives: 294 us -> none  [the longest x1 267 us: local(): lax.psum(jnp.dot(left_rows.T, left_rows, precision=highest), 'ctx')]
    reduce_scatter x1 -> x0, waiting for transfers between devices: 284 us -> none  [local(): lax.psum_scatter(lax.dot_general(activation, signal, (((0,), (0,)), ((),...]
    psum x1 -> x0, waiting for transfers between devices: 263 us -> none  [local(): right_factor = lax.psum(right_term, ('dp', 'ctx')) / replicas]
    all_to_all x0 -> x5, blocking collectives: none -> 102 us  [exchange(): return lax.all_to_all(block, axes, 0, 0, tiled=True)]
    dot_general x5 -> x0, matrix products: 62.3 us -> none  [the longest x1 58.7 us: local(): lax.dot_general(activation, signal, (((0,), (0,)), ((), ())), preferred_e...]
    pallas_call x0 -> x6, Pallas kernels: none -> 21.8 us  [the longest x1 14.2 us: conv_product(): pl.pallas_call(conv_kernel, grid=(channels // BLOCK,), in_specs=[pl.Block...]
    another operation x5 -> x0, other arithmetic: 12.1 us -> none  [the longest x3 6.52 us: local(): factor = jnp.linalg.cholesky(gram_matrix)]
  transfers between devices with their start and end apart: 4 -> 3, of which waited for: 2 -> 1; matrix products, arithmetic and copies ran while one was open for 0% -> 1% of each run, Pallas kernels for 0% -> 0%
where the time goes in v1:
time: 148 us; the launch traced here: 147 us
  blocking collectives  102 us (69%)
  Pallas kernels  21.8 us (15%)
  starting transfers between devices  12.2 us (8%)
  local copies, waits for them, and re-layouts  5.23 us (4%)
  waiting for transfers between devices  4.16 us (3%)
    all_to_all x5, blocking collectives, exchange(): return lax.all_to_all(block, axes, 0, 0, tiled=True)  102 us
    pallas_call x1, Pallas kernels, conv_product(): pl.pallas_call(conv_kernel, grid=(channels // BLOCK,), in_specs=[pl.Block...  14.2 us
    pallas_call x5, Pallas kernels, call(): pl.pallas_call(kernel, out_shape=[jax.ShapeDtypeStruct(shape, F32) for sh...  7.6 us
    ppermute x1, starting transfers between devices, local(): low = lax.ppermute(block[frames - RIM:], CTX, forward)  5.38 us
    ppermute x1, starting transfers between devices, local(): high = lax.ppermute(block[:RIM], CTX, backward)  4.69 us
    ppermute x1, waiting for transfers between devices, local(): received = lax.ppermute(send, 'c', [(0, 1), (1, 0)])  4.15 us
    unnamed x10, local copies, waits for them, and re-layouts  3.02 us
  transfers between devices with their start and end apart: 3, of which 1 were waited for; matrix products, arithmetic and copies ran while one was open for 1% of the time, Pallas kernels for 0%

profile of v1, /device:TPU:1, one launch (start us, length us, event | category | flops | bytes accessed | tf_op | source)
XLA Modules:
  0.0 147.1 jit_solution(8329620994323832486)
XLA Ops:
  0.6 0.8 slice_bitcast_fusion
  1.4 5.4 %collective-permute-start = (bf16[16,1024]{1,0:T(8,128)(2,1)S(1)}, bf16[16,1024]{1,0:T(8,128)(2,1)S(1)}, u32[]{:S(2)}, u32[]{:S(2)}) collective-permute-start(bf16[16,1024]{1,0:T(8,128)(2,1)S(1)} %get-tuple-element.22), channel_id=1, source_target_pairs={{0,1},{1,2},{2,3},{3,4},{4,5},{5,6},{6,7},{7,8},{8,9},{9,10},{10,1... | collective-permute-start | bytes 98312 | tf_op jit(solution)/shard_map/ppermute | solution.py:181
  6.8 4.7 %collective-permute-start.1 = (bf16[16,1024]{1,0:T(8,128)(2,1)S(1)}, bf16[16,1024]{1,0:T(8,128)(2,1)S(1)}, u32[]{:S(2)}, u32[]{:S(2)}) collective-permute-start(bf16[16,1024]{1,0:T(8,128)(2,1)S(1)} %get-tuple-element.21), channel_id=1, source_target_pairs={{1,0},{2,1},{3,2},{4,3},{5,4},{6,5},{7,6},{8,7},{9,8},{10,9},{11,1... | collective-permute-start | bytes 98312 | tf_op jit(solution)/shard_map/ppermute | solution.py:182
  11.5 0.9 pad.4.taps_ref
  12.4 0.0 copy-start
  12.5 1.4 copy-done
  13.9 1.4 copy-done.1
  15.3 14.2 %conv_product.1 = (f32[512,1024]{1,0:T(8,128)S(1)}, f32[512,1024]{1,0:T(8,128)}) custom-call(s32[1]{0:T(128)} %bitcast.core_ref, bf16[768,1024]{1,0:T(8,128)(2,1)S(1)} %bitcast.12, bf16[16,1024]{1,0:T(8,128)(2,1)S(1)} %collective-permute-done.low_ref, bf16[16,1024]{1,0:T(8,128)(2,1)S(1)} %collective-permute-done.1.high_ref, f32[32,1024]{1,0:T(8,128)S(1)} %pad.4.taps_ref, ...), custom_call_target="tpu_custom_call" | custom-call | tf_op jit(solution)/shard_map/conv_product/pallas_call | solution.py:77
  29.4 2.1 %collective-permute-start.2 = (f32[512,1024]{1,0:T(8,128)}, f32[512,1024]{1,0:T(8,128)S(1)}, u32[]{:S(2)}, u32[]{:S(2)}) collective-permute-start(f32[512,1024]{1,0:T(8,128)} %get-tuple-element.13), channel_id=1, source_target_pairs={{0,1},{1,0},{2,3},{3,2},{4,5},{5,4},{6,7},{7,6},{8,9},{9,8},{10,11... | collective-permute-start | bytes 6291464 | tf_op jit(solution)/shard_map/ppermute | solution.py:186
  31.5 4.2 %collective-permute-done.2 = f32[512,1024]{1,0:T(8,128)S(1)} collective-permute-done((f32[512,1024]{1,0:T(8,128)}, f32[512,1024]{1,0:T(8,128)S(1)}, u32[]{:S(2)}, u32[]{:S(2)}) %collective-permute-start.2) | collective-permute-done | bytes 2097184 | tf_op jit(solution)/shard_map/ppermute | solution.py:186
  35.7 0.5 add_convert_fusion
  36.2 0.0 copy-start.2
  36.2 38.2 %all_to_all.29.parts_ref = bf16[32,16,1024]{2,1,0:T(8,128)(2,1)S(1)} all-to-all(bf16[32,16,1024]{2,1,0:T(8,128)(2,1)S(1)} %bitcast.16), channel_id=1, replica_groups=mesh['x'=4,'h'=2,'y'=4,'z'=8,'c'=2] {'y','z'}, dimensions={0} | all-to-all | bytes 2097152 | tf_op jit(solution)/shard_map/all_to_all | solution.py:166
  74.4 0.4 merge_kernel.1
  74.8 0.1 reshape.16
  75.0 15.6 %all_to_all.30 = f32[8,1,1024]{2,1,0:T(1,128)S(1)} all-to-all(f32[8,1,1024]{2,1,0:T(1,128)S(1)} %reshape.16), channel_id=1, replica_groups=mesh['x'=4,'h'=2,'y'=4,'z'=8,'c'=2] {'x','h'}, dimensions={0} | all-to-all | bytes 65536 | tf_op jit(solution)/shard_map/all_to_all | solution.py:166
  90.5 0.5 broadcast.2
  91.0 0.7 reduce
  91.8 0.1 reshape.17.parts_ref
  91.8 0.4 term_kernel.1
  92.3 16.2 %all_to_all.31.parts_ref = f32[32,2,1152]{2,1,0:T(2,128)S(1)} all-to-all(f32[32,2,1152]{2,1,0:T(2,128)S(1)} %get-tuple-element.16), channel_id=1, replica_groups=mesh['x'=4,'h'=2,'y'=4,'z'=8,'c'=2] {'x','z'}, dimensions={0} | all-to-all | bytes 589824 | tf_op jit(solution)/shard_map/all_to_all | solution.py:166
  108.5 16.8 %all_to_all.32.parts_ref = f32[16,2,1152]{2,1,0:T(2,128)S(1)} all-to-all(f32[16,2,1152]{2,1,0:T(2,128)S(1)} %total_kernel.2), channel_id=1, replica_groups=mesh['x'=4,'h'=2,'y'=4,'z'=8,'c'=2] {'h','y','c'}, dimensions={0} | all-to-all | bytes 294912 | tf_op jit(solution)/shard_map/all_to_all | solution.py:166
  125.3 15.1 %all_to_all.33.rows_ref = f32[32,2,1152]{2,1,0:T(2,128)S(1)} all-to-all(f32[32,2,1152]{2,1,0:T(2,128)S(1)} %total_kernel.3), channel_id=1, replica_groups=mesh['x'=4,'h'=2,'y'=4,'z'=8,'c'=2] {'x','z'}, dimensions={0} | all-to-all | bytes 589824 | tf_op jit(solution)/shard_map/all_to_all | solution.py:166
  140.4 6.7 %finish_kernel.1 = (f32[64,1024]{1,0:T(8,128)}, f32[16,1024]{1,0:T(8,128)}, f32[16,1024]{1,0:T(8,128)}) custom-call(f32[32,2,1152]{2,1,0:T(2,128)S(1)} %all_to_all.33.rows_ref, f32[16,64]{1,0:T(8,128)S(1)} %get-tuple-element.17.left_ref, f32[16,1024]{1,0:T(8,128)S(1)} %get-tuple-element.15.merged_ref), custom_call_target="tpu_custom_call" | custom-call | tf_op jit(solution)/shard_map/finish_kernel/pallas_call | solution.py:156
  (8 shorter events, 0.1 us)
Async XLA Ops:
  1.4 11.0 %collective-permute-start = (bf16[16,1024]{1,0:T(8,128)(2,1)S(1)}, bf16[16,1024]{1,0:T(8,128)(2,1)S(1)}, u32[]{:S(2)}, u32[]{:S(2)}) collective-permute-start(bf16[16,1024]{1,0:T(8,128)(2,1)S(1)} %get-tuple-element.22), channel_id=1, source_target_pairs={{0,1},{1,2},{2,3},{3,4},{4,5},{5,6},{6,7},{7,8},{8,9},{9,10},{10,1... | collective-permute-start | bytes 98312 | tf_op jit(solution)/shard_map/ppermute | solution.py:181
  6.8 5.6 %collective-permute-start.1 = (bf16[16,1024]{1,0:T(8,128)(2,1)S(1)}, bf16[16,1024]{1,0:T(8,128)(2,1)S(1)}, u32[]{:S(2)}, u32[]{:S(2)}) collective-permute-start(bf16[16,1024]{1,0:T(8,128)(2,1)S(1)} %get-tuple-element.21), channel_id=1, source_target_pairs={{1,0},{2,1},{3,2},{4,3},{5,4},{6,5},{7,6},{8,7},{9,8},{10,9},{11,1... | collective-permute-start | bytes 98312 | tf_op jit(solution)/shard_map/ppermute | solution.py:182
  12.4 1.4 copy-start
  13.9 1.4 copy-start.1
  29.4 6.3 %collective-permute-start.2 = (f32[512,1024]{1,0:T(8,128)}, f32[512,1024]{1,0:T(8,128)S(1)}, u32[]{:S(2)}, u32[]{:S(2)}) collective-permute-start(f32[512,1024]{1,0:T(8,128)} %get-tuple-element.13), channel_id=1, source_target_pairs={{0,1},{1,0},{2,3},{3,2},{4,5},{5,4},{6,7},{7,6},{8,9},{9,8},{10,11... | collective-permute-start | bytes 6291464 | tf_op jit(solution)/shard_map/ppermute | solution.py:186
  36.2 38.2 %copy-start.2 = (f32[1024,64]{0,1:T(8,128)S(1)}, f32[1024,64]{0,1:T(8,128)}, u32[]{:S(2)}) copy-start(f32[1024,64]{0,1:T(8,128)} %param.9) | copy-start | bytes 786436
  36.2 38.2 %copy-start.3 = (f32[1,16,1024]{2,1,0:T(8,128)S(1)}, f32[1,16,1024]{2,1,0:T(8,128)}, u32[]{:S(2)}) copy-start(f32[1,16,1024]{2,1,0:T(8,128)} %param.8) | copy-start | bytes 196612

commit v2 on v1

--- a/solution.py
+++ b/solution.py
@@ -14,11 +14,10 @@
 DP = ("x", "h")
 CTX = ("y", "z", "c")
 CHIPS = ("y", "z")
-NEAR = ("x", "z")
-FAR = ("h", "y", "c")
 RIM = 16
 BLOCK = 256
 STEP = 96
+PANEL = 8
 PARAMS = pltpu.CompilerParams(vmem_limit_bytes=48 << 20)
 
 
@@ -40,7 +39,7 @@
                     tap = 8 * tile + shift
                     if tap == 0:
                         continue
-                    term = taps_ref[tap : tap + 1, cols] * rows[8 * tile : 8 * tile + STEP + 8]
+                    term = taps_ref[tap - 1 : tap, cols] * rows[8 * tile : 8 * tile + STEP + 8]
                     part = term if part is None else part + term
                 if shift:
                     part = pltpu.roll(part, STEP + 8 - shift, 0)
@@ -93,31 +92,30 @@
     )(core, block, low, high, taps, signal)
 
 
-def merge_kernel(inverse_root, parts_ref, carried_ref, right_ref, merged_ref, left_ref):
+def merge_kernel(inverse_root, parts_ref, carried_ref, merged_ref, copies_ref):
     total = parts_ref[0].astype(F32)
     for index in range(1, parts_ref.shape[0]):
         total = total + parts_ref[index].astype(F32)
     merged = total * inverse_root + carried_ref[...]
     merged_ref[...] = merged
+    for index in range(copies_ref.shape[0]):
+        copies_ref[index] = merged
+
+
+def term_kernel(parts_ref, right_ref, left_ref, term_ref):
+    mean = parts_ref[0]
+    for index in range(1, parts_ref.shape[0]):
+        mean = mean + parts_ref[index]
     left = lax.dot_general(
-        merged, right_ref[...], (((1,), (1,)), ((), ())), precision=HIGHEST, preferred_element_type=F32
-    )
-    for index in range(left_ref.shape[0]):
-        left_ref[index] = left
-
-
-def term_kernel(parts_ref, merged_ref, left_ref, term_ref):
-    left = parts_ref[0]
-    for index in range(1, parts_ref.shape[0]):
-        left = left + parts_ref[index]
+        mean, right_ref[...], (((1,), (1,)), ((), ())), precision=HIGHEST, preferred_element_type=F32
+    )
     left_ref[...] = left
-    share = left * (1.0 / parts_ref.shape[0])
-    joined = jnp.concatenate([merged_ref[...], jnp.zeros_like(left), share], axis=1)
+    joined = jnp.concatenate([mean, jnp.zeros_like(left), left], axis=1)
     term = lax.dot_general(
         left, joined, (((0,), (0,)), ((), ())), precision=HIGHEST, preferred_element_type=F32
     )
     for index in range(term_ref.shape[0]):
-        term_ref[index] = term[2 * index : 2 * index + 2]
+        term_ref[index] = term[index : index + 1]
 
 
 def total_kernel(parts_ref, total_ref):
@@ -128,19 +126,40 @@
         total_ref[index] = total
 
 
+def eliminate(rest, rank):
+    done = []
+    for start in range(0, rank, PANEL):
+        row = lax.broadcasted_iota(jnp.int32, rest.shape, 0)
+        first = rank + start
+        columns = [
+            jnp.broadcast_to(rest[:, first + j : first + j + 1], rest.shape) for j in range(PANEL)
+        ]
+        top = rest[:PANEL]
+        scaled = []
+        for j in range(PANEL):
+            inverse = 1.0 / columns[j][j : j + 1]
+            scaled.append(top[j : j + 1] * inverse)
+            below = jnp.where(row > j, columns[j], 0.0)
+            columns[j] = below
+            for i in range(j + 1, PANEL):
+                columns[i] = columns[i] - below * (columns[i][j : j + 1] * inverse)
+            top = top - below[:PANEL] * scaled[j]
+        done.append(top)
+        rest = rest[PANEL:]
+        if start + PANEL < rank:
+            for j in range(PANEL):
+                rest = rest - columns[j][PANEL:] * scaled[j]
+    return jnp.concatenate(done, axis=0)
+
+
 def finish_kernel(replicas, rows_ref, left_ref, merged_ref, right_ref, estimate_ref, error_ref, wide_ref):
     rank = left_ref.shape[1]
     features = merged_ref.shape[1]
     for index in range(rows_ref.shape[0]):
-        wide_ref[2 * index : 2 * index + 2] = rows_ref[index]
+        wide_ref[index : index + 1] = rows_ref[index]
     row = lax.broadcasted_iota(jnp.int32, (rank, 2 * rank), 0)
     lane = lax.broadcasted_iota(jnp.int32, (rank, 2 * rank), 1)
-    work = wide_ref[:, features:] + (row == lane).astype(F32)
-    for step in range(rank - 1):
-        column = work[:, rank + step : rank + step + 1]
-        pivot_row = work[step : step + 1]
-        scaled = pivot_row / pivot_row[:, rank + step : rank + step + 1]
-        work = work - jnp.where(row > step, column, 0.0) * scaled
+    work = eliminate(wide_ref[:, features:] + (row == lane).astype(F32), rank)
     pivots = jnp.sum(jnp.where(row + rank == lane, work, 0.0), axis=1, keepdims=True)
     inverse = (work * (1.0 / jnp.sqrt(pivots)))[:, :rank]
     dot = functools.partial(lax.dot_general, precision=HIGHEST, preferred_element_type=F32)
@@ -170,7 +189,6 @@
     replicas = lax.axis_size(DP)
     contexts = lax.axis_size(CTX)
     chips = lax.axis_size(CHIPS)
-    near, far = lax.axis_size(NEAR), lax.axis_size(FAR)
     block = gated_input[0]
     frames, channels = block.shape
     features = upstream.shape[2]
@@ -180,30 +198,27 @@
     backward = [(target, source) for source, target in forward]
     low = lax.ppermute(block[frames - RIM :], CTX, forward)
     high = lax.ppermute(block[:RIM], CTX, backward)
-    taps = jnp.pad(depth_kernel, ((1, 0), (0, 0)))
     core = lax.axis_index("c").reshape(1)
-    keep, send = conv_product(core, block, low, high, taps, upstream[0])
+    keep, send = conv_product(core, block, low, high, depth_kernel, upstream[0])
     received = lax.ppermute(send, "c", [(0, 1), (1, 0)])
     pair_sum = (keep + received).astype(BF16)
     parts = exchange(pair_sum, CHIPS).reshape(chips, owned, features)
     inverse_root = 1.0 / math.sqrt(frames * contexts)
-    merged, left_parts = call(
+    merged, copies = call(
         functools.partial(merge_kernel, inverse_root),
-        [(owned, features), (replicas, owned, rank)],
+        [(owned, features), (replicas, owned, features)],
         parts,
         carried_error[0],
-        right_init.T,
-    )
-    left_parts = exchange(left_parts, DP)
+    )
     width = features + 2 * rank
-    pair = rank // near
-    left, term = call(term_kernel, [(owned, rank), (near, pair, width)], left_parts, merged)
-    (near_sum,) = call(total_kernel, [(far, pair, width)], exchange(term, NEAR))
-    (far_sum,) = call(total_kernel, [(near, pair, width)], exchange(near_sum, FAR))
+    left, term = call(
+        term_kernel, [(owned, rank), (rank, 1, width)], exchange(copies, DP), right_init.T
+    )
+    (total,) = call(total_kernel, [(rank, 1, width)], exchange(term, CTX))
     right, estimate, error = call(
         functools.partial(finish_kernel, replicas),
         [(rank, features), (owned, features), (owned, features)],
-        exchange(far_sum, NEAR),
+        exchange(total, CTX),
         left,
         merged,
         scratch=[pltpu.VMEM((rank, width), F32)],

time: 148 us -> 146 us (0.986)
  Pallas kernels: 21.8 us -> 18.6 us
    ppermute x1, starting transfers between devices: 4.69 us -> 8.77 us  [local(): high = lax.ppermute(block[:RIM], CTX, backward)]
    ppermute x1, starting transfers between devices: 5.38 us -> 1.92 us  [local(): low = lax.ppermute(block[frames - RIM:], CTX, forward)]
    pallas_call x5 -> x4, Pallas kernels: 7.6 us -> 4.36 us  [call(): pl.pallas_call(kernel, out_shape=[jax.ShapeDtypeStruct(shape, F32) for sh...]
    all_to_all x5 -> x4, blocking collectives: 102 us -> 103 us  [exchange(): return lax.all_to_all(block, axes, 0, 0, tiled=True)]
  transfers between devices with their start and end apart: 3 -> 3, of which waited for: 1 -> 2; matrix products, arithmetic and copies ran while one was open for 1% -> 0% of each run, Pallas kernels for 0% -> 0%
where the time goes in v2:
time: 146 us; the launch traced here: 145 us
  blocking collectives  103 us (71%)
  Pallas kernels  18.6 us (13%)
  starting transfers between devices  12.7 us (9%)
  waiting for transfers between devices  5.39 us (4%)
  local copies, waits for them, and re-layouts  4.51 us (3%)
    all_to_all x4, blocking collectives, exchange(): return lax.all_to_all(block, axes, 0, 0, tiled=True)  103 us
    pallas_call x1, Pallas kernels, conv_product(): pl.pallas_call(conv_kernel, grid=(channels // BLOCK,), in_specs=[pl.Block...  14.2 us
    ppermute x1, starting transfers between devices, local(): high = lax.ppermute(block[:RIM], CTX, backward)  8.77 us
    pallas_call x4, Pallas kernels, call(): pl.pallas_call(kernel, out_shape=[jax.ShapeDtypeStruct(shape, F32) for sh...  4.36 us
    ppermute x1, waiting for transfers between devices, local(): received = lax.ppermute(send, 'c', [(0, 1), (1, 0)])  4.23 us
    unnamed x10, local copies, waits for them, and re-layouts  3.73 us
  transfers between devices with their start and end apart: 3, of which 2 were waited for; matrix products, arithmetic and copies ran while one was open for 0% of the time, Pallas kernels for 0%

profile of v2, /device:TPU:1, one launch (start us, length us, event | category | flops | bytes accessed | tf_op | source)
XLA Modules:
  0.0 145.1 jit_solution(7657065136390190445)
XLA Ops:
  0.6 0.8 slice_bitcast_fusion
  1.4 8.8 %collective-permute-start.1 = (bf16[16,1024]{1,0:T(8,128)(2,1)S(1)}, bf16[16,1024]{1,0:T(8,128)(2,1)S(1)}, u32[]{:S(2)}, u32[]{:S(2)}) collective-permute-start(bf16[16,1024]{1,0:T(8,128)(2,1)S(1)} %get-tuple-element.21), channel_id=1, source_target_pairs={{1,0},{2,1},{3,2},{4,3},{5,4},{6,5},{7,6},{8,7},{9,8},{10,9},{11,1... | collective-permute-start | bytes 98312 | tf_op jit(solution)/shard_map/ppermute | solution.py:200
  10.2 1.9 %collective-permute-start = (bf16[16,1024]{1,0:T(8,128)(2,1)S(1)}, bf16[16,1024]{1,0:T(8,128)(2,1)S(1)}, u32[]{:S(2)}, u32[]{:S(2)}) collective-permute-start(bf16[16,1024]{1,0:T(8,128)(2,1)S(1)} %get-tuple-element.22), channel_id=1, source_target_pairs={{0,1},{1,2},{2,3},{3,4},{4,5},{5,6},{6,7},{7,8},{8,9},{9,10},{10,1... | collective-permute-start | bytes 98312 | tf_op jit(solution)/shard_map/ppermute | solution.py:199
  12.1 0.0 collective-permute-done.1.high_ref
  12.1 1.2 collective-permute-done.low_ref
  13.3 1.4 copy-done
  14.7 1.4 copy-done.1
  16.1 0.9 copy-done.3
  17.0 14.2 %conv_product.1 = (f32[512,1024]{1,0:T(8,128)S(1)}, f32[512,1024]{1,0:T(8,128)}) custom-call(s32[1]{0:T(128)} %bitcast.core_ref, bf16[768,1024]{1,0:T(8,128)(2,1)S(1)} %bitcast.12, bf16[16,1024]{1,0:T(8,128)(2,1)S(1)} %collective-permute-done.low_ref, bf16[16,1024]{1,0:T(8,128)(2,1)S(1)} %collective-permute-done.1.high_ref, f32[31,1024]{1,0:T(8,128)S(1)} %copy-done.3, ...), custom_call_target="tpu_custom_call" | custom-call | tf_op jit(solution)/shard_map/conv_product/pallas_call | solution.py:76
  31.2 2.0 %collective-permute-start.2 = (f32[512,1024]{1,0:T(8,128)}, f32[512,1024]{1,0:T(8,128)S(1)}, u32[]{:S(2)}, u32[]{:S(2)}) collective-permute-start(f32[512,1024]{1,0:T(8,128)} %get-tuple-element.13), channel_id=1, source_target_pairs={{0,1},{1,0},{2,3},{3,2},{4,5},{5,4},{6,7},{7,6},{8,9},{9,8},{10,11... | collective-permute-start | bytes 6291464 | tf_op jit(solution)/shard_map/ppermute | solution.py:203
  33.3 4.2 %collective-permute-done.2 = f32[512,1024]{1,0:T(8,128)S(1)} collective-permute-done((f32[512,1024]{1,0:T(8,128)}, f32[512,1024]{1,0:T(8,128)S(1)}, u32[]{:S(2)}, u32[]{:S(2)}) %collective-permute-start.2) | collective-permute-done | bytes 2097184 | tf_op jit(solution)/shard_map/ppermute | solution.py:203
  37.5 0.5 add_convert_fusion
  38.0 0.0 copy-start.4
  38.0 0.0 copy-start.2
  38.0 37.0 %all_to_all.24.parts_ref = bf16[32,16,1024]{2,1,0:T(8,128)(2,1)S(1)} all-to-all(bf16[32,16,1024]{2,1,0:T(8,128)(2,1)S(1)} %bitcast.16), channel_id=1, replica_groups=mesh['x'=4,'h'=2,'y'=4,'z'=8,'c'=2] {'y','z'}, dimensions={0} | all-to-all | bytes 2097152 | tf_op jit(solution)/shard_map/all_to_all | solution.py:185
  75.0 0.0 copy-done.4
  75.0 0.2 merge_kernel.1
  75.2 19.0 %all_to_all.25.parts_ref = f32[8,16,1024]{2,1,0:T(8,128)S(1)} all-to-all(f32[8,16,1024]{2,1,0:T(8,128)S(1)} %get-tuple-element.14), channel_id=1, replica_groups=mesh['x'=4,'h'=2,'y'=4,'z'=8,'c'=2] {'x','h'}, dimensions={0} | all-to-all | bytes 1048576 | tf_op jit(solution)/shard_map/all_to_all | solution.py:185
  94.2 0.0 copy-done.2
  94.2 1.2 term_kernel.1
  95.4 28.6 %all_to_all.26.parts_ref = f32[64,1,1152]{2,1,0:T(1,128)S(1)} all-to-all(f32[64,1,1152]{2,1,0:T(1,128)S(1)} %get-tuple-element.15), channel_id=1, replica_groups=mesh['x'=4,'h'=2,'y'=4,'z'=8,'c'=2] {'y','z','c'}, dimensions={0} | all-to-all | bytes 589824 | tf_op jit(solution)/shard_map/all_to_all | solution.py:185
  123.9 0.1 total_kernel.1
  124.0 18.1 %all_to_all.27.rows_ref = f32[64,1,1152]{2,1,0:T(1,128)S(1)} all-to-all(f32[64,1,1152]{2,1,0:T(1,128)S(1)} %total_kernel.1), channel_id=1, replica_groups=mesh['x'=4,'h'=2,'y'=4,'z'=8,'c'=2] {'y','z','c'}, dimensions={0} | all-to-all | bytes 589824 | tf_op jit(solution)/shard_map/all_to_all | solution.py:185
  142.2 2.9 %finish_kernel.1 = (f32[64,1024]{1,0:T(8,128)}, f32[16,1024]{1,0:T(8,128)}, f32[16,1024]{1,0:T(8,128)}) custom-call(f32[64,1,1152]{2,1,0:T(1,128)S(1)} %all_to_all.27.rows_ref, f32[16,64]{1,0:T(8,128)S(1)} %get-tuple-element.16.left_ref, f32[16,1024]{1,0:T(8,128)S(1)} %get-tuple-element.17.merged_ref), custom_call_target="tpu_custom_call" | custom-call | tf_op jit(solution)/shard_map/finish_kernel/pallas_call | solution.py:175
  (3 shorter events, 0.0 us)
Async XLA Ops:
  1.4 10.7 %collective-permute-start.1 = (bf16[16,1024]{1,0:T(8,128)(2,1)S(1)}, bf16[16,1024]{1,0:T(8,128)(2,1)S(1)}, u32[]{:S(2)}, u32[]{:S(2)}) collective-permute-start(bf16[16,1024]{1,0:T(8,128)(2,1)S(1)} %get-tuple-element.21), channel_id=1, source_target_pairs={{1,0},{2,1},{3,2},{4,3},{5,4},{6,5},{7,6},{8,7},{9,8},{10,9},{11,1... | collective-permute-start | bytes 98312 | tf_op jit(solution)/shard_map/ppermute | solution.py:200
  10.2 3.1 %collective-permute-start = (bf16[16,1024]{1,0:T(8,128)(2,1)S(1)}, bf16[16,1024]{1,0:T(8,128)(2,1)S(1)}, u32[]{:S(2)}, u32[]{:S(2)}) collective-permute-start(bf16[16,1024]{1,0:T(8,128)(2,1)S(1)} %get-tuple-element.22), channel_id=1, source_target_pairs={{0,1},{1,2},{2,3},{3,4},{4,5},{5,6},{6,7},{7,8},{8,9},{9,10},{10,1... | collective-permute-start | bytes 98312 | tf_op jit(solution)/shard_map/ppermute | solution.py:199
  13.3 1.4 copy-start
  14.7 1.4 copy-start.1
  16.1 0.9 copy-start.3
  31.2 6.3 %collective-permute-start.2 = (f32[512,1024]{1,0:T(8,128)}, f32[512,1024]{1,0:T(8,128)S(1)}, u32[]{:S(2)}, u32[]{:S(2)}) collective-permute-start(f32[512,1024]{1,0:T(8,128)} %get-tuple-element.13), channel_id=1, source_target_pairs={{0,1},{1,0},{2,3},{3,2},{4,5},{5,4},{6,7},{7,6},{8,9},{9,8},{10,11... | collective-permute-start | bytes 6291464 | tf_op jit(solution)/shard_map/ppermute | solution.py:203
  38.0 37.0 %copy-start.4 = (f32[1,16,1024]{2,1,0:T(8,128)S(1)}, f32[1,16,1024]{2,1,0:T(8,128)}, u32[]{:S(2)}) copy-start(f32[1,16,1024]{2,1,0:T(8,128)} %param.8) | copy-start | bytes 196612
  38.0 56.2 %copy-start.2 = (f32[1024,64]{0,1:T(8,128)S(1)}, f32[1024,64]{0,1:T(8,128)}, u32[]{:S(2)}) copy-start(f32[1024,64]{0,1:T(8,128)} %param.9) | copy-start | bytes 786436

commit v3 on v2

--- a/solution.py
+++ b/solution.py
@@ -13,21 +13,47 @@
 HIGHEST = lax.Precision.HIGHEST
 DP = ("x", "h")
 CTX = ("y", "z", "c")
-CHIPS = ("y", "z")
+ROWS = ("x", "h", "y")
+NEAR = ("x", "z")
+FAR = ("h", "y", "c")
 RIM = 16
 BLOCK = 256
-STEP = 96
+STEP = 192
 PANEL = 8
 PARAMS = pltpu.CompilerParams(vmem_limit_bytes=48 << 20)
 
 
-def conv_kernel(core_ref, x_ref, low_ref, high_ref, taps_ref, up_ref, keep_ref, send_ref, wide_ref, act_ref):
-    frames, width = x_ref.shape
+def conv_kernel(
+    core_ref, block_hbm, low_ref, high_ref, taps_hbm, up_hbm, keep_ref, send_ref,
+    block_ref, taps_ref, up_ref, wide_ref, act_ref, sems,
+):
+    frames, width = act_ref.shape
+    count = block_ref.shape[0]
+    step = pl.program_id(0)
+
+    def block_copy(index):
+        cols = pl.ds(pl.multiple_of(index * width, width), width)
+        return pltpu.make_async_copy(block_hbm.at[:, cols], block_ref.at[index], sems.at[index])
+
+    taps_copy = pltpu.make_async_copy(taps_hbm, taps_ref, sems.at[count])
+    up_copy = pltpu.make_async_copy(up_hbm, up_ref, sems.at[count + 1])
+
+    @pl.when(step == 0)
+    def _():
+        block_copy(0).start()
+        taps_copy.start()
+        for index in range(1, count):
+            block_copy(index).start()
+        up_copy.start()
+        taps_copy.wait()
+
+    block_copy(step).wait()
     wide_ref[0:RIM] = low_ref[...].astype(F32)
-    wide_ref[RIM : RIM + frames] = x_ref[...].astype(F32)
+    wide_ref[RIM : RIM + frames] = block_ref[step].astype(F32)
     wide_ref[RIM + frames :] = high_ref[...].astype(F32)
     for lane in range(0, width, 128):
         cols = slice(lane, lane + 128)
+        tap_cols = pl.ds(pl.multiple_of(step * width + lane, 128), 128)
 
         def chunk(index, _):
             base = pl.multiple_of(index * STEP, STEP)
@@ -39,7 +65,7 @@
                     tap = 8 * tile + shift
                     if tap == 0:
                         continue
-                    term = taps_ref[tap - 1 : tap, cols] * rows[8 * tile : 8 * tile + STEP + 8]
+                    term = taps_ref[tap - 1 : tap, tap_cols] * rows[8 * tile : 8 * tile + STEP + 8]
                     part = term if part is None else part + term
                 if shift:
                     part = pltpu.roll(part, STEP + 8 - shift, 0)
@@ -50,12 +76,16 @@
             return 0
 
         lax.fori_loop(0, frames // STEP, chunk, 0)
+
+    @pl.when(step == 0)
+    def _():
+        up_copy.wait()
+
     product = lax.dot_general(
         act_ref[...], up_ref[...], (((0,), (0,)), ((), ())), preferred_element_type=F32
     )
     pieces = product.reshape(width // 32, 2, 16, product.shape[1])
-    first = pieces[:, 0].reshape(width // 2, -1)
-    second = pieces[:, 1].reshape(width // 2, -1)
+    first, second = pieces[:, 0][:, None], pieces[:, 1][:, None]
 
     @pl.when(core_ref[0] == 0)
     def _():
@@ -71,51 +101,73 @@
 def conv_product(core, block, low, high, taps, signal):
     frames, channels = block.shape
     features = signal.shape[1]
-    half = jax.ShapeDtypeStruct((channels // 2, features), F32)
-    column = lambda rows: pl.BlockSpec((rows, BLOCK), lambda i: (0, i))
+    count = channels // BLOCK
+    half = jax.ShapeDtypeStruct((BLOCK // 32, count, 16, features), F32)
+    rim = pl.BlockSpec((RIM, BLOCK), lambda i: (0, i))
+    far = pl.BlockSpec(memory_space=pltpu.HBM)
+    block, taps, signal = (
+        pltpu.with_memory_space_constraint(array, pltpu.HBM) for array in (block, taps, signal)
+    )
     return pl.pallas_call(
         conv_kernel,
-        grid=(channels // BLOCK,),
-        in_specs=[
-            pl.BlockSpec(memory_space=pltpu.SMEM),
-            column(frames),
-            column(RIM),
-            column(RIM),
-            column(taps.shape[0]),
-            pl.BlockSpec((frames, features), lambda i: (0, 0)),
+        grid=(count,),
+        in_specs=[pl.BlockSpec(memory_space=pltpu.SMEM), far, rim, rim, far, far],
+        out_specs=[pl.BlockSpec((BLOCK // 32, 1, 16, features), lambda i: (0, i, 0, 0))] * 2,
+        out_shape=[half, half],
+        scratch_shapes=[
+            pltpu.VMEM((count, frames, BLOCK), BF16),
+            pltpu.VMEM(taps.shape, F32),
+            pltpu.VMEM(signal.shape, BF16),
+            pltpu.VMEM((frames + 2 * RIM, BLOCK), F32),
+            pltpu.VMEM((frames, BLOCK), BF16),
+            pltpu.SemaphoreType.DMA((count + 2,)),
         ],
-        out_specs=[pl.BlockSpec((BLOCK // 2, features), lambda i: (i, 0))] * 2,
-        out_shape=[half, half],
-        scratch_shapes=[pltpu.VMEM((frames + 2 * RIM, BLOCK), F32), pltpu.VMEM((frames, BLOCK), BF16)],
         compiler_params=PARAMS,
         name="conv_product",
     )(core, block, low, high, taps, signal)
 
 
-def merge_kernel(inverse_root, parts_ref, carried_ref, merged_ref, copies_ref):
+def merge_kernel(inverse_root, place_ref, parts_ref, carried_ref, right_ref, left_ref, *refs):
+    out_refs, rows_ref = refs[:-1], refs[-1]
+    sources, count, owned, features = parts_ref.shape
+    place = place_ref[0]
     total = parts_ref[0].astype(F32)
-    for index in range(1, parts_ref.shape[0]):
+    for index in range(1, sources):
         total = total + parts_ref[index].astype(F32)
-    merged = total * inverse_root + carried_ref[...]
+    rows_ref[...] = total * inverse_root
+    rows_ref[place] = rows_ref[place] + carried_ref[...]
+    left = lax.dot_general(
+        rows_ref[...].reshape(count * owned, features), right_ref[...], (((1,), (1,)), ((), ())),
+        precision=HIGHEST, preferred_element_type=F32,
+    )
+    for index in range(count):
+        top = left[index * owned : index * owned + owned // 2]
+        low = left[index * owned + owned // 2 : (index + 1) * owned]
+        packed = jnp.concatenate([top, low], axis=1)
+        for copy in range(left_ref.shape[0]):
+            left_ref[copy, index] = packed
+    for shift, out_ref in enumerate(out_refs):
+        out_ref[...] = rows_ref[lax.rem(place + shift, count)]
+
+
+def term_kernel(replicas, left_parts_ref, *refs):
+    row_refs, (merged_ref, left_ref, term_ref) = refs[:-3], refs[-3:]
+    merged = row_refs[0][...]
+    for ref in row_refs[1:]:
+        merged = merged + ref[...]
     merged_ref[...] = merged
-    for index in range(copies_ref.shape[0]):
-        copies_ref[index] = merged
-
-
-def term_kernel(parts_ref, right_ref, left_ref, term_ref):
-    mean = parts_ref[0]
-    for index in range(1, parts_ref.shape[0]):
-        mean = mean + parts_ref[index]
-    left = lax.dot_general(
-        mean, right_ref[...], (((1,), (1,)), ((), ())), precision=HIGHEST, preferred_element_type=F32
-    )
+    packed = left_parts_ref[0]
+    for index in range(1, left_parts_ref.shape[0]):
+        packed = packed + left_parts_ref[index]
+    rank = left_ref.shape[1]
+    left = jnp.concatenate([packed[:, :rank], packed[:, rank:]], axis=0)
     left_ref[...] = left
-    joined = jnp.concatenate([mean, jnp.zeros_like(left), left], axis=1)
+    joined = jnp.concatenate([merged, jnp.zeros_like(left), left * (1.0 / replicas)], axis=1)
     term = lax.dot_general(
         left, joined, (((0,), (0,)), ((), ())), precision=HIGHEST, preferred_element_type=F32
     )
     for index in range(term_ref.shape[0]):
-        term_ref[index] = term[index : index + 1]
+        term_ref[index] = term[2 * index : 2 * index + 2]
 
 
 def total_kernel(parts_ref, total_ref):
@@ -156,7 +208,7 @@
     rank = left_ref.shape[1]
     features = merged_ref.shape[1]
     for index in range(rows_ref.shape[0]):
-        wide_ref[index : index + 1] = rows_ref[index]
+        wide_ref[2 * index : 2 * index + 2] = rows_ref[index]
     row = lax.broadcasted_iota(jnp.int32, (rank, 2 * rank), 0)
     lane = lax.broadcasted_iota(jnp.int32, (rank, 2 * rank), 1)
     work = eliminate(wide_ref[:, features:] + (row == lane).astype(F32), rank)
@@ -171,9 +223,11 @@
     error_ref[...] = merged_ref[...] - estimate
 
 
-def call(kernel, outs, *args, scratch=()):
+def call(kernel, outs, *args, smem=0, scratch=()):
+    spaces = [pltpu.SMEM] * smem + [pltpu.VMEM] * (len(args) - smem)
     return pl.pallas_call(
         kernel,
+        in_specs=[pl.BlockSpec(memory_space=space) for space in spaces],
         out_shape=[jax.ShapeDtypeStruct(shape, F32) for shape in outs],
         scratch_shapes=list(scratch),
         compiler_params=PARAMS,
@@ -188,7 +242,6 @@
 def local(gated_input, upstream, depth_kernel, carried_error, right_init):
     replicas = lax.axis_size(DP)
     contexts = lax.axis_size(CTX)
-    chips = lax.axis_size(CHIPS)
     block = gated_input[0]
     frames, channels = block.shape
     features = upstream.shape[2]
@@ -202,23 +255,40 @@
     keep, send = conv_product(core, block, low, high, depth_kernel, upstream[0])
     received = lax.ppermute(send, "c", [(0, 1), (1, 0)])
     pair_sum = (keep + received).astype(BF16)
-    parts = exchange(pair_sum, CHIPS).reshape(chips, owned, features)
+    parts = exchange(pair_sum, "z")
     inverse_root = 1.0 / math.sqrt(frames * contexts)
-    merged, copies = call(
+    runs = lax.axis_size("y")
+    row = (owned, features)
+    left_parts, *shifted = call(
         functools.partial(merge_kernel, inverse_root),
-        [(owned, features), (replicas, owned, features)],
+        [(replicas, runs, owned // 2, 2 * rank)] + [row] * runs,
+        lax.axis_index("y").reshape(1),
         parts,
         carried_error[0],
-    )
+        right_init.T,
+        smem=1,
+        scratch=[pltpu.VMEM((runs, owned, features), F32)],
+    )
+    for shift in range(1, runs):
+        shifted[shift] = lax.ppermute(
+            shifted[shift], "y", [(i, (i + shift) % runs) for i in range(runs)]
+        )
+    left_parts = exchange(left_parts.reshape(replicas * runs, owned // 2, 2 * rank), ROWS)
     width = features + 2 * rank
-    left, term = call(
-        term_kernel, [(owned, rank), (rank, 1, width)], exchange(copies, DP), right_init.T
-    )
-    (total,) = call(total_kernel, [(rank, 1, width)], exchange(term, CTX))
+    near, far = lax.axis_size(NEAR), lax.axis_size(FAR)
+    pair = rank // near
+    merged, left, term = call(
+        functools.partial(term_kernel, replicas),
+        [row, (owned, rank), (near, pair, width)],
+        left_parts,
+        *shifted,
+    )
+    (near_sum,) = call(total_kernel, [(far, pair, width)], exchange(term, NEAR))
+    (far_sum,) = call(total_kernel, [(near, pair, width)], exchange(near_sum, FAR))
     right, estimate, error = call(
         functools.partial(finish_kernel, replicas),
-        [(rank, features), (owned, features), (owned, features)],
-        exchange(total, CTX),
+        [(rank, features), row, row],
+        exchange(far_sum, NEAR),
         left,
         merged,
         scratch=[pltpu.VMEM((rank, width), F32)],

time: 146 us -> 151 us (1.034)
  blocking collectives: 103 us -> 48.5 us
  waiting for transfers between devices: 5.39 us -> 36.4 us
  starting transfers between devices: 12.7 us -> 43.1 us
  local copies, waits for them, and re-layouts: 4.51 us -> 0.79 us
    all_to_all x4 -> x3, blocking collectives: 103 us -> 48.5 us  [exchange(): return lax.all_to_all(block, axes, 0, 0, tiled=True)]
    all_to_all x0 -> x2, waiting for transfers between devices: none -> 29.2 us  [exchange(): return lax.all_to_all(block, axes, 0, 0, tiled=True)]
    all_to_all x0 -> x2, starting transfers between devices: none -> 20.2 us  [exchange(): return lax.all_to_all(block, axes, 0, 0, tiled=True)]
    ppermute x0 -> x3, starting transfers between devices: none -> 10.2 us  [local(): lax.ppermute(shifted[shift], 'y', [(i, (i + shift) % runs) for i in range...]
    unnamed x10 -> x4, local copies, waits for them, and re-layouts: 3.73 us -> 0.01 us
    ppermute x0 -> x3, waiting for transfers between devices: none -> 1.9 us  [local(): lax.ppermute(shifted[shift], 'y', [(i, (i + shift) % runs) for i in range...]
    pallas_call x5 -> x6, Pallas kernels: 18.6 us -> 18.7 us  [the longest x1 13.8 us: conv_product(): pl.pallas_call(conv_kernel, grid=(count,), in_specs=[pl.BlockSpec(memory_...]
  transfers between devices with their start and end apart: 3 -> 8, of which waited for: 2 -> 5; matrix products, arithmetic and copies ran while one was open for 0% -> 0% of each run, Pallas kernels for 0% -> 0%
where the time goes in v3:
time: 151 us; the launch traced here: 150 us
  blocking collectives  48.5 us (32%)
  starting transfers between devices  43.1 us (29%)
  waiting for transfers between devices  36.4 us (24%)
  Pallas kernels  18.7 us (12%)
    all_to_all x3, blocking collectives, exchange(): return lax.all_to_all(block, axes, 0, 0, tiled=True)  48.5 us
    all_to_all x2, waiting for transfers between devices, exchange(): return lax.all_to_all(block, axes, 0, 0, tiled=True)  29.2 us
    all_to_all x2, starting transfers between devices, exchange(): return lax.all_to_all(block, axes, 0, 0, tiled=True)  20.2 us
    pallas_call x1, Pallas kernels, conv_product(): pl.pallas_call(conv_kernel, grid=(count,), in_specs=[pl.BlockSpec(memory_...  13.8 us
    ppermute x3, starting transfers between devices, local(): lax.ppermute(shifted[shift], 'y', [(i, (i + shift) % runs) for i in range...  10.2 us
    ppermute x1, starting transfers between devices, local(): high = lax.ppermute(block[:RIM], CTX, backward)  8.77 us
    pallas_call x5, Pallas kernels, call(): pl.pallas_call(kernel, in_specs=[pl.BlockSpec(memory_space=space) for spa...  4.85 us
    ppermute x1, waiting for transfers between devices, local(): received = lax.ppermute(send, 'c', [(0, 1), (1, 0)])  4.06 us
  transfers between devices with their start and end apart: 8, of which 5 were waited for; matrix products, arithmetic and copies ran while one was open for 0% of the time, Pallas kernels for 0%

profile of v3, /device:TPU:1, one launch (start us, length us, event | category | flops | bytes accessed | tf_op | source)
XLA Modules:
  0.0 149.5 jit_solution(9959434801490495228)
XLA Ops:
  0.6 0.8 slice_bitcast_fusion
  1.4 8.8 %collective-permute-start.1 = (bf16[16,1024]{1,0:T(8,128)(2,1)S(1)}, bf16[16,1024]{1,0:T(8,128)(2,1)S(1)}, u32[]{:S(2)}, u32[]{:S(2)}) collective-permute-start(bf16[16,1024]{1,0:T(8,128)(2,1)S(1)} %get-tuple-element.29), channel_id=1, source_target_pairs={{1,0},{2,1},{3,2},{4,3},{5,4},{6,5},{7,6},{8,7},{9,8},{10,9},{11,1... | collective-permute-start | bytes 98312 | tf_op jit(solution)/shard_map/ppermute | solution.py:253
  10.2 1.9 %collective-permute-start = (bf16[16,1024]{1,0:T(8,128)(2,1)S(1)}, bf16[16,1024]{1,0:T(8,128)(2,1)S(1)}, u32[]{:S(2)}, u32[]{:S(2)}) collective-permute-start(bf16[16,1024]{1,0:T(8,128)(2,1)S(1)} %get-tuple-element.30), channel_id=1, source_target_pairs={{0,1},{1,2},{2,3},{3,4},{4,5},{5,6},{6,7},{7,8},{8,9},{9,10},{10,1... | collective-permute-start | bytes 98312 | tf_op jit(solution)/shard_map/ppermute | solution.py:252
  12.1 0.0 collective-permute-done.1.high_ref
  12.1 1.2 collective-permute-done.low_ref
  13.3 13.8 %conv_product.1 = (f32[8,4,16,1024]{3,2,1,0:T(8,128)S(1)}, f32[8,4,16,1024]{3,2,1,0:T(8,128)S(1)}) custom-call(s32[1]{0:T(128)} %bitcast.1.core_ref, bf16[768,1024]{1,0:T(8,128)(2,1)} %bitcast.15, bf16[16,1024]{1,0:T(8,128)(2,1)S(1)} %collective-permute-done.low_ref, bf16[16,1024]{1,0:T(8,128)(2,1)S(1)} %collective-permute-done.1.high_ref, ...), custom_call_target="tpu_custom_call" | custom-call | tf_op jit(solution)/shard_map/conv_product/pallas_call | solution.py:111
  27.1 2.0 %collective-permute-start.2 = (f32[8,4,16,1024]{3,2,1,0:T(8,128)S(1)}, f32[8,4,16,1024]{3,2,1,0:T(8,128)S(1)}, u32[]{:S(2)}, u32[]{:S(2)}) collective-permute-start(f32[8,4,16,1024]{3,2,1,0:T(8,128)S(1)} %get-tuple-element.17), channel_id=1, source_target_pairs={{0,1},{1,0},{2,3},{3,2},{4,5},{5,4},{6,7},{7,6},{8,9},{9,8},{10,11... | collective-permute-start | bytes 6291464 | tf_op jit(solution)/shard_map/ppermute | solution.py:256
  29.1 4.1 %collective-permute-done.2 = f32[8,4,16,1024]{3,2,1,0:T(8,128)S(1)} collective-permute-done((f32[8,4,16,1024]{3,2,1,0:T(8,128)S(1)}, f32[8,4,16,1024]{3,2,1,0:T(8,128)S(1)}, u32[]{:S(2)}, u32[]{:S(2)}) %collective-permute-start.2) | collective-permute-done | bytes 2097184 | tf_op jit(solution)/shard_map/ppermute | solution.py:256
  33.2 1.3 add_convert_fusion
  34.5 7.8 %all-to-all-start = ((bf16[8,4,16,1024]{3,2,1,0:T(8,128)(2,1)}), bf16[8,4,16,1024]{3,2,1,0:T(8,128)(2,1)S(1)}, u32[]{:S(2)}, u32[]{:S(2)}) async-start(bf16[8,4,16,1024]{3,2,1,0:T(8,128)(2,1)} %add_convert_fusion), calls=%async_computation | async-start | bytes 2097152 | tf_op jit(solution)/shard_map/all_to_all | solution.py:239
  42.3 29.2 %all-to-all-done.parts_ref = bf16[8,4,16,1024]{3,2,1,0:T(8,128)(2,1)S(1)} async-done(((bf16[8,4,16,1024]{3,2,1,0:T(8,128)(2,1)}), bf16[8,4,16,1024]{3,2,1,0:T(8,128)(2,1)S(1)}, u32[]{:S(2)}, u32[]{:S(2)}) %all-to-all-start) | async-done | bytes 1048608 | tf_op jit(solution)/shard_map/all_to_all | solution.py:239
  71.5 1.3 merge_kernel.1
  72.8 12.5 %all-to-all-start.1 = ((f32[32,8,128]{2,1,0:T(8,128)}), f32[32,8,128]{2,1,0:T(8,128)S(1)}, u32[]{:S(2)}, u32[]{:S(2)}) async-start(f32[32,8,128]{2,1,0:T(8,128)} %bitcast.8), calls=%async_computation.1 | async-start | bytes 262144 | tf_op jit(solution)/shard_map/all_to_all | solution.py:239
  85.3 3.1 %collective-permute-start.3 = (f32[16,1024]{1,0:T(8,128)S(1)}, f32[16,1024]{1,0:T(8,128)S(1)}, u32[]{:S(2)}, u32[]{:S(2)}) collective-permute-start(f32[16,1024]{1,0:T(8,128)S(1)} %get-tuple-element.20), channel_id=1, source_target_pairs={{0,16},{16,32},{32,48},{48,0},{1,17},{17,33},{33,49},{49,1},{2,18}... | collective-permute-start | bytes 196616 | tf_op jit(solution)/shard_map/ppermute | solution.py:273
  88.4 4.0 %collective-permute-start.4 = (f32[16,1024]{1,0:T(8,128)S(1)}, f32[16,1024]{1,0:T(8,128)S(1)}, u32[]{:S(2)}, u32[]{:S(2)}) collective-permute-start(f32[16,1024]{1,0:T(8,128)S(1)} %get-tuple-element.21), channel_id=1, source_target_pairs={{0,32},{16,48},{32,0},{48,16},{1,33},{17,49},{33,1},{49,17},{2,34}... | collective-permute-start | bytes 196616 | tf_op jit(solution)/shard_map/ppermute | solution.py:273
  92.4 3.1 %collective-permute-start.5 = (f32[16,1024]{1,0:T(8,128)S(1)}, f32[16,1024]{1,0:T(8,128)S(1)}, u32[]{:S(2)}, u32[]{:S(2)}) collective-permute-start(f32[16,1024]{1,0:T(8,128)S(1)} %get-tuple-element.22), channel_id=1, source_target_pairs={{0,48},{16,0},{32,16},{48,32},{1,49},{17,1},{33,17},{49,33},{2,50}... | collective-permute-start | bytes 196616 | tf_op jit(solution)/shard_map/ppermute | solution.py:273
  95.5 0.2 collective-permute-done.4.refs_2_
  95.8 1.7 %collective-permute-done.5.refs_3_ = f32[16,1024]{1,0:T(8,128)S(1)} collective-permute-done((f32[16,1024]{1,0:T(8,128)S(1)}, f32[16,1024]{1,0:T(8,128)S(1)}, u32[]{:S(2)}, u32[]{:S(2)}) %collective-permute-start.5) | collective-permute-done | bytes 65568 | tf_op jit(solution)/shard_map/ppermute | solution.py:273
  97.4 0.0 all-to-all-done.1.left_parts_ref
  97.4 0.5 term_kernel.1
  98.0 14.0 %all_to_all.25.parts_ref = f32[32,2,1152]{2,1,0:T(2,128)S(1)} all-to-all(f32[32,2,1152]{2,1,0:T(2,128)S(1)} %get-tuple-element.23), channel_id=1, replica_groups=mesh['x'=4,'h'=2,'y'=4,'z'=8,'c'=2] {'x','z'}, dimensions={0} | all-to-all | bytes 589824 | tf_op jit(solution)/shard_map/all_to_all | solution.py:239
  112.0 19.8 %all_to_all.26.parts_ref = f32[16,2,1152]{2,1,0:T(2,128)S(1)} all-to-all(f32[16,2,1152]{2,1,0:T(2,128)S(1)} %total_kernel.2), channel_id=1, replica_groups=mesh['x'=4,'h'=2,'y'=4,'z'=8,'c'=2] {'h','y','c'}, dimensions={0} | all-to-all | bytes 294912 | tf_op jit(solution)/shard_map/all_to_all | solution.py:239
  131.9 14.7 %all_to_all.27.rows_ref = f32[32,2,1152]{2,1,0:T(2,128)S(1)} all-to-all(f32[32,2,1152]{2,1,0:T(2,128)S(1)} %total_kernel.3), channel_id=1, replica_groups=mesh['x'=4,'h'=2,'y'=4,'z'=8,'c'=2] {'x','z'}, dimensions={0} | all-to-all | bytes 589824 | tf_op jit(solution)/shard_map/all_to_all | solution.py:239
  146.6 2.9 %finish_kernel.1 = (f32[64,1024]{1,0:T(8,128)}, f32[16,1024]{1,0:T(8,128)}, f32[16,1024]{1,0:T(8,128)}) custom-call(f32[32,2,1152]{2,1,0:T(2,128)S(1)} %all_to_all.27.rows_ref, f32[16,64]{1,0:T(8,128)S(1)} %get-tuple-element.24.left_ref, f32[16,1024]{1,0:T(8,128)S(1)} %get-tuple-element.25.merged_ref), custom_call_target="tpu_custom_call" | custom-call | tf_op jit(solution)/shard_map/finish_kernel/pallas_call | solution.py:228
  (7 shorter events, 0.1 us)
Async XLA Ops:
  1.4 10.7 %collective-permute-start.1 = (bf16[16,1024]{1,0:T(8,128)(2,1)S(1)}, bf16[16,1024]{1,0:T(8,128)(2,1)S(1)}, u32[]{:S(2)}, u32[]{:S(2)}) collective-permute-start(bf16[16,1024]{1,0:T(8,128)(2,1)S(1)} %get-tuple-element.29), channel_id=1, source_target_pairs={{1,0},{2,1},{3,2},{4,3},{5,4},{6,5},{7,6},{8,7},{9,8},{10,9},{11,1... | collective-permute-start | bytes 98312 | tf_op jit(solution)/shard_map/ppermute | solution.py:253
  10.2 3.1 %collective-permute-start = (bf16[16,1024]{1,0:T(8,128)(2,1)S(1)}, bf16[16,1024]{1,0:T(8,128)(2,1)S(1)}, u32[]{:S(2)}, u32[]{:S(2)}) collective-permute-start(bf16[16,1024]{1,0:T(8,128)(2,1)S(1)} %get-tuple-element.30), channel_id=1, source_target_pairs={{0,1},{1,2},{2,3},{3,4},{4,5},{5,6},{6,7},{7,8},{8,9},{9,10},{10,1... | collective-permute-start | bytes 98312 | tf_op jit(solution)/shard_map/ppermute | solution.py:252
  27.1 6.1 %collective-permute-start.2 = (f32[8,4,16,1024]{3,2,1,0:T(8,128)S(1)}, f32[8,4,16,1024]{3,2,1,0:T(8,128)S(1)}, u32[]{:S(2)}, u32[]{:S(2)}) collective-permute-start(f32[8,4,16,1024]{3,2,1,0:T(8,128)S(1)} %get-tuple-element.17), channel_id=1, source_target_pairs={{0,1},{1,0},{2,3},{3,2},{4,5},{5,4},{6,7},{7,6},{8,9},{9,8},{10,11... | collective-permute-start | bytes 6291464 | tf_op jit(solution)/shard_map/ppermute | solution.py:256
  34.5 37.0 %copy-start = (f32[1024,64]{0,1:T(8,128)S(1)}, f32[1024,64]{0,1:T(8,128)}, u32[]{:S(2)}) copy-start(f32[1024,64]{0,1:T(8,128)} %param.9) | copy-start | bytes 786436
  34.5 37.0 %copy-start.1 = (f32[1,16,1024]{2,1,0:T(8,128)S(1)}, f32[1,16,1024]{2,1,0:T(8,128)}, u32[]{:S(2)}) copy-start(f32[1,16,1024]{2,1,0:T(8,128)} %param.8) | copy-start | bytes 196612
  34.5 37.0 %all-to-all-start = ((bf16[8,4,16,1024]{3,2,1,0:T(8,128)(2,1)}), bf16[8,4,16,1024]{3,2,1,0:T(8,128)(2,1)S(1)}, u32[]{:S(2)}, u32[]{:S(2)}) async-start(bf16[8,4,16,1024]{3,2,1,0:T(8,128)(2,1)} %add_convert_fusion), calls=%async_computation | async-start | bytes 2097152 | tf_op jit(solution)/shard_map/all_to_all | solution.py:239
  72.8 24.6 %all-to-all-start.1 = ((f32[32,8,128]{2,1,0:T(8,128)}), f32[32,8,128]{2,1,0:T(8,128)S(1)}, u32[]{:S(2)}, u32[]{:S(2)}) async-start(f32[32,8,128]{2,1,0:T(8,128)} %bitcast.8), calls=%async_computation.1 | async-start | bytes 262144 | tf_op jit(solution)/shard_map/all_to_all | solution.py:239
  85.3 10.2 %collective-permute-start.3 = (f32[16,1024]{1,0:T(8,128)S(1)}, f32[16,1024]{1,0:T(8,128)S(1)}, u32[]{:S(2)}, u32[]{:S(2)}) collective-permute-start(f32[16,1024]{1,0:T(8,128)S(1)} %get-tuple-element.20), channel_id=1, source_target_pairs={{0,16},{16,32},{32,48},{48,0},{1,17},{17,33},{33,49},{49,1},{2,18}... | collective-permute-start | bytes 196616 | tf_op jit(solution)/shard_map/ppermute | solution.py:273
  88.4 7.3 %collective-permute-start.4 = (f32[16,1024]{1,0:T(8,128)S(1)}, f32[16,1024]{1,0:T(8,128)S(1)}, u32[]{:S(2)}, u32[]{:S(2)}) collective-permute-start(f32[16,1024]{1,0:T(8,128)S(1)} %get-tuple-element.21), channel_id=1, source_target_pairs={{0,32},{16,48},{32,0},{48,16},{1,33},{17,49},{33,1},{49,17},{2,34}... | collective-permute-start | bytes 196616 | tf_op jit(solution)/shard_map/ppermute | solution.py:273
  92.4 5.0 %collective-permute-start.5 = (f32[16,1024]{1,0:T(8,128)S(1)}, f32[16,1024]{1,0:T(8,128)S(1)}, u32[]{:S(2)}, u32[]{:S(2)}) collective-permute-start(f32[16,1024]{1,0:T(8,128)S(1)} %get-tuple-element.22), channel_id=1, source_target_pairs={{0,48},{16,0},{32,16},{48,32},{1,49},{17,1},{33,17},{49,33},{2,50}... | collective-permute-start | bytes 196616 | tf_op jit(solution)/shard_map/ppermute | solution.py:273

commit v4 on v3

--- a/solution.py
+++ b/solution.py
@@ -13,11 +13,13 @@
 HIGHEST = lax.Precision.HIGHEST
 DP = ("x", "h")
 CTX = ("y", "z", "c")
-ROWS = ("x", "h", "y")
+CHIPS = ("y", "z")
 NEAR = ("x", "z")
 FAR = ("h", "y", "c")
 RIM = 16
-BLOCK = 256
+LANES = 128
+TILE = 8
+BLOCK = 512
 STEP = 192
 PANEL = 8
 PARAMS = pltpu.CompilerParams(vmem_limit_bytes=48 << 20)
@@ -25,10 +27,11 @@
 
 def conv_kernel(
     core_ref, block_hbm, low_ref, high_ref, taps_hbm, up_hbm, keep_ref, send_ref,
-    block_ref, taps_ref, up_ref, wide_ref, act_ref, sems,
+    block_ref, taps_ref, up_ref, wide_ref, sums_ref, weights_ref, act_ref, sems,
 ):
     frames, width = act_ref.shape
     count = block_ref.shape[0]
+    rows = frames + 2 * RIM
     step = pl.program_id(0)
 
     def block_copy(index):
@@ -48,31 +51,62 @@
         taps_copy.wait()
 
     block_copy(step).wait()
-    wide_ref[0:RIM] = low_ref[...].astype(F32)
-    wide_ref[RIM : RIM + frames] = block_ref[step].astype(F32)
-    wide_ref[RIM + frames :] = high_ref[...].astype(F32)
-    for lane in range(0, width, 128):
-        cols = slice(lane, lane + 128)
-        tap_cols = pl.ds(pl.multiple_of(step * width + lane, 128), 128)
+    for group in range(width // LANES):
+        cols = slice(LANES * group, LANES * (group + 1))
+        tap_cols = pl.ds(pl.multiple_of(step * width + LANES * group, LANES), LANES)
+        wide_ref[group, 0:RIM] = low_ref[:, cols].astype(F32)
+        wide_ref[group, RIM : RIM + frames] = block_ref[step, :, cols].astype(F32)
+        wide_ref[group, RIM + frames : rows] = high_ref[:, cols].astype(F32)
+        sums_ref[group, 0 : rows - TILE] = wide_ref[group, 0 : rows - TILE] + wide_ref[group, TILE:rows]
+        weights_ref[group, 0:1] = jnp.zeros((1, LANES), F32)
+        weights_ref[group, 1:32] = taps_ref[:, tap_cols]
+        weights_ref[group, 32:40] = weights_ref[group, 0:8] + weights_ref[group, 8:16]
+        weights_ref[group, 40:48] = weights_ref[group, 16:24] + weights_ref[group, 24:32]
+
+    pairs = STEP // (2 * TILE)
+    for group in range(width // LANES):
 
         def chunk(index, _):
             base = pl.multiple_of(index * STEP, STEP)
-            rows = wide_ref[pl.ds(base, STEP + 2 * RIM), cols]
-            total = None
-            for shift in range(8):
-                part = None
-                for tile in range(4):
-                    tap = 8 * tile + shift
-                    if tap == 0:
-                        continue
-                    term = taps_ref[tap - 1 : tap, tap_cols] * rows[8 * tile : 8 * tile + STEP + 8]
-                    part = term if part is None else part + term
-                if shift:
-                    part = pltpu.roll(part, STEP + 8 - shift, 0)
-                part = part[:STEP]
-                total = part if total is None else total + part
-            half = 0.5 * total
-            act_ref[pl.ds(base, STEP), cols] = (half + half * jnp.tanh(half)).astype(BF16)
+            even, odd, both = [None] * (pairs + 1), [None] * pairs, [None] * pairs
+
+            def add(totals, place, weight, value):
+                term = weight * value
+                totals[place] = term if totals[place] is None else totals[place] + term
+
+            for shift in range(TILE):
+
+                def weight(first):
+                    return weights_ref[group, first + shift : first + shift + 1]
+
+                def tiles(ref, first, number):
+                    return [
+                        ref[group, pl.ds(base + shift + TILE * (first + 2 * k), TILE)]
+                        for k in range(number)
+                    ]
+
+                values = tiles(wide_ref, 0, pairs + 2)
+                for k in range(pairs + 1):
+                    if shift:
+                        add(even, k, weight(0), values[k])
+                    add(even, k, weight(16), values[k + 1])
+                values = tiles(wide_ref, 1, pairs + 1)
+                for k in range(pairs):
+                    add(odd, k, weight(8), values[k])
+                    add(odd, k, weight(24), values[k + 1])
+                values = tiles(sums_ref, 1, pairs + 1)
+                for k in range(pairs):
+                    add(both, k, weight(32), values[k])
+                    add(both, k, weight(40), values[k + 1])
+            for k in range(pairs):
+                total = jnp.concatenate(
+                    [even[k] + odd[k], both[k] - (even[k + 1] + odd[k])], axis=0
+                )
+                half = 0.5 * total
+                act_ref[
+                    pl.ds(pl.multiple_of(base + 2 * TILE * k, 2 * TILE), 2 * TILE),
+                    LANES * group : LANES * (group + 1),
+                ] = (half + half * jnp.tanh(half)).astype(BF16)
             return 0
 
         lax.fori_loop(0, frames // STEP, chunk, 0)
@@ -85,7 +119,7 @@
         act_ref[...], up_ref[...], (((0,), (0,)), ((), ())), preferred_element_type=F32
     )
     pieces = product.reshape(width // 32, 2, 16, product.shape[1])
-    first, second = pieces[:, 0][:, None], pieces[:, 1][:, None]
+    first, second = pieces[:, 0], pieces[:, 1]
 
     @pl.when(core_ref[0] == 0)
     def _():
@@ -102,7 +136,8 @@
     frames, channels = block.shape
     features = signal.shape[1]
     count = channels // BLOCK
-    half = jax.ShapeDtypeStruct((BLOCK // 32, count, 16, features), F32)
+    groups = BLOCK // LANES
+    half = jax.ShapeDtypeStruct((channels // 32, 16, features), F32)
     rim = pl.BlockSpec((RIM, BLOCK), lambda i: (0, i))
     far = pl.BlockSpec(memory_space=pltpu.HBM)
     block, taps, signal = (
@@ -112,13 +147,15 @@
         conv_kernel,
         grid=(count,),
         in_specs=[pl.BlockSpec(memory_space=pltpu.SMEM), far, rim, rim, far, far],
-        out_specs=[pl.BlockSpec((BLOCK // 32, 1, 16, features), lambda i: (0, i, 0, 0))] * 2,
+        out_specs=[pl.BlockSpec((BLOCK // 32, 16, features), lambda i: (i, 0, 0))] * 2,
         out_shape=[half, half],
         scratch_shapes=[
             pltpu.VMEM((count, frames, BLOCK), BF16),
             pltpu.VMEM(taps.shape, F32),
             pltpu.VMEM(signal.shape, BF16),
-            pltpu.VMEM((frames + 2 * RIM, BLOCK), F32),
+            pltpu.VMEM((groups, frames + 2 * RIM, LANES), F32),
+            pltpu.VMEM((groups, frames + 2 * RIM, LANES), F32),
+            pltpu.VMEM((groups, 48, LANES), F32),
             pltpu.VMEM((frames, BLOCK), BF16),
             pltpu.SemaphoreType.DMA((count + 2,)),
         ],
@@ -127,42 +164,34 @@
     )(core, block, low, high, taps, signal)
 
 
-def merge_kernel(inverse_root, place_ref, parts_ref, carried_ref, right_ref, left_ref, *refs):
-    out_refs, rows_ref = refs[:-1], refs[-1]
-    sources, count, owned, features = parts_ref.shape
-    place = place_ref[0]
+def pair_kernel(keep_ref, received_ref, pair_ref):
+    pair_ref[...] = (keep_ref[...] + received_ref[...]).astype(BF16)
+
+
+def merge_kernel(inverse_root, parts_ref, carried_ref, right_ref, merged_ref, left_ref):
     total = parts_ref[0].astype(F32)
-    for index in range(1, sources):
+    for index in range(1, parts_ref.shape[0]):
         total = total + parts_ref[index].astype(F32)
-    rows_ref[...] = total * inverse_root
-    rows_ref[place] = rows_ref[place] + carried_ref[...]
+    merged = total * inverse_root + carried_ref[...]
+    merged_ref[...] = merged
     left = lax.dot_general(
-        rows_ref[...].reshape(count * owned, features), right_ref[...], (((1,), (1,)), ((), ())),
-        precision=HIGHEST, preferred_element_type=F32,
-    )
-    for index in range(count):
-        top = left[index * owned : index * owned + owned // 2]
-        low = left[index * owned + owned // 2 : (index + 1) * owned]
-        packed = jnp.concatenate([top, low], axis=1)
-        for copy in range(left_ref.shape[0]):
-            left_ref[copy, index] = packed
-    for shift, out_ref in enumerate(out_refs):
-        out_ref[...] = rows_ref[lax.rem(place + shift, count)]
-
-
-def term_kernel(replicas, left_parts_ref, *refs):
-    row_refs, (merged_ref, left_ref, term_ref) = refs[:-3], refs[-3:]
-    merged = row_refs[0][...]
-    for ref in row_refs[1:]:
-        merged = merged + ref[...]
-    merged_ref[...] = merged
-    packed = left_parts_ref[0]
-    for index in range(1, left_parts_ref.shape[0]):
-        packed = packed + left_parts_ref[index]
+        merged, right_ref[...], (((1,), (1,)), ((), ())), precision=HIGHEST, preferred_element_type=F32
+    )
+    middle = left.shape[0] // 2
+    packed = jnp.concatenate([left[:middle], left[middle:]], axis=1)
+    for index in range(left_ref.shape[0]):
+        left_ref[index] = packed
+
+
+def term_kernel(parts_ref, merged_ref, left_ref, term_ref):
+    packed = parts_ref[0]
+    for index in range(1, parts_ref.shape[0]):
+        packed = packed + parts_ref[index]
     rank = left_ref.shape[1]
     left = jnp.concatenate([packed[:, :rank], packed[:, rank:]], axis=0)
     left_ref[...] = left
-    joined = jnp.concatenate([merged, jnp.zeros_like(left), left * (1.0 / replicas)], axis=1)
+    share = left * (1.0 / parts_ref.shape[0])
+    joined = jnp.concatenate([merged_ref[...], jnp.zeros_like(left), share], axis=1)
     term = lax.dot_general(
         left, joined, (((0,), (0,)), ((), ())), precision=HIGHEST, preferred_element_type=F32
     )
@@ -223,12 +252,10 @@
     error_ref[...] = merged_ref[...] - estimate
 
 
-def call(kernel, outs, *args, smem=0, scratch=()):
-    spaces = [pltpu.SMEM] * smem + [pltpu.VMEM] * (len(args) - smem)
+def call(kernel, outs, *args, scratch=()):
     return pl.pallas_call(
         kernel,
-        in_specs=[pl.BlockSpec(memory_space=space) for space in spaces],
-        out_shape=[jax.ShapeDtypeStruct(shape, F32) for shape in outs],
+        out_shape=[jax.ShapeDtypeStruct(out, F32) if isinstance(out, tuple) else out for out in outs],
         scratch_shapes=list(scratch),
         compiler_params=PARAMS,
         name=getattr(kernel, "func", kernel).__name__,
@@ -254,37 +281,23 @@
     core = lax.axis_index("c").reshape(1)
     keep, send = conv_product(core, block, low, high, depth_kernel, upstream[0])
     received = lax.ppermute(send, "c", [(0, 1), (1, 0)])
-    pair_sum = (keep + received).astype(BF16)
-    parts = exchange(pair_sum, "z")
+    (pair_sum,) = call(pair_kernel, [pltpu.VMEM(keep.shape, BF16)], keep, received)
     inverse_root = 1.0 / math.sqrt(frames * contexts)
-    runs = lax.axis_size("y")
     row = (owned, features)
-    left_parts, *shifted = call(
+    merged, left_parts = call(
         functools.partial(merge_kernel, inverse_root),
-        [(replicas, runs, owned // 2, 2 * rank)] + [row] * runs,
-        lax.axis_index("y").reshape(1),
-        parts,
+        [row, pltpu.VMEM((replicas, owned // 2, 2 * rank), F32)],
+        exchange(pair_sum, CHIPS),
         carried_error[0],
         right_init.T,
-        smem=1,
-        scratch=[pltpu.VMEM((runs, owned, features), F32)],
-    )
-    for shift in range(1, runs):
-        shifted[shift] = lax.ppermute(
-            shifted[shift], "y", [(i, (i + shift) % runs) for i in range(runs)]
-        )
-    left_parts = exchange(left_parts.reshape(replicas * runs, owned // 2, 2 * rank), ROWS)
+    )
     width = features + 2 * rank
     near, far = lax.axis_size(NEAR), lax.axis_size(FAR)
-    pair = rank // near
-    merged, left, term = call(
-        functools.partial(term_kernel, replicas),
-        [row, (owned, rank), (near, pair, width)],
-        left_parts,
-        *shifted,
-    )
-    (near_sum,) = call(total_kernel, [(far, pair, width)], exchange(term, NEAR))
-    (far_sum,) = call(total_kernel, [(near, pair, width)], exchange(near_sum, FAR))
+    near_form = pltpu.VMEM((near, rank // near, width), F32)
+    far_form = pltpu.VMEM((far, rank // near, width), F32)
+    left, term = call(term_kernel, [(owned, rank), near_form], exchange(left_parts, DP), merged)
+    (near_sum,) = call(total_kernel, [far_form], exchange(term, NEAR))
+    (far_sum,) = call(total_kernel, [near_form], exchange(near_sum, FAR))
     right, estimate, error = call(
         functools.partial(finish_kernel, replicas),
         [(rank, features), row, row],

time: 151 us -> 137 us (0.907)
  blocking collectives: 48.5 us -> 102 us
  waiting for transfers between devices: 36.4 us -> 5.16 us
  starting transfers between devices: 43.1 us -> 12.7 us
  Pallas kernels: 18.7 us -> 14.3 us
    all_to_all x3 -> x5, blocking collectives: 48.5 us -> 102 us  [exchange(): return lax.all_to_all(block, axes, 0, 0, tiled=True)]
    all_to_all x2 -> x0, waiting for transfers between devices: 29.2 us -> none  [exchange(): return lax.all_to_all(block, axes, 0, 0, tiled=True)]
    all_to_all x2 -> x0, starting transfers between devices: 20.2 us -> none  [exchange(): return lax.all_to_all(block, axes, 0, 0, tiled=True)]
    ppermute x3 -> x0, starting transfers between devices: 10.2 us -> none  [local(): lax.ppermute(shifted[shift], 'y', [(i, (i + shift) % runs) for i in range...]
    pallas_call x1, Pallas kernels: 13.8 us -> 10.1 us  [conv_product(): pl.pallas_call(conv_kernel, grid=(count,), in_specs=[pl.BlockSpec(memory_...]
    ppermute x3 -> x0, waiting for transfers between devices: 1.9 us -> none  [local(): lax.ppermute(shifted[shift], 'y', [(i, (i + shift) % runs) for i in range...]
    pallas_call x5 -> x6, Pallas kernels: 4.85 us -> 4.17 us  [call(): pl.pallas_call(kernel, out_shape=[jax.ShapeDtypeStruct(out, F32) if isins...]
  transfers between devices with their start and end apart: 8 -> 3, of which waited for: 5 -> 2; matrix products, arithmetic and copies ran while one was open for 0% -> 0% of each run, Pallas kernels for 0% -> 0%
where the time goes in v4:
time: 137 us; the launch traced here: 136 us
  blocking collectives  102 us (74%)
  Pallas kernels  14.3 us (10%)
  starting transfers between devices  12.7 us (9%)
  waiting for transfers between devices  5.16 us (4%)
    all_to_all x5, blocking collectives, exchange(): return lax.all_to_all(block, axes, 0, 0, tiled=True)  102 us
    pallas_call x1, Pallas kernels, conv_product(): pl.pallas_call(conv_kernel, grid=(count,), in_specs=[pl.BlockSpec(memory_...  10.1 us
    ppermute x1, starting transfers between devices, local(): high = lax.ppermute(block[:RIM], CTX, backward)  8.77 us
    pallas_call x6, Pallas kernels, call(): pl.pallas_call(kernel, out_shape=[jax.ShapeDtypeStruct(out, F32) if isins...  4.17 us
    ppermute x1, waiting for transfers between devices, local(): received = lax.ppermute(send, 'c', [(0, 1), (1, 0)])  4 us
  transfers between devices with their start and end apart: 3, of which 2 were waited for; matrix products, arithmetic and copies ran while one was open for 0% of the time, Pallas kernels for 0%

profile of v4, /device:TPU:1, one launch (start us, length us, event | category | flops | bytes accessed | tf_op | source)
XLA Modules:
  0.0 135.7 jit_solution(6729332021920027804)
XLA Ops:
  0.6 0.8 slice_bitcast_fusion
  1.4 8.8 %collective-permute-start.1 = (bf16[16,1024]{1,0:T(8,128)(2,1)S(1)}, bf16[16,1024]{1,0:T(8,128)(2,1)S(1)}, u32[]{:S(2)}, u32[]{:S(2)}) collective-permute-start(bf16[16,1024]{1,0:T(8,128)(2,1)S(1)} %get-tuple-element.21), channel_id=1, source_target_pairs={{1,0},{2,1},{3,2},{4,3},{5,4},{6,5},{7,6},{8,7},{9,8},{10,9},{11,1... | collective-permute-start | bytes 98312 | tf_op jit(solution)/shard_map/ppermute | solution.py:280
  10.2 1.9 %collective-permute-start = (bf16[16,1024]{1,0:T(8,128)(2,1)S(1)}, bf16[16,1024]{1,0:T(8,128)(2,1)S(1)}, u32[]{:S(2)}, u32[]{:S(2)}) collective-permute-start(bf16[16,1024]{1,0:T(8,128)(2,1)S(1)} %get-tuple-element.22), channel_id=1, source_target_pairs={{0,1},{1,2},{2,3},{3,4},{4,5},{5,6},{6,7},{7,8},{8,9},{9,10},{10,1... | collective-permute-start | bytes 98312 | tf_op jit(solution)/shard_map/ppermute | solution.py:279
  12.1 0.0 collective-permute-done.1.high_ref
  12.1 1.2 collective-permute-done.low_ref
  13.3 10.1 %conv_product.1 = (f32[32,16,1024]{2,1,0:T(8,128)S(1)}, f32[32,16,1024]{2,1,0:T(8,128)S(1)}) custom-call(s32[1]{0:T(128)} %bitcast.core_ref, bf16[768,1024]{1,0:T(8,128)(2,1)} %bitcast.13, bf16[16,1024]{1,0:T(8,128)(2,1)S(1)} %collective-permute-done.low_ref, bf16[16,1024]{1,0:T(8,128)(2,1)S(1)} %collective-permute-done.1.high_ref, f32[31,1024]{1,0:T(8,128)} %taps_hbm.1, ...), custom_call_target="tpu_custom_call" | custom-call | tf_op jit(solution)/shard_map/conv_product/pallas_call | solution.py:146
  23.4 2.0 %collective-permute-start.2 = (f32[32,16,1024]{2,1,0:T(8,128)S(1)}, f32[32,16,1024]{2,1,0:T(8,128)S(1)}, u32[]{:S(2)}, u32[]{:S(2)}) collective-permute-start(f32[32,16,1024]{2,1,0:T(8,128)S(1)} %get-tuple-element.13), channel_id=1, source_target_pairs={{0,1},{1,0},{2,3},{3,2},{4,5},{5,4},{6,7},{7,6},{8,9},{9,8},{10,11... | collective-permute-start | bytes 6291464 | tf_op jit(solution)/shard_map/ppermute | solution.py:283
  25.4 4.0 %collective-permute-done.2.received_ref = f32[32,16,1024]{2,1,0:T(8,128)S(1)} collective-permute-done((f32[32,16,1024]{2,1,0:T(8,128)S(1)}, f32[32,16,1024]{2,1,0:T(8,128)S(1)}, u32[]{:S(2)}, u32[]{:S(2)}) %collective-permute-start.2) | collective-permute-done | bytes 2097184 | tf_op jit(solution)/shard_map/ppermute | solution.py:283
  29.4 0.2 pair_kernel.1
  29.6 0.0 copy-start
  29.6 0.0 copy-start.1
  29.7 37.0 %all_to_all.25.parts_ref = bf16[32,16,1024]{2,1,0:T(8,128)(2,1)S(1)} all-to-all(bf16[32,16,1024]{2,1,0:T(8,128)(2,1)S(1)} %pair_kernel.1), channel_id=1, replica_groups=mesh['x'=4,'h'=2,'y'=4,'z'=8,'c'=2] {'y','z'}, dimensions={0} | all-to-all | bytes 2097152 | tf_op jit(solution)/shard_map/all_to_all | solution.py:266
  66.7 0.0 copy-done
  66.7 0.0 copy-done.1
  66.7 0.5 merge_kernel.1
  67.2 16.5 %all_to_all.26.parts_ref = f32[8,8,128]{2,1,0:T(8,128)S(1)} all-to-all(f32[8,8,128]{2,1,0:T(8,128)S(1)} %get-tuple-element.14), channel_id=1, replica_groups=mesh['x'=4,'h'=2,'y'=4,'z'=8,'c'=2] {'x','h'}, dimensions={0} | all-to-all | bytes 65536 | tf_op jit(solution)/shard_map/all_to_all | solution.py:266
  83.7 0.5 term_kernel.1
  84.2 16.9 %all_to_all.27.parts_ref = f32[32,2,1152]{2,1,0:T(2,128)S(1)} all-to-all(f32[32,2,1152]{2,1,0:T(2,128)S(1)} %get-tuple-element.16), channel_id=1, replica_groups=mesh['x'=4,'h'=2,'y'=4,'z'=8,'c'=2] {'x','z'}, dimensions={0} | all-to-all | bytes 589824 | tf_op jit(solution)/shard_map/all_to_all | solution.py:266
  101.1 16.4 %all_to_all.28.parts_ref = f32[16,2,1152]{2,1,0:T(2,128)S(1)} all-to-all(f32[16,2,1152]{2,1,0:T(2,128)S(1)} %total_kernel.2), channel_id=1, replica_groups=mesh['x'=4,'h'=2,'y'=4,'z'=8,'c'=2] {'h','y','c'}, dimensions={0} | all-to-all | bytes 294912 | tf_op jit(solution)/shard_map/all_to_all | solution.py:266
  117.5 15.2 %all_to_all.29.rows_ref = f32[32,2,1152]{2,1,0:T(2,128)S(1)} all-to-all(f32[32,2,1152]{2,1,0:T(2,128)S(1)} %total_kernel.3), channel_id=1, replica_groups=mesh['x'=4,'h'=2,'y'=4,'z'=8,'c'=2] {'x','z'}, dimensions={0} | all-to-all | bytes 589824 | tf_op jit(solution)/shard_map/all_to_all | solution.py:266
  132.8 2.9 %finish_kernel.1 = (f32[64,1024]{1,0:T(8,128)}, f32[16,1024]{1,0:T(8,128)}, f32[16,1024]{1,0:T(8,128)}) custom-call(f32[32,2,1152]{2,1,0:T(2,128)S(1)} %all_to_all.29.rows_ref, f32[16,64]{1,0:T(8,128)S(1)} %get-tuple-element.17.left_ref, f32[16,1024]{1,0:T(8,128)S(1)} %get-tuple-element.15.merged_ref), custom_call_target="tpu_custom_call" | custom-call | tf_op jit(solution)/shard_map/finish_kernel/pallas_call | solution.py:256
  (2 shorter events, 0.1 us)
Async XLA Ops:
  1.4 10.7 %collective-permute-start.1 = (bf16[16,1024]{1,0:T(8,128)(2,1)S(1)}, bf16[16,1024]{1,0:T(8,128)(2,1)S(1)}, u32[]{:S(2)}, u32[]{:S(2)}) collective-permute-start(bf16[16,1024]{1,0:T(8,128)(2,1)S(1)} %get-tuple-element.21), channel_id=1, source_target_pairs={{1,0},{2,1},{3,2},{4,3},{5,4},{6,5},{7,6},{8,7},{9,8},{10,9},{11,1... | collective-permute-start | bytes 98312 | tf_op jit(solution)/shard_map/ppermute | solution.py:280
  10.2 3.1 %collective-permute-start = (bf16[16,1024]{1,0:T(8,128)(2,1)S(1)}, bf16[16,1024]{1,0:T(8,128)(2,1)S(1)}, u32[]{:S(2)}, u32[]{:S(2)}) collective-permute-start(bf16[16,1024]{1,0:T(8,128)(2,1)S(1)} %get-tuple-element.22), channel_id=1, source_target_pairs={{0,1},{1,2},{2,3},{3,4},{4,5},{5,6},{6,7},{7,8},{8,9},{9,10},{10,1... | collective-permute-start | bytes 98312 | tf_op jit(solution)/shard_map/ppermute | solution.py:279
  23.4 6.1 %collective-permute-start.2 = (f32[32,16,1024]{2,1,0:T(8,128)S(1)}, f32[32,16,1024]{2,1,0:T(8,128)S(1)}, u32[]{:S(2)}, u32[]{:S(2)}) collective-permute-start(f32[32,16,1024]{2,1,0:T(8,128)S(1)} %get-tuple-element.13), channel_id=1, source_target_pairs={{0,1},{1,0},{2,3},{3,2},{4,5},{5,4},{6,7},{7,6},{8,9},{9,8},{10,11... | collective-permute-start | bytes 6291464 | tf_op jit(solution)/shard_map/ppermute | solution.py:283
  29.6 37.0 %copy-start = (f32[1024,64]{0,1:T(8,128)S(1)}, f32[1024,64]{0,1:T(8,128)}, u32[]{:S(2)}) copy-start(f32[1024,64]{0,1:T(8,128)} %param.9) | copy-start | bytes 786436
  29.6 37.0 %copy-start.1 = (f32[1,16,1024]{2,1,0:T(8,128)S(1)}, f32[1,16,1024]{2,1,0:T(8,128)}, u32[]{:S(2)}) copy-start(f32[1,16,1024]{2,1,0:T(8,128)} %param.8) | copy-start | bytes 196612

commit v5 on v4

--- a/solution.py
+++ b/solution.py
@@ -13,58 +13,62 @@
 HIGHEST = lax.Precision.HIGHEST
 DP = ("x", "h")
 CTX = ("y", "z", "c")
-CHIPS = ("y", "z")
 NEAR = ("x", "z")
 FAR = ("h", "y", "c")
 RIM = 16
 LANES = 128
 TILE = 8
-BLOCK = 512
-STEP = 192
-PANEL = 8
+STEP = 256
+PANEL = 16
 PARAMS = pltpu.CompilerParams(vmem_limit_bytes=48 << 20)
 
 
 def conv_kernel(
-    core_ref, block_hbm, low_ref, high_ref, taps_hbm, up_hbm, keep_ref, send_ref,
-    block_ref, taps_ref, up_ref, wide_ref, sums_ref, weights_ref, act_ref, sems,
+    core_ref, block_hbm, other_ref, near_ref, far_ref, taps_hbm, act_ref,
+    block_ref, taps_ref, wide_ref, sums_ref, weights_ref, sems,
 ):
-    frames, width = act_ref.shape
-    count = block_ref.shape[0]
-    rows = frames + 2 * RIM
-    step = pl.program_id(0)
+    count, frames, width = block_ref.shape
+    rows = 2 * frames + 2 * RIM
+    core = core_ref[0]
+    lane = lax.broadcasted_iota(jnp.int32, (1, LANES), 1)
+    first = lax.rem(lane // 16, 2) == core_ref[1]
+    own = pl.multiple_of(RIM + frames * core, RIM)
+    partner = pl.multiple_of(RIM + frames * (1 - core), RIM)
+    pairs = STEP // (2 * TILE)
 
     def block_copy(index):
         cols = pl.ds(pl.multiple_of(index * width, width), width)
         return pltpu.make_async_copy(block_hbm.at[:, cols], block_ref.at[index], sems.at[index])
 
+    def picked(value):
+        value = value.astype(F32)
+        return jnp.where(first, value[:, :LANES], value[:, LANES:])
+
     taps_copy = pltpu.make_async_copy(taps_hbm, taps_ref, sems.at[count])
-    up_copy = pltpu.make_async_copy(up_hbm, up_ref, sems.at[count + 1])
-
-    @pl.when(step == 0)
-    def _():
-        block_copy(0).start()
-        taps_copy.start()
-        for index in range(1, count):
-            block_copy(index).start()
-        up_copy.start()
-        taps_copy.wait()
-
-    block_copy(step).wait()
-    for group in range(width // LANES):
-        cols = slice(LANES * group, LANES * (group + 1))
-        tap_cols = pl.ds(pl.multiple_of(step * width + LANES * group, LANES), LANES)
-        wide_ref[group, 0:RIM] = low_ref[:, cols].astype(F32)
-        wide_ref[group, RIM : RIM + frames] = block_ref[step, :, cols].astype(F32)
-        wide_ref[group, RIM + frames : rows] = high_ref[:, cols].astype(F32)
-        sums_ref[group, 0 : rows - TILE] = wide_ref[group, 0 : rows - TILE] + wide_ref[group, TILE:rows]
-        weights_ref[group, 0:1] = jnp.zeros((1, LANES), F32)
-        weights_ref[group, 1:32] = taps_ref[:, tap_cols]
-        weights_ref[group, 32:40] = weights_ref[group, 0:8] + weights_ref[group, 8:16]
-        weights_ref[group, 40:48] = weights_ref[group, 16:24] + weights_ref[group, 24:32]
-
-    pairs = STEP // (2 * TILE)
-    for group in range(width // LANES):
+    for index in range(count):
+        block_copy(index).start()
+        if index == 0:
+            taps_copy.start()
+
+    def group(step, _):
+        cols = pl.ds(pl.multiple_of(step * width, width), width)
+        out_cols = pl.ds(pl.multiple_of(step * LANES, LANES), LANES)
+        near, far = picked(near_ref[:, cols]), picked(far_ref[:, cols])
+        wide_ref[0:RIM] = jnp.where(core == 0, near, far)
+        wide_ref[rows - RIM : rows] = jnp.where(core == 0, far, near)
+        wide_ref[pl.ds(partner, frames)] = picked(other_ref[:, cols])
+
+        @pl.when(step == 0)
+        def _():
+            taps_copy.wait()
+
+        weights_ref[0:1] = jnp.zeros((1, LANES), F32)
+        weights_ref[1:32] = picked(taps_ref[:, cols])
+        weights_ref[32:40] = weights_ref[0:8] + weights_ref[8:16]
+        weights_ref[40:48] = weights_ref[16:24] + weights_ref[24:32]
+        block_copy(step).wait()
+        wide_ref[pl.ds(own, frames)] = picked(block_ref[step])
+        sums_ref[0 : rows - TILE] = wide_ref[0 : rows - TILE] + wide_ref[TILE:rows]
 
         def chunk(index, _):
             base = pl.multiple_of(index * STEP, STEP)
@@ -76,13 +80,12 @@
 
             for shift in range(TILE):
 
-                def weight(first):
-                    return weights_ref[group, first + shift : first + shift + 1]
-
-                def tiles(ref, first, number):
+                def weight(row):
+                    return weights_ref[row + shift : row + shift + 1]
+
+                def tiles(ref, start, number):
                     return [
-                        ref[group, pl.ds(base + shift + TILE * (first + 2 * k), TILE)]
-                        for k in range(number)
+                        ref[pl.ds(base + shift + TILE * (start + 2 * k), TILE)] for k in range(number)
                     ]
 
                 values = tiles(wide_ref, 0, pairs + 2)
@@ -103,69 +106,58 @@
                     [even[k] + odd[k], both[k] - (even[k + 1] + odd[k])], axis=0
                 )
                 half = 0.5 * total
-                act_ref[
-                    pl.ds(pl.multiple_of(base + 2 * TILE * k, 2 * TILE), 2 * TILE),
-                    LANES * group : LANES * (group + 1),
-                ] = (half + half * jnp.tanh(half)).astype(BF16)
+                place = pl.ds(pl.multiple_of(base + 2 * TILE * k, 2 * TILE), 2 * TILE)
+                act_ref[place, out_cols] = (half + half * jnp.tanh(half)).astype(BF16)
             return 0
 
-        lax.fori_loop(0, frames // STEP, chunk, 0)
-
-    @pl.when(step == 0)
-    def _():
-        up_copy.wait()
-
-    product = lax.dot_general(
-        act_ref[...], up_ref[...], (((0,), (0,)), ((), ())), preferred_element_type=F32
-    )
-    pieces = product.reshape(width // 32, 2, 16, product.shape[1])
-    first, second = pieces[:, 0], pieces[:, 1]
-
-    @pl.when(core_ref[0] == 0)
-    def _():
-        keep_ref[...] = first
-        send_ref[...] = second
-
-    @pl.when(core_ref[0] == 1)
-    def _():
-        keep_ref[...] = second
-        send_ref[...] = first
-
-
-def conv_product(core, block, low, high, taps, signal):
+        lax.fori_loop(0, 2 * frames // STEP, chunk, 0)
+        return 0
+
+    lax.fori_loop(0, count, group, 0)
+
+
+def activation(core, block, other, near, far, taps):
     frames, channels = block.shape
-    features = signal.shape[1]
-    count = channels // BLOCK
-    groups = BLOCK // LANES
-    half = jax.ShapeDtypeStruct((channels // 32, 16, features), F32)
-    rim = pl.BlockSpec((RIM, BLOCK), lambda i: (0, i))
-    far = pl.BlockSpec(memory_space=pltpu.HBM)
-    block, taps, signal = (
-        pltpu.with_memory_space_constraint(array, pltpu.HBM) for array in (block, taps, signal)
-    )
+    width = 2 * LANES
+    count = channels // width
+    rows = 2 * frames + 2 * RIM
+    smem, vmem, hbm = (
+        pl.BlockSpec(memory_space=space) for space in (pltpu.SMEM, pltpu.VMEM, pltpu.HBM)
+    )
+    block, taps = (pltpu.with_memory_space_constraint(array, pltpu.HBM) for array in (block, taps))
     return pl.pallas_call(
         conv_kernel,
-        grid=(count,),
-        in_specs=[pl.BlockSpec(memory_space=pltpu.SMEM), far, rim, rim, far, far],
-        out_specs=[pl.BlockSpec((BLOCK // 32, 16, features), lambda i: (i, 0, 0))] * 2,
-        out_shape=[half, half],
+        in_specs=[smem, hbm, vmem, vmem, vmem, hbm],
+        out_specs=vmem,
+        out_shape=pltpu.VMEM((2 * frames, channels // 2), BF16),
         scratch_shapes=[
-            pltpu.VMEM((count, frames, BLOCK), BF16),
+            pltpu.VMEM((count, frames, width), BF16),
             pltpu.VMEM(taps.shape, F32),
-            pltpu.VMEM(signal.shape, BF16),
-            pltpu.VMEM((groups, frames + 2 * RIM, LANES), F32),
-            pltpu.VMEM((groups, frames + 2 * RIM, LANES), F32),
-            pltpu.VMEM((groups, 48, LANES), F32),
-            pltpu.VMEM((frames, BLOCK), BF16),
-            pltpu.SemaphoreType.DMA((count + 2,)),
+            pltpu.VMEM((rows, LANES), F32),
+            pltpu.VMEM((rows, LANES), F32),
+            pltpu.VMEM((48, LANES), F32),
+            pltpu.SemaphoreType.DMA((count + 1,)),
         ],
         compiler_params=PARAMS,
-        name="conv_product",
-    )(core, block, low, high, taps, signal)
-
-
-def pair_kernel(keep_ref, received_ref, pair_ref):
-    pair_ref[...] = (keep_ref[...] + received_ref[...]).astype(BF16)
+        name="activation",
+    )(core, block, other, near, far, taps)
+
+
+def product_kernel(core_ref, act_ref, own_ref, other_ref, product_ref):
+    frames = own_ref.shape[0]
+    core = core_ref[0]
+
+    def part(first, signal_ref):
+        act = act_ref[pl.ds(pl.multiple_of(first, frames), frames)]
+        return lax.dot_general(
+            act, signal_ref[...], (((0,), (0,)), ((), ())), preferred_element_type=F32
+        )
+
+    total = part(frames * core, own_ref) + part(frames * (1 - core), other_ref)
+    blocks, _, quarter, owned, features = product_ref.shape
+    pieces = total.reshape(blocks, quarter, 2, owned, features).astype(BF16)
+    for parity in range(2):
+        product_ref[:, lax.rem(parity + core_ref[1], 2)] = pieces[:, :, parity]
 
 
 def merge_kernel(inverse_root, parts_ref, carried_ref, right_ref, merged_ref, left_ref):
@@ -252,9 +244,11 @@
     error_ref[...] = merged_ref[...] - estimate
 
 
-def call(kernel, outs, *args, scratch=()):
+def call(kernel, outs, *args, smem=0, scratch=()):
+    spaces = [pltpu.SMEM] * smem + [pltpu.VMEM] * (len(args) - smem)
     return pl.pallas_call(
         kernel,
+        in_specs=[pl.BlockSpec(memory_space=space) for space in spaces],
         out_shape=[jax.ShapeDtypeStruct(out, F32) if isinstance(out, tuple) else out for out in outs],
         scratch_shapes=list(scratch),
         compiler_params=PARAMS,
@@ -262,8 +256,8 @@
     )(*args)
 
 
-def exchange(block, axes):
-    return lax.all_to_all(block, axes, 0, 0, tiled=True)
+def exchange(block, axes, groups=None):
+    return lax.all_to_all(block, axes, 0, 0, tiled=True, axis_index_groups=groups)
 
 
 def local(gated_input, upstream, depth_kernel, carried_error, right_init):
@@ -274,20 +268,41 @@
     features = upstream.shape[2]
     rank = right_init.shape[1]
     owned = channels // contexts
-    forward = [(i, i + 1) for i in range(contexts - 1)]
-    backward = [(target, source) for source, target in forward]
-    low = lax.ppermute(block[frames - RIM :], CTX, forward)
-    high = lax.ppermute(block[:RIM], CTX, backward)
-    core = lax.axis_index("c").reshape(1)
-    keep, send = conv_product(core, block, low, high, depth_kernel, upstream[0])
-    received = lax.ppermute(send, "c", [(0, 1), (1, 0)])
-    (pair_sum,) = call(pair_kernel, [pltpu.VMEM(keep.shape, BF16)], keep, received)
+    core = lax.axis_index("c")
+    swap = [(0, 1), (1, 0)]
+    ends = lax.dynamic_slice_in_dim(block, core * (frames - RIM), RIM, axis=0)
+    one = [(i, i + 1 if i % 2 else i - 1) for i in range(1, contexts - 1)]
+    two = [(i, i + 2 if i % 2 else i - 2) for i in range(1, contexts - 1)]
+    ends, block = lax.optimization_barrier((ends, block))
+    near = lax.ppermute(ends, CTX, one)
+    far = lax.ppermute(ends, CTX, two)
+    other = lax.ppermute(block, "c", swap)
+    signal = upstream[0]
+    other_signal = lax.ppermute(signal, "c", swap)
+    depth = lax.axis_size("z")
+    side = [(2 * z) // depth for z in range(depth)]
+    teams = [
+        [2 * chip + (team + side[chip % depth]) % 2 for chip in range(contexts // 2)]
+        for team in range(2)
+    ]
+    team = lax.rem(core + (2 * lax.axis_index("z")) // depth, 2)
+    core = jnp.stack([core, team])
+    act = activation(core, block, other, near, far, depth_kernel)
+    (product,) = call(
+        product_kernel,
+        [pltpu.VMEM((channels // 256, 2, 4, owned, features), BF16)],
+        core,
+        act,
+        signal,
+        other_signal,
+        smem=1,
+    )
     inverse_root = 1.0 / math.sqrt(frames * contexts)
     row = (owned, features)
     merged, left_parts = call(
         functools.partial(merge_kernel, inverse_root),
         [row, pltpu.VMEM((replicas, owned // 2, 2 * rank), F32)],
-        exchange(pair_sum, CHIPS),
+        exchange(product.reshape(channels // 32, owned, features), CTX, teams),
         carried_error[0],
         right_init.T,
     )

time: 137 us -> 134 us (0.978)
  starting transfers between devices: 12.7 us -> 16.6 us
  waiting for transfers between devices: 5.16 us -> 1.48 us
  blocking collectives: 102 us -> 99.3 us
    ppermute x3 -> x4, starting transfers between devices: 12.7 us -> 16.6 us  [the longest x1 8.78 us: local(): other = lax.ppermute(block, 'c', swap)]
    ppermute x3 -> x4, waiting for transfers between devices: 5.16 us -> 1.48 us  [the longest x1 1.48 us: local(): near = lax.ppermute(ends, CTX, one)]
    all_to_all x5, blocking collectives: 102 us -> 99.3 us  [exchange(): lax.all_to_all(block, axes, 0, 0, tiled=True, axis_index_groups=groups)]
  transfers between devices with their start and end apart: 3 -> 4, of which waited for: 2 -> 1; matrix products, arithmetic and copies ran while one was open for 0% -> 0% of each run, Pallas kernels for 0% -> 6%
where the time goes in v5:
time: 134 us; the launch traced here: 133 us
  blocking collectives  99.3 us (74%)
  starting transfers between devices  16.6 us (12%)
  Pallas kernels  14.2 us (11%)
  waiting for transfers between devices  1.48 us (1%)
    all_to_all x5, blocking collectives, exchange(): lax.all_to_all(block, axes, 0, 0, tiled=True, axis_index_groups=groups)  99.3 us
    ppermute x1, starting transfers between devices, local(): other = lax.ppermute(block, 'c', swap)  8.78 us
    pallas_call x1, Pallas kernels, activation(): pl.pallas_call(conv_kernel, in_specs=[smem, hbm, vmem, vmem, vmem, hbm],...  7.99 us
    pallas_call x6, Pallas kernels, call(): pl.pallas_call(kernel, in_specs=[pl.BlockSpec(memory_space=space) for spa...  6.24 us
    ppermute x1, starting transfers between devices, local(): near = lax.ppermute(ends, CTX, one)  4.65 us
  transfers between devices with their start and end apart: 4, of which 1 were waited for; matrix products, arithmetic and copies ran while one was open for 0% of the time, Pallas kernels for 6%

profile of v5, /device:TPU:1, one launch (start us, length us, event | category | flops | bytes accessed | tf_op | source)
XLA Modules:
  0.0 133.3 jit_solution(745886354678875659)
XLA Ops:
  0.6 0.8 dynamic-slice_bitcast_fusion
  1.4 8.8 %collective-permute-start = (bf16[768,1024]{1,0:T(8,128)(2,1)}, bf16[768,1024]{1,0:T(8,128)(2,1)S(1)}, u32[]{:S(2)}, u32[]{:S(2)}) collective-permute-start(bf16[768,1024]{1,0:T(8,128)(2,1)} %bitcast.16), channel_id=1, source_target_pairs={{0,1},{1,0},{2,3},{3,2},{4,5},{5,4},{6,7},{7,6},{8,9},{9,8},{10,11... | collective-permute-start | bytes 4718600 | tf_op jit(solution)/shard_map/ppermute | solution.py:279
  10.2 1.9 %collective-permute-start.3 = (bf16[768,1024]{1,0:T(8,128)(2,1)}, bf16[768,1024]{1,0:T(8,128)(2,1)S(1)}, u32[]{:S(2)}, u32[]{:S(2)}) collective-permute-start(bf16[768,1024]{1,0:T(8,128)(2,1)} %bitcast.12), channel_id=1, source_target_pairs={{0,1},{1,0},{2,3},{3,2},{4,5},{5,4},{6,7},{7,6},{8,9},{9,8},{10,11... | collective-permute-start | bytes 4718600 | tf_op jit(solution)/shard_map/ppermute | solution.py:281
  12.1 1.3 collective-permute-start.2
  13.4 4.7 %collective-permute-start.1 = (bf16[16,1024]{1,0:T(8,128)(2,1)S(1)}, bf16[16,1024]{1,0:T(8,128)(2,1)S(1)}, u32[]{:S(2)}, u32[]{:S(2)}) collective-permute-start(bf16[16,1024]{1,0:T(8,128)(2,1)S(1)} %dynamic-slice_bitcast_fusion), channel_id=1, source_target_pairs={{1,2},{2,1},{3,4},{4,3},{5,6},{6,5},{7,8},{8,7},{9,10},{10,9},{11,... | collective-permute-start | bytes 98312 | tf_op jit(solution)/shard_map/ppermute | solution.py:277
  18.1 0.1 pad_add_fusion.core_ref
  18.2 0.0 collective-permute-done.2.far_ref
  18.2 1.5 %collective-permute-done.1.near_ref = bf16[16,1024]{1,0:T(8,128)(2,1)S(1)} collective-permute-done((bf16[16,1024]{1,0:T(8,128)(2,1)S(1)}, bf16[16,1024]{1,0:T(8,128)(2,1)S(1)}, u32[]{:S(2)}, u32[]{:S(2)}) %collective-permute-start.1) | collective-permute-done | bytes 32800 | tf_op jit(solution)/shard_map/ppermute | solution.py:277
  19.7 0.0 collective-permute-done.other_ref
  19.7 8.0 %activation.1.act_ref = bf16[1536,512]{1,0:T(8,128)(2,1)S(1)} custom-call(s32[2]{0:T(128)S(1)} %pad_add_fusion.core_ref, bf16[768,1024]{1,0:T(8,128)(2,1)} %bitcast.17, bf16[768,1024]{1,0:T(8,128)(2,1)S(1)} %collective-permute-done.other_ref, bf16[16,1024]{1,0:T(8,128)(2,1)S(1)} %collective-permute-done.1.near_ref, ...), custom_call_target="tpu_custom_call" | custom-call | tf_op jit(solution)/shard_map/activation/pallas_call | solution.py:128
  27.7 0.0 collective-permute-done.3.other_ref
  27.7 0.0 copy-done
  27.7 2.4 %product_kernel.1 = bf16[4,2,4,16,1024]{4,3,2,1,0:T(8,128)(2,1)S(1)} custom-call(s32[2]{0:T(128)S(1)} %pad_add_fusion.core_ref, bf16[1536,512]{1,0:T(8,128)(2,1)S(1)} %activation.1.act_ref, bf16[768,1024]{1,0:T(8,128)(2,1)S(1)} %bitcast.13, bf16[768,1024]{1,0:T(8,128)(2,1)S(1)} %collective-permute-done.3.other_ref), custom_call_target="tpu_custom_call" | custom-call | tf_op jit(solution)/shard_map/product_kernel/pallas_call | solution.py:249
  30.1 0.0 copy-start.1
  30.1 0.0 copy-start.2
  30.1 36.8 %all_to_all.25.parts_ref = bf16[32,16,1024]{2,1,0:T(8,128)(2,1)S(1)} all-to-all(bf16[32,16,1024]{2,1,0:T(8,128)(2,1)S(1)} %bitcast.11), channel_id=1, replica_groups={{0,2,4,6,9,11,13,15,16,18,20,22,25,27,29,31,32,34,36,38,41,43,45,47,48,..., dimensions={0} | all-to-all | bytes 2097152 | tf_op jit(solution)/shard_map/all_to_all | solution.py:260
  66.9 0.0 copy-done.1
  66.9 0.5 merge_kernel.1
  67.4 15.3 %all_to_all.26.parts_ref = f32[8,8,128]{2,1,0:T(8,128)S(1)} all-to-all(f32[8,8,128]{2,1,0:T(8,128)S(1)} %get-tuple-element.14), channel_id=1, replica_groups=mesh['x'=4,'h'=2,'y'=4,'z'=8,'c'=2] {'x','h'}, dimensions={0} | all-to-all | bytes 65536 | tf_op jit(solution)/shard_map/all_to_all | solution.py:260
  82.7 0.5 term_kernel.1
  83.3 15.8 %all_to_all.27.parts_ref = f32[32,2,1152]{2,1,0:T(2,128)S(1)} all-to-all(f32[32,2,1152]{2,1,0:T(2,128)S(1)} %get-tuple-element.16), channel_id=1, replica_groups=mesh['x'=4,'h'=2,'y'=4,'z'=8,'c'=2] {'x','z'}, dimensions={0} | all-to-all | bytes 589824 | tf_op jit(solution)/shard_map/all_to_all | solution.py:260
  99.1 16.4 %all_to_all.28.parts_ref = f32[16,2,1152]{2,1,0:T(2,128)S(1)} all-to-all(f32[16,2,1152]{2,1,0:T(2,128)S(1)} %total_kernel.2), channel_id=1, replica_groups=mesh['x'=4,'h'=2,'y'=4,'z'=8,'c'=2] {'h','y','c'}, dimensions={0} | all-to-all | bytes 294912 | tf_op jit(solution)/shard_map/all_to_all | solution.py:260
  115.6 14.9 %all_to_all.29.rows_ref = f32[32,2,1152]{2,1,0:T(2,128)S(1)} all-to-all(f32[32,2,1152]{2,1,0:T(2,128)S(1)} %total_kernel.3), channel_id=1, replica_groups=mesh['x'=4,'h'=2,'y'=4,'z'=8,'c'=2] {'x','z'}, dimensions={0} | all-to-all | bytes 589824 | tf_op jit(solution)/shard_map/all_to_all | solution.py:260
  130.5 2.8 %finish_kernel.1 = (f32[64,1024]{1,0:T(8,128)}, f32[16,1024]{1,0:T(8,128)}, f32[16,1024]{1,0:T(8,128)}) custom-call(f32[32,2,1152]{2,1,0:T(2,128)S(1)} %all_to_all.29.rows_ref, f32[16,64]{1,0:T(8,128)S(1)} %get-tuple-element.17.left_ref, f32[16,1024]{1,0:T(8,128)S(1)} %get-tuple-element.15.merged_ref), custom_call_target="tpu_custom_call" | custom-call | tf_op jit(solution)/shard_map/finish_kernel/pallas_call | solution.py:249
  (4 shorter events, 0.1 us)
Async XLA Ops:
  1.4 18.3 %collective-permute-start = (bf16[768,1024]{1,0:T(8,128)(2,1)}, bf16[768,1024]{1,0:T(8,128)(2,1)S(1)}, u32[]{:S(2)}, u32[]{:S(2)}) collective-permute-start(bf16[768,1024]{1,0:T(8,128)(2,1)} %bitcast.16), channel_id=1, source_target_pairs={{0,1},{1,0},{2,3},{3,2},{4,5},{5,4},{6,7},{7,6},{8,9},{9,8},{10,11... | collective-permute-start | bytes 4718600 | tf_op jit(solution)/shard_map/ppermute | solution.py:279
  10.2 17.5 %collective-permute-start.3 = (bf16[768,1024]{1,0:T(8,128)(2,1)}, bf16[768,1024]{1,0:T(8,128)(2,1)S(1)}, u32[]{:S(2)}, u32[]{:S(2)}) collective-permute-start(bf16[768,1024]{1,0:T(8,128)(2,1)} %bitcast.12), channel_id=1, source_target_pairs={{0,1},{1,0},{2,3},{3,2},{4,5},{5,4},{6,7},{7,6},{8,9},{9,8},{10,11... | collective-permute-start | bytes 4718600 | tf_op jit(solution)/shard_map/ppermute | solution.py:281
  12.1 6.1 %collective-permute-start.2 = (bf16[16,1024]{1,0:T(8,128)(2,1)S(1)}, bf16[16,1024]{1,0:T(8,128)(2,1)S(1)}, u32[]{:S(2)}, u32[]{:S(2)}) collective-permute-start(bf16[16,1024]{1,0:T(8,128)(2,1)S(1)} %dynamic-slice_bitcast_fusion), channel_id=1, source_target_pairs={{1,3},{2,0},{3,5},{4,2},{5,7},{6,4},{7,9},{8,6},{9,11},{10,8},{11,... | collective-permute-start | bytes 98312 | tf_op jit(solution)/shard_map/ppermute | solution.py:278
  13.4 6.2 %collective-permute-start.1 = (bf16[16,1024]{1,0:T(8,128)(2,1)S(1)}, bf16[16,1024]{1,0:T(8,128)(2,1)S(1)}, u32[]{:S(2)}, u32[]{:S(2)}) collective-permute-start(bf16[16,1024]{1,0:T(8,128)(2,1)S(1)} %dynamic-slice_bitcast_fusion), channel_id=1, source_target_pairs={{1,2},{2,1},{3,4},{4,3},{5,6},{6,5},{7,8},{8,7},{9,10},{10,9},{11,... | collective-permute-start | bytes 98312 | tf_op jit(solution)/shard_map/ppermute | solution.py:277
  18.2 9.5 %copy-start = (bf16[1,768,1024]{2,1,0:T(8,128)(2,1)S(1)}, bf16[1,768,1024]{2,1,0:T(8,128)(2,1)}, u32[]{:S(2)}) copy-start(bf16[1,768,1024]{2,1,0:T(8,128)(2,1)} %param.6) | copy-start | bytes 4718596
  30.1 36.8 %copy-start.1 = (f32[1024,64]{0,1:T(8,128)S(1)}, f32[1024,64]{0,1:T(8,128)}, u32[]{:S(2)}) copy-start(f32[1024,64]{0,1:T(8,128)} %param.9) | copy-start | bytes 786436
  30.1 36.8 %copy-start.2 = (f32[1,16,1024]{2,1,0:T(8,128)S(1)}, f32[1,16,1024]{2,1,0:T(8,128)}, u32[]{:S(2)}) copy-start(f32[1,16,1024]{2,1,0:T(8,128)} %param.8) | copy-start | bytes 196612

commit v6 on v5

--- a/solution.py
+++ b/solution.py
@@ -13,8 +13,8 @@
 HIGHEST = lax.Precision.HIGHEST
 DP = ("x", "h")
 CTX = ("y", "z", "c")
-NEAR = ("x", "z")
-FAR = ("h", "y", "c")
+NEAR = ('y', 'c')
+FAR = ('z',)
 RIM = 16
 LANES = 128
 TILE = 8
@@ -24,14 +24,14 @@
 
 
 def conv_kernel(
-    core_ref, block_hbm, other_ref, near_ref, far_ref, taps_hbm, act_ref,
+    place_ref, block_hbm, other_ref, near_ref, far_ref, taps_hbm, act_ref,
     block_ref, taps_ref, wide_ref, sums_ref, weights_ref, sems,
 ):
     count, frames, width = block_ref.shape
     rows = 2 * frames + 2 * RIM
-    core = core_ref[0]
+    core = place_ref[0]
     lane = lax.broadcasted_iota(jnp.int32, (1, LANES), 1)
-    first = lax.rem(lane // 16, 2) == core_ref[1]
+    first = lax.rem(lane // 16, 2) == place_ref[1]
     own = pl.multiple_of(RIM + frames * core, RIM)
     partner = pl.multiple_of(RIM + frames * (1 - core), RIM)
     pairs = STEP // (2 * TILE)
@@ -116,7 +116,7 @@
     lax.fori_loop(0, count, group, 0)
 
 
-def activation(core, block, other, near, far, taps):
+def activation(place, block, other, near, far, taps):
     frames, channels = block.shape
     width = 2 * LANES
     count = channels // width
@@ -140,12 +140,12 @@
         ],
         compiler_params=PARAMS,
         name="activation",
-    )(core, block, other, near, far, taps)
-
-
-def product_kernel(core_ref, act_ref, own_ref, other_ref, product_ref):
+    )(place, block, other, near, far, taps)
+
+
+def product_kernel(place_ref, act_ref, own_ref, other_ref, product_ref):
     frames = own_ref.shape[0]
-    core = core_ref[0]
+    core = place_ref[0]
 
     def part(first, signal_ref):
         act = act_ref[pl.ds(pl.multiple_of(first, frames), frames)]
@@ -157,10 +157,10 @@
     blocks, _, quarter, owned, features = product_ref.shape
     pieces = total.reshape(blocks, quarter, 2, owned, features).astype(BF16)
     for parity in range(2):
-        product_ref[:, lax.rem(parity + core_ref[1], 2)] = pieces[:, :, parity]
-
-
-def merge_kernel(inverse_root, parts_ref, carried_ref, right_ref, merged_ref, left_ref):
+        product_ref[:, lax.rem(parity + place_ref[1], 2)] = pieces[:, :, parity]
+
+
+def merge_kernel(inverse_root, parts_ref, carried_ref, right_ref, merged_ref, shares_ref):
     total = parts_ref[0].astype(F32)
     for index in range(1, parts_ref.shape[0]):
         total = total + parts_ref[index].astype(F32)
@@ -169,26 +169,33 @@
     left = lax.dot_general(
         merged, right_ref[...], (((1,), (1,)), ((), ())), precision=HIGHEST, preferred_element_type=F32
     )
-    middle = left.shape[0] // 2
-    packed = jnp.concatenate([left[:middle], left[middle:]], axis=1)
-    for index in range(left_ref.shape[0]):
-        left_ref[index] = packed
-
-
-def term_kernel(parts_ref, merged_ref, left_ref, term_ref):
-    packed = parts_ref[0]
+    owned = left.shape[0]
+    packed = jnp.concatenate([left[: owned // 2], left[owned // 2 :]], axis=1)
+    for index in range(shares_ref.shape[0]):
+        shares_ref[index, :owned] = merged[:, LANES * index : LANES * (index + 1)]
+        shares_ref[index, owned:] = packed
+
+
+def term_kernel(place_ref, parts_ref, left_ref, term_ref, gram_ref):
+    total = parts_ref[0]
     for index in range(1, parts_ref.shape[0]):
-        packed = packed + parts_ref[index]
-    rank = left_ref.shape[1]
+        total = total + parts_ref[index]
+    owned, rank = left_ref.shape
+    packed = total[owned:]
     left = jnp.concatenate([packed[:, :rank], packed[:, rank:]], axis=0)
     left_ref[...] = left
-    share = left * (1.0 / parts_ref.shape[0])
-    joined = jnp.concatenate([merged_ref[...], jnp.zeros_like(left), share], axis=1)
-    term = lax.dot_general(
-        left, joined, (((0,), (0,)), ((), ())), precision=HIGHEST, preferred_element_type=F32
-    )
+    dot = functools.partial(
+        lax.dot_general,
+        dimension_numbers=(((0,), (0,)), ((), ())),
+        precision=HIGHEST,
+        preferred_element_type=F32,
+    )
+    term = dot(left, total[:owned])
+    gram_ref[...] = dot(left, jnp.concatenate([jnp.zeros_like(left), left], axis=1))
+    gram = gram_ref[pl.ds(pl.multiple_of(TILE * place_ref[2], TILE), TILE)]
     for index in range(term_ref.shape[0]):
-        term_ref[index] = term[2 * index : 2 * index + 2]
+        term_ref[index, :rank] = term
+        term_ref[index, rank:] = gram
 
 
 def total_kernel(parts_ref, total_ref):
@@ -229,7 +236,8 @@
     rank = left_ref.shape[1]
     features = merged_ref.shape[1]
     for index in range(rows_ref.shape[0]):
-        wide_ref[2 * index : 2 * index + 2] = rows_ref[index]
+        wide_ref[:, LANES * index : LANES * (index + 1)] = rows_ref[index, :rank]
+        wide_ref[TILE * index : TILE * (index + 1), features:] = rows_ref[index, rank:]
     row = lax.broadcasted_iota(jnp.int32, (rank, 2 * rank), 0)
     lane = lax.broadcasted_iota(jnp.int32, (rank, 2 * rank), 1)
     work = eliminate(wide_ref[:, features:] + (row == lane).astype(F32), rank)
@@ -286,12 +294,12 @@
         for team in range(2)
     ]
     team = lax.rem(core + (2 * lax.axis_index("z")) // depth, 2)
-    core = jnp.stack([core, team])
-    act = activation(core, block, other, near, far, depth_kernel)
+    place = jnp.stack([core, team, lax.axis_index(DP)])
+    act = activation(place, block, other, near, far, depth_kernel)
     (product,) = call(
         product_kernel,
         [pltpu.VMEM((channels // 256, 2, 4, owned, features), BF16)],
-        core,
+        place,
         act,
         signal,
         other_signal,
@@ -299,27 +307,32 @@
     )
     inverse_root = 1.0 / math.sqrt(frames * contexts)
     row = (owned, features)
-    merged, left_parts = call(
+    merged, shares = call(
         functools.partial(merge_kernel, inverse_root),
-        [row, pltpu.VMEM((replicas, owned // 2, 2 * rank), F32)],
+        [row, pltpu.VMEM((replicas, owned + owned // 2, LANES), F32)],
         exchange(product.reshape(channels // 32, owned, features), CTX, teams),
         carried_error[0],
         right_init.T,
     )
-    width = features + 2 * rank
     near, far = lax.axis_size(NEAR), lax.axis_size(FAR)
-    near_form = pltpu.VMEM((near, rank // near, width), F32)
-    far_form = pltpu.VMEM((far, rank // near, width), F32)
-    left, term = call(term_kernel, [(owned, rank), near_form], exchange(left_parts, DP), merged)
-    (near_sum,) = call(total_kernel, [far_form], exchange(term, NEAR))
-    (far_sum,) = call(total_kernel, [near_form], exchange(near_sum, FAR))
+    size = (rank + TILE, LANES)
+    left, term = call(
+        term_kernel,
+        [(owned, rank), pltpu.VMEM((near, *size), F32)],
+        place,
+        exchange(shares, DP),
+        smem=1,
+        scratch=[pltpu.VMEM((rank, LANES), F32)],
+    )
+    (near_sum,) = call(total_kernel, [pltpu.VMEM((far, *size), F32)], exchange(term, NEAR))
+    (far_sum,) = call(total_kernel, [pltpu.VMEM((replicas, *size), F32)], exchange(near_sum, FAR))
     right, estimate, error = call(
         functools.partial(finish_kernel, replicas),
         [(rank, features), row, row],
-        exchange(far_sum, NEAR),
+        exchange(far_sum, DP),
         left,
         merged,
-        scratch=[pltpu.VMEM((rank, width), F32)],
+        scratch=[pltpu.VMEM((rank, features + 2 * rank), F32)],
     )
     return right.T, estimate, error[None]
 

time: 134 us -> 132 us (0.985)
  blocking collectives: 99.3 us -> 95.9 us
    all_to_all x5, blocking collectives: 99.3 us -> 95.9 us  [exchange(): lax.all_to_all(block, axes, 0, 0, tiled=True, axis_index_groups=groups)]
where the time goes in v6:
time: 132 us; the launch traced here: 130 us
  blocking collectives  95.9 us (73%)
  starting transfers between devices  16.6 us (13%)
  Pallas kernels  14.5 us (11%)
  waiting for transfers between devices  1.48 us (1%)
    all_to_all x5, blocking collectives, exchange(): lax.all_to_all(block, axes, 0, 0, tiled=True, axis_index_groups=groups)  95.9 us
    ppermute x1, starting transfers between devices, local(): other = lax.ppermute(block, 'c', swap)  8.78 us
    pallas_call x1, Pallas kernels, activation(): pl.pallas_call(conv_kernel, in_specs=[smem, hbm, vmem, vmem, vmem, hbm],...  7.99 us
    pallas_call x6, Pallas kernels, call(): pl.pallas_call(kernel, in_specs=[pl.BlockSpec(memory_space=space) for spa...  6.5 us
    ppermute x1, starting transfers between devices, local(): near = lax.ppermute(ends, CTX, one)  4.65 us
  transfers between devices with their start and end apart: 4, of which 1 were waited for; matrix products, arithmetic and copies ran while one was open for 0% of the time, Pallas kernels for 6%

profile of v6, /device:TPU:1, one launch (start us, length us, event | category | flops | bytes accessed | tf_op | source)
XLA Modules:
  0.0 130.1 jit_solution(8587486869677287196)
XLA Ops:
  0.6 0.8 dynamic-slice_bitcast_fusion
  1.4 8.8 %collective-permute-start = (bf16[768,1024]{1,0:T(8,128)(2,1)}, bf16[768,1024]{1,0:T(8,128)(2,1)S(1)}, u32[]{:S(2)}, u32[]{:S(2)}) collective-permute-start(bf16[768,1024]{1,0:T(8,128)(2,1)} %bitcast.17), channel_id=1, source_target_pairs={{0,1},{1,0},{2,3},{3,2},{4,5},{5,4},{6,7},{7,6},{8,9},{9,8},{10,11... | collective-permute-start | bytes 4718600 | tf_op jit(solution)/shard_map/ppermute | solution.py:287
  10.2 1.9 %collective-permute-start.3 = (bf16[768,1024]{1,0:T(8,128)(2,1)}, bf16[768,1024]{1,0:T(8,128)(2,1)S(1)}, u32[]{:S(2)}, u32[]{:S(2)}) collective-permute-start(bf16[768,1024]{1,0:T(8,128)(2,1)} %bitcast.13), channel_id=1, source_target_pairs={{0,1},{1,0},{2,3},{3,2},{4,5},{5,4},{6,7},{7,6},{8,9},{9,8},{10,11... | collective-permute-start | bytes 4718600 | tf_op jit(solution)/shard_map/ppermute | solution.py:289
  12.1 1.3 collective-permute-start.2
  13.4 4.7 %collective-permute-start.1 = (bf16[16,1024]{1,0:T(8,128)(2,1)S(1)}, bf16[16,1024]{1,0:T(8,128)(2,1)S(1)}, u32[]{:S(2)}, u32[]{:S(2)}) collective-permute-start(bf16[16,1024]{1,0:T(8,128)(2,1)S(1)} %dynamic-slice_bitcast_fusion), channel_id=1, source_target_pairs={{1,2},{2,1},{3,4},{4,3},{5,6},{6,5},{7,8},{8,7},{9,10},{10,9},{11,... | collective-permute-start | bytes 98312 | tf_op jit(solution)/shard_map/ppermute | solution.py:285
  18.1 0.1 pad_add_fusion.place_ref
  18.2 0.0 collective-permute-done.2.far_ref
  18.2 1.5 %collective-permute-done.1.near_ref = bf16[16,1024]{1,0:T(8,128)(2,1)S(1)} collective-permute-done((bf16[16,1024]{1,0:T(8,128)(2,1)S(1)}, bf16[16,1024]{1,0:T(8,128)(2,1)S(1)}, u32[]{:S(2)}, u32[]{:S(2)}) %collective-permute-start.1) | collective-permute-done | bytes 32800 | tf_op jit(solution)/shard_map/ppermute | solution.py:285
  19.7 0.0 collective-permute-done.other_ref
  19.7 8.0 %activation.1.act_ref = bf16[1536,512]{1,0:T(8,128)(2,1)S(1)} custom-call(s32[3]{0:T(128)S(1)} %pad_add_fusion.place_ref, bf16[768,1024]{1,0:T(8,128)(2,1)} %bitcast.18, bf16[768,1024]{1,0:T(8,128)(2,1)S(1)} %collective-permute-done.other_ref, bf16[16,1024]{1,0:T(8,128)(2,1)S(1)} %collective-permute-done.1.near_ref, ...), custom_call_target="tpu_custom_call" | custom-call | tf_op jit(solution)/shard_map/activation/pallas_call | solution.py:128
  27.7 0.0 collective-permute-done.3.other_ref
  27.7 0.0 copy-done
  27.7 2.4 %product_kernel.1 = bf16[4,2,4,16,1024]{4,3,2,1,0:T(8,128)(2,1)S(1)} custom-call(s32[3]{0:T(128)S(1)} %pad_add_fusion.place_ref, bf16[1536,512]{1,0:T(8,128)(2,1)S(1)} %activation.1.act_ref, bf16[768,1024]{1,0:T(8,128)(2,1)S(1)} %bitcast.14, bf16[768,1024]{1,0:T(8,128)(2,1)S(1)} %collective-permute-done.3.other_ref), custom_call_target="tpu_custom_call" | custom-call | tf_op jit(solution)/shard_map/product_kernel/pallas_call | solution.py:257
  30.1 0.0 copy-start.1
  30.1 0.0 copy-start.2
  30.1 36.8 %all_to_all.25.parts_ref = bf16[32,16,1024]{2,1,0:T(8,128)(2,1)S(1)} all-to-all(bf16[32,16,1024]{2,1,0:T(8,128)(2,1)S(1)} %bitcast.12), channel_id=1, replica_groups={{0,2,4,6,9,11,13,15,16,18,20,22,25,27,29,31,32,34,36,38,41,43,45,47,48,..., dimensions={0} | all-to-all | bytes 2097152 | tf_op jit(solution)/shard_map/all_to_all | solution.py:268
  66.9 0.0 copy-done.1
  66.9 0.5 merge_kernel.1
  67.4 15.7 %all_to_all.26.parts_ref = f32[8,24,128]{2,1,0:T(8,128)S(1)} all-to-all(f32[8,24,128]{2,1,0:T(8,128)S(1)} %get-tuple-element.14), channel_id=1, replica_groups=mesh['x'=4,'h'=2,'y'=4,'z'=8,'c'=2] {'x','h'}, dimensions={0} | all-to-all | bytes 196608 | tf_op jit(solution)/shard_map/all_to_all | solution.py:268
  83.1 0.9 term_kernel.1
  84.0 16.8 %all_to_all.27.parts_ref = f32[8,72,128]{2,1,0:T(8,128)S(1)} all-to-all(f32[8,72,128]{2,1,0:T(8,128)S(1)} %get-tuple-element.15), channel_id=1, replica_groups=mesh['x'=4,'h'=2,'y'=4,'z'=8,'c'=2] {'y','c'}, dimensions={0} | all-to-all | bytes 589824 | tf_op jit(solution)/shard_map/all_to_all | solution.py:268
  100.8 13.6 %all_to_all.28.parts_ref = f32[8,72,128]{2,1,0:T(8,128)S(1)} all-to-all(f32[8,72,128]{2,1,0:T(8,128)S(1)} %total_kernel.2), channel_id=1, replica_groups=mesh['x'=4,'h'=2,'y'=4,'z'=8,'c'=2] {'z'}, dimensions={0} | all-to-all | bytes 589824 | tf_op jit(solution)/shard_map/all_to_all | solution.py:268
  114.5 12.9 %all_to_all.29.rows_ref = f32[8,72,128]{2,1,0:T(8,128)S(1)} all-to-all(f32[8,72,128]{2,1,0:T(8,128)S(1)} %total_kernel.3), channel_id=1, replica_groups=mesh['x'=4,'h'=2,'y'=4,'z'=8,'c'=2] {'x','h'}, dimensions={0} | all-to-all | bytes 589824 | tf_op jit(solution)/shard_map/all_to_all | solution.py:268
  127.4 2.7 %finish_kernel.1 = (f32[64,1024]{1,0:T(8,128)}, f32[16,1024]{1,0:T(8,128)}, f32[16,1024]{1,0:T(8,128)}) custom-call(f32[8,72,128]{2,1,0:T(8,128)S(1)} %all_to_all.29.rows_ref, f32[16,64]{1,0:T(8,128)S(1)} %get-tuple-element.16.left_ref, f32[16,1024]{1,0:T(8,128)S(1)} %get-tuple-element.17.merged_ref), custom_call_target="tpu_custom_call" | custom-call | tf_op jit(solution)/shard_map/finish_kernel/pallas_call | solution.py:257
  (4 shorter events, 0.1 us)
Async XLA Ops:
  1.4 18.3 %collective-permute-start = (bf16[768,1024]{1,0:T(8,128)(2,1)}, bf16[768,1024]{1,0:T(8,128)(2,1)S(1)}, u32[]{:S(2)}, u32[]{:S(2)}) collective-permute-start(bf16[768,1024]{1,0:T(8,128)(2,1)} %bitcast.17), channel_id=1, source_target_pairs={{0,1},{1,0},{2,3},{3,2},{4,5},{5,4},{6,7},{7,6},{8,9},{9,8},{10,11... | collective-permute-start | bytes 4718600 | tf_op jit(solution)/shard_map/ppermute | solution.py:287
  10.2 17.5 %collective-permute-start.3 = (bf16[768,1024]{1,0:T(8,128)(2,1)}, bf16[768,1024]{1,0:T(8,128)(2,1)S(1)}, u32[]{:S(2)}, u32[]{:S(2)}) collective-permute-start(bf16[768,1024]{1,0:T(8,128)(2,1)} %bitcast.13), channel_id=1, source_target_pairs={{0,1},{1,0},{2,3},{3,2},{4,5},{5,4},{6,7},{7,6},{8,9},{9,8},{10,11... | collective-permute-start | bytes 4718600 | tf_op jit(solution)/shard_map/ppermute | solution.py:289
  12.1 6.1 %collective-permute-start.2 = (bf16[16,1024]{1,0:T(8,128)(2,1)S(1)}, bf16[16,1024]{1,0:T(8,128)(2,1)S(1)}, u32[]{:S(2)}, u32[]{:S(2)}) collective-permute-start(bf16[16,1024]{1,0:T(8,128)(2,1)S(1)} %dynamic-slice_bitcast_fusion), channel_id=1, source_target_pairs={{1,3},{2,0},{3,5},{4,2},{5,7},{6,4},{7,9},{8,6},{9,11},{10,8},{11,... | collective-permute-start | bytes 98312 | tf_op jit(solution)/shard_map/ppermute | solution.py:286
  13.4 6.2 %collective-permute-start.1 = (bf16[16,1024]{1,0:T(8,128)(2,1)S(1)}, bf16[16,1024]{1,0:T(8,128)(2,1)S(1)}, u32[]{:S(2)}, u32[]{:S(2)}) collective-permute-start(bf16[16,1024]{1,0:T(8,128)(2,1)S(1)} %dynamic-slice_bitcast_fusion), channel_id=1, source_target_pairs={{1,2},{2,1},{3,4},{4,3},{5,6},{6,5},{7,8},{8,7},{9,10},{10,9},{11,... | collective-permute-start | bytes 98312 | tf_op jit(solution)/shard_map/ppermute | solution.py:285
  18.2 9.5 %copy-start = (bf16[1,768,1024]{2,1,0:T(8,128)(2,1)S(1)}, bf16[1,768,1024]{2,1,0:T(8,128)(2,1)}, u32[]{:S(2)}) copy-start(bf16[1,768,1024]{2,1,0:T(8,128)(2,1)} %param.6) | copy-start | bytes 4718596
  30.1 36.8 %copy-start.1 = (f32[1024,64]{0,1:T(8,128)S(1)}, f32[1024,64]{0,1:T(8,128)}, u32[]{:S(2)}) copy-start(f32[1024,64]{0,1:T(8,128)} %param.9) | copy-start | bytes 786436
  30.1 36.8 %copy-start.2 = (f32[1,16,1024]{2,1,0:T(8,128)S(1)}, f32[1,16,1024]{2,1,0:T(8,128)}, u32[]{:S(2)}) copy-start(f32[1,16,1024]{2,1,0:T(8,128)} %param.8) | copy-start | bytes 196612

commit v7 on v6

--- a/solution.py
+++ b/solution.py
@@ -13,8 +13,7 @@
 HIGHEST = lax.Precision.HIGHEST
 DP = ("x", "h")
 CTX = ("y", "z", "c")
-NEAR = ('y', 'c')
-FAR = ('z',)
+SPREAD = ("x", "h", "c")
 RIM = 16
 LANES = 128
 TILE = 8
@@ -171,26 +170,35 @@
     )
     owned = left.shape[0]
     packed = jnp.concatenate([left[: owned // 2], left[owned // 2 :]], axis=1)
+    copies = shares_ref.shape[0] * LANES // merged.shape[1]
     for index in range(shares_ref.shape[0]):
-        shares_ref[index, :owned] = merged[:, LANES * index : LANES * (index + 1)]
+        first = LANES * (index // copies)
+        shares_ref[index, :owned] = merged[:, first : first + LANES]
         shares_ref[index, owned:] = packed
 
 
-def term_kernel(place_ref, parts_ref, left_ref, term_ref, gram_ref):
-    total = parts_ref[0]
-    for index in range(1, parts_ref.shape[0]):
-        total = total + parts_ref[index]
+def term_kernel(place_ref, parts_ref, left_ref, term_ref, rows_ref, gram_ref):
     owned, rank = left_ref.shape
-    packed = total[owned:]
-    left = jnp.concatenate([packed[:, :rank], packed[:, rank:]], axis=0)
-    left_ref[...] = left
+    sources = rows_ref.shape[0]
+    lefts, means = [], []
+    for source in range(sources):
+        total = parts_ref[source]
+        for index in range(source + sources, parts_ref.shape[0], sources):
+            total = total + parts_ref[index]
+        packed = total[owned:]
+        left = jnp.concatenate([packed[:, :rank], packed[:, rank:]], axis=0)
+        rows_ref[source] = left
+        lefts.append(left)
+        means.append(total[:owned])
+    left_ref[...] = rows_ref[place_ref[3]]
+    left, mean = jnp.concatenate(lefts, axis=0), jnp.concatenate(means, axis=0)
     dot = functools.partial(
         lax.dot_general,
         dimension_numbers=(((0,), (0,)), ((), ())),
         precision=HIGHEST,
         preferred_element_type=F32,
     )
-    term = dot(left, total[:owned])
+    term = dot(left, mean)
     gram_ref[...] = dot(left, jnp.concatenate([jnp.zeros_like(left), left], axis=1))
     gram = gram_ref[pl.ds(pl.multiple_of(TILE * place_ref[2], TILE), TILE)]
     for index in range(term_ref.shape[0]):
@@ -294,7 +302,7 @@
         for team in range(2)
     ]
     team = lax.rem(core + (2 * lax.axis_index("z")) // depth, 2)
-    place = jnp.stack([core, team, lax.axis_index(DP)])
+    place = jnp.stack([core, team, lax.axis_index(DP), lax.axis_index("c")])
     act = activation(place, block, other, near, far, depth_kernel)
     (product,) = call(
         product_kernel,
@@ -307,29 +315,29 @@
     )
     inverse_root = 1.0 / math.sqrt(frames * contexts)
     row = (owned, features)
+    spread = lax.axis_size(SPREAD)
     merged, shares = call(
         functools.partial(merge_kernel, inverse_root),
-        [row, pltpu.VMEM((replicas, owned + owned // 2, LANES), F32)],
+        [row, pltpu.VMEM((spread, owned + owned // 2, LANES), F32)],
         exchange(product.reshape(channels // 32, owned, features), CTX, teams),
         carried_error[0],
         right_init.T,
     )
-    near, far = lax.axis_size(NEAR), lax.axis_size(FAR)
     size = (rank + TILE, LANES)
     left, term = call(
         term_kernel,
-        [(owned, rank), pltpu.VMEM((near, *size), F32)],
+        [(owned, rank), pltpu.VMEM((lax.axis_size("y"), *size), F32)],
         place,
-        exchange(shares, DP),
+        exchange(shares, SPREAD),
         smem=1,
-        scratch=[pltpu.VMEM((rank, LANES), F32)],
-    )
-    (near_sum,) = call(total_kernel, [pltpu.VMEM((far, *size), F32)], exchange(term, NEAR))
-    (far_sum,) = call(total_kernel, [pltpu.VMEM((replicas, *size), F32)], exchange(near_sum, FAR))
+        scratch=[pltpu.VMEM((spread // replicas, owned, rank), F32), pltpu.VMEM((rank, LANES), F32)],
+    )
+    (total,) = call(total_kernel, [pltpu.VMEM((lax.axis_size("z"), *size), F32)], exchange(term, "y"))
+    (total,) = call(total_kernel, [pltpu.VMEM((replicas, *size), F32)], exchange(total, "z"))
     right, estimate, error = call(
         functools.partial(finish_kernel, replicas),
         [(rank, features), row, row],
-        exchange(far_sum, DP),
+        exchange(total, DP),
         left,
         merged,
         scratch=[pltpu.VMEM((rank, features + 2 * rank), F32)],

time: 132 us -> 130 us (0.985)
  the two profiles are of different devices: /device:TPU:1 before, /device:TPU:2 now
where the time goes in v7:
time: 130 us; the launch traced here: 129 us
  blocking collectives  103 us (79%)
  Pallas kernels  14.5 us (11%)
  starting transfers between devices  6.27 us (5%)
  waiting for transfers between devices  4.09 us (3%)
    all_to_all x5, blocking collectives, exchange(): lax.all_to_all(block, axes, 0, 0, tiled=True, axis_index_groups=groups)  103 us
    pallas_call x1, Pallas kernels, activation(): pl.pallas_call(conv_kernel, in_specs=[smem, hbm, vmem, vmem, vmem, hbm],...  7.99 us
    pallas_call x6, Pallas kernels, call(): pl.pallas_call(kernel, in_specs=[pl.BlockSpec(memory_space=space) for spa...  6.5 us
    ppermute x1, waiting for transfers between devices, local(): far = lax.ppermute(ends, CTX, two)  4.09 us
  transfers between devices with their start and end apart: 4, of which 1 were waited for; matrix products, arithmetic and copies ran while one was open for 0% of the time, Pallas kernels for 6%

profile of v7, /device:TPU:2, one launch (start us, length us, event | category | flops | bytes accessed | tf_op | source)
XLA Modules:
  0.0 129.2 jit_solution(18039048191804771594)
XLA Ops:
  0.6 0.8 dynamic-slice_bitcast_fusion
  1.4 1.9 %collective-permute-start = (bf16[768,1024]{1,0:T(8,128)(2,1)}, bf16[768,1024]{1,0:T(8,128)(2,1)S(1)}, u32[]{:S(2)}, u32[]{:S(2)}) collective-permute-start(bf16[768,1024]{1,0:T(8,128)(2,1)} %bitcast.17), channel_id=1, source_target_pairs={{0,1},{1,0},{2,3},{3,2},{4,5},{5,4},{6,7},{7,6},{8,9},{9,8},{10,11... | collective-permute-start | bytes 4718600 | tf_op jit(solution)/shard_map/ppermute | solution.py:295
  3.3 2.4 %collective-permute-start.3 = (bf16[768,1024]{1,0:T(8,128)(2,1)}, bf16[768,1024]{1,0:T(8,128)(2,1)S(1)}, u32[]{:S(2)}, u32[]{:S(2)}) collective-permute-start(bf16[768,1024]{1,0:T(8,128)(2,1)} %bitcast.13), channel_id=1, source_target_pairs={{0,1},{1,0},{2,3},{3,2},{4,5},{5,4},{6,7},{7,6},{8,9},{9,8},{10,11... | collective-permute-start | bytes 4718600 | tf_op jit(solution)/shard_map/ppermute | solution.py:297
  5.7 1.3 %collective-permute-start.2 = (bf16[16,1024]{1,0:T(8,128)(2,1)S(1)}, bf16[16,1024]{1,0:T(8,128)(2,1)S(1)}, u32[]{:S(2)}, u32[]{:S(2)}) collective-permute-start(bf16[16,1024]{1,0:T(8,128)(2,1)S(1)} %dynamic-slice_bitcast_fusion), channel_id=1, source_target_pairs={{1,3},{2,0},{3,5},{4,2},{5,7},{6,4},{7,9},{8,6},{9,11},{10,8},{11,... | collective-permute-start | bytes 98312 | tf_op jit(solution)/shard_map/ppermute | solution.py:294
  7.0 0.7 collective-permute-start.1
  7.7 0.1 pad_add_fusion.place_ref
  7.8 4.1 %collective-permute-done.2.far_ref = bf16[16,1024]{1,0:T(8,128)(2,1)S(1)} collective-permute-done((bf16[16,1024]{1,0:T(8,128)(2,1)S(1)}, bf16[16,1024]{1,0:T(8,128)(2,1)S(1)}, u32[]{:S(2)}, u32[]{:S(2)}) %collective-permute-start.2) | collective-permute-done | bytes 32800 | tf_op jit(solution)/shard_map/ppermute | solution.py:294
  11.9 0.0 collective-permute-done.1.near_ref
  11.9 0.0 collective-permute-done.other_ref
  11.9 8.0 %activation.1.act_ref = bf16[1536,512]{1,0:T(8,128)(2,1)S(1)} custom-call(s32[4]{0:T(128)S(1)} %pad_add_fusion.place_ref, bf16[768,1024]{1,0:T(8,128)(2,1)} %bitcast.18, bf16[768,1024]{1,0:T(8,128)(2,1)S(1)} %collective-permute-done.other_ref, bf16[16,1024]{1,0:T(8,128)(2,1)S(1)} %collective-permute-done.1.near_ref, ...), custom_call_target="tpu_custom_call" | custom-call | tf_op jit(solution)/shard_map/activation/pallas_call | solution.py:127
  19.9 0.0 collective-permute-done.3.other_ref
  19.9 0.0 copy-done
  19.9 2.4 %product_kernel.1 = bf16[4,2,4,16,1024]{4,3,2,1,0:T(8,128)(2,1)S(1)} custom-call(s32[4]{0:T(128)S(1)} %pad_add_fusion.place_ref, bf16[1536,512]{1,0:T(8,128)(2,1)S(1)} %activation.1.act_ref, bf16[768,1024]{1,0:T(8,128)(2,1)S(1)} %bitcast.14, bf16[768,1024]{1,0:T(8,128)(2,1)S(1)} %collective-permute-done.3.other_ref), custom_call_target="tpu_custom_call" | custom-call | tf_op jit(solution)/shard_map/product_kernel/pallas_call | solution.py:265
  22.3 0.0 copy-start.1
  22.3 0.0 copy-start.2
  22.3 44.0 %all_to_all.25.parts_ref = bf16[32,16,1024]{2,1,0:T(8,128)(2,1)S(1)} all-to-all(bf16[32,16,1024]{2,1,0:T(8,128)(2,1)S(1)} %bitcast.12), channel_id=1, replica_groups={{0,2,4,6,9,11,13,15,16,18,20,22,25,27,29,31,32,34,36,38,41,43,45,47,48,..., dimensions={0} | all-to-all | bytes 2097152 | tf_op jit(solution)/shard_map/all_to_all | solution.py:276
  66.3 0.0 copy-done.1
  66.4 0.5 merge_kernel.1
  66.8 18.2 %all_to_all.26.parts_ref = f32[16,24,128]{2,1,0:T(8,128)S(1)} all-to-all(f32[16,24,128]{2,1,0:T(8,128)S(1)} %get-tuple-element.14), channel_id=1, replica_groups=mesh['x'=4,'h'=2,'y'=4,'z'=8,'c'=2] {'x','h','c'}, dimensions={0} | all-to-all | bytes 393216 | tf_op jit(solution)/shard_map/all_to_all | solution.py:276
  85.1 0.9 term_kernel.1
  86.0 10.8 %all_to_all.27.parts_ref = f32[4,72,128]{2,1,0:T(8,128)S(1)} all-to-all(f32[4,72,128]{2,1,0:T(8,128)S(1)} %get-tuple-element.15), channel_id=1, replica_groups=mesh['x'=4,'h'=2,'y'=4,'z'=8,'c'=2] {'y'}, dimensions={0} | all-to-all | bytes 294912 | tf_op jit(solution)/shard_map/all_to_all | solution.py:276
  96.8 15.4 %all_to_all.28.parts_ref = f32[8,72,128]{2,1,0:T(8,128)S(1)} all-to-all(f32[8,72,128]{2,1,0:T(8,128)S(1)} %total_kernel.2), channel_id=1, replica_groups=mesh['x'=4,'h'=2,'y'=4,'z'=8,'c'=2] {'z'}, dimensions={0} | all-to-all | bytes 589824 | tf_op jit(solution)/shard_map/all_to_all | solution.py:276
  112.2 14.2 %all_to_all.29.rows_ref = f32[8,72,128]{2,1,0:T(8,128)S(1)} all-to-all(f32[8,72,128]{2,1,0:T(8,128)S(1)} %total_kernel.3), channel_id=1, replica_groups=mesh['x'=4,'h'=2,'y'=4,'z'=8,'c'=2] {'x','h'}, dimensions={0} | all-to-all | bytes 589824 | tf_op jit(solution)/shard_map/all_to_all | solution.py:276
  126.4 2.7 %finish_kernel.1 = (f32[64,1024]{1,0:T(8,128)}, f32[16,1024]{1,0:T(8,128)}, f32[16,1024]{1,0:T(8,128)}) custom-call(f32[8,72,128]{2,1,0:T(8,128)S(1)} %all_to_all.29.rows_ref, f32[16,64]{1,0:T(8,128)S(1)} %get-tuple-element.16.left_ref, f32[16,1024]{1,0:T(8,128)S(1)} %get-tuple-element.17.merged_ref), custom_call_target="tpu_custom_call" | custom-call | tf_op jit(solution)/shard_map/finish_kernel/pallas_call | solution.py:265
  (4 shorter events, 0.1 us)
Async XLA Ops:
  1.4 10.5 %collective-permute-start = (bf16[768,1024]{1,0:T(8,128)(2,1)}, bf16[768,1024]{1,0:T(8,128)(2,1)S(1)}, u32[]{:S(2)}, u32[]{:S(2)}) collective-permute-start(bf16[768,1024]{1,0:T(8,128)(2,1)} %bitcast.17), channel_id=1, source_target_pairs={{0,1},{1,0},{2,3},{3,2},{4,5},{5,4},{6,7},{7,6},{8,9},{9,8},{10,11... | collective-permute-start | bytes 4718600 | tf_op jit(solution)/shard_map/ppermute | solution.py:295
  3.3 16.6 %collective-permute-start.3 = (bf16[768,1024]{1,0:T(8,128)(2,1)}, bf16[768,1024]{1,0:T(8,128)(2,1)S(1)}, u32[]{:S(2)}, u32[]{:S(2)}) collective-permute-start(bf16[768,1024]{1,0:T(8,128)(2,1)} %bitcast.13), channel_id=1, source_target_pairs={{0,1},{1,0},{2,3},{3,2},{4,5},{5,4},{6,7},{7,6},{8,9},{9,8},{10,11... | collective-permute-start | bytes 4718600 | tf_op jit(solution)/shard_map/ppermute | solution.py:297
  5.7 6.2 %collective-permute-start.2 = (bf16[16,1024]{1,0:T(8,128)(2,1)S(1)}, bf16[16,1024]{1,0:T(8,128)(2,1)S(1)}, u32[]{:S(2)}, u32[]{:S(2)}) collective-permute-start(bf16[16,1024]{1,0:T(8,128)(2,1)S(1)} %dynamic-slice_bitcast_fusion), channel_id=1, source_target_pairs={{1,3},{2,0},{3,5},{4,2},{5,7},{6,4},{7,9},{8,6},{9,11},{10,8},{11,... | collective-permute-start | bytes 98312 | tf_op jit(solution)/shard_map/ppermute | solution.py:294
  7.0 4.9 %collective-permute-start.1 = (bf16[16,1024]{1,0:T(8,128)(2,1)S(1)}, bf16[16,1024]{1,0:T(8,128)(2,1)S(1)}, u32[]{:S(2)}, u32[]{:S(2)}) collective-permute-start(bf16[16,1024]{1,0:T(8,128)(2,1)S(1)} %dynamic-slice_bitcast_fusion), channel_id=1, source_target_pairs={{1,2},{2,1},{3,4},{4,3},{5,6},{6,5},{7,8},{8,7},{9,10},{10,9},{11,... | collective-permute-start | bytes 98312 | tf_op jit(solution)/shard_map/ppermute | solution.py:293
  7.8 12.1 %copy-start = (bf16[1,768,1024]{2,1,0:T(8,128)(2,1)S(1)}, bf16[1,768,1024]{2,1,0:T(8,128)(2,1)}, u32[]{:S(2)}) copy-start(bf16[1,768,1024]{2,1,0:T(8,128)(2,1)} %param.6) | copy-start | bytes 4718596
  22.3 44.0 %copy-start.1 = (f32[1024,64]{0,1:T(8,128)S(1)}, f32[1024,64]{0,1:T(8,128)}, u32[]{:S(2)}) copy-start(f32[1024,64]{0,1:T(8,128)} %param.9) | copy-start | bytes 786436
  22.3 44.0 %copy-start.2 = (f32[1,16,1024]{2,1,0:T(8,128)S(1)}, f32[1,16,1024]{2,1,0:T(8,128)}, u32[]{:S(2)}) copy-start(f32[1,16,1024]{2,1,0:T(8,128)} %param.8) | copy-start | bytes 196612

commit v8 on v7

--- a/solution.py
+++ b/solution.py
@@ -198,12 +198,15 @@
         precision=HIGHEST,
         preferred_element_type=F32,
     )
-    term = dot(left, mean)
-    gram_ref[...] = dot(left, jnp.concatenate([jnp.zeros_like(left), left], axis=1))
+    both = dot(left, jnp.concatenate([mean, jnp.zeros_like(left), left], axis=1))
+    term = both[:, :LANES]
+    gram_ref[...] = both[:, LANES:]
     gram = gram_ref[pl.ds(pl.multiple_of(TILE * place_ref[2], TILE), TILE)]
+    gram_ref[...] = term
+    term = gram_ref[pl.ds(pl.multiple_of(rank // 2 * place_ref[3], rank // 2), rank // 2)]
     for index in range(term_ref.shape[0]):
-        term_ref[index, :rank] = term
-        term_ref[index, rank:] = gram
+        term_ref[index, : rank // 2] = term
+        term_ref[index, rank // 2 :] = gram
 
 
 def total_kernel(parts_ref, total_ref):
@@ -243,9 +246,12 @@
 def finish_kernel(replicas, rows_ref, left_ref, merged_ref, right_ref, estimate_ref, error_ref, wide_ref):
     rank = left_ref.shape[1]
     features = merged_ref.shape[1]
-    for index in range(rows_ref.shape[0]):
-        wide_ref[:, LANES * index : LANES * (index + 1)] = rows_ref[index, :rank]
-        wide_ref[TILE * index : TILE * (index + 1), features:] = rows_ref[index, rank:]
+    half = rank // 2
+    for index in range(rows_ref.shape[1]):
+        cols = slice(LANES * index, LANES * (index + 1))
+        wide_ref[:half, cols] = rows_ref[0, index, :half]
+        wide_ref[half:, cols] = rows_ref[1, index, :half]
+        wide_ref[TILE * index : TILE * (index + 1), features:] = rows_ref[0, index, half:]
     row = lax.broadcasted_iota(jnp.int32, (rank, 2 * rank), 0)
     lane = lax.broadcasted_iota(jnp.int32, (rank, 2 * rank), 1)
     work = eliminate(wide_ref[:, features:] + (row == lane).astype(F32), rank)
@@ -323,7 +329,7 @@
         carried_error[0],
         right_init.T,
     )
-    size = (rank + TILE, LANES)
+    size = (rank // 2 + TILE, LANES)
     left, term = call(
         term_kernel,
         [(owned, rank), pltpu.VMEM((lax.axis_size("y"), *size), F32)],
@@ -337,7 +343,7 @@
     right, estimate, error = call(
         functools.partial(finish_kernel, replicas),
         [(rank, features), row, row],
-        exchange(total, DP),
+        lax.all_gather(exchange(total, DP), "c"),
         left,
         merged,
         scratch=[pltpu.VMEM((rank, features + 2 * rank), F32)],

time: 130 us -> 130 us (level)
  the two profiles are of different devices: /device:TPU:2 before, /device:TPU:1 now
where the time goes in v8:
time: 130 us; the launch traced here: 129 us
  blocking collectives  94.8 us (73%)
  starting transfers between devices  16.6 us (13%)
  Pallas kernels  14.5 us (11%)
  waiting for transfers between devices  1.48 us (1%)
    all_to_all x5, blocking collectives, exchange(): lax.all_to_all(block, axes, 0, 0, tiled=True, axis_index_groups=groups)  88.5 us
    ppermute x1, starting transfers between devices, local(): other = lax.ppermute(block, 'c', swap)  8.78 us
    pallas_call x1, Pallas kernels, activation(): pl.pallas_call(conv_kernel, in_specs=[smem, hbm, vmem, vmem, vmem, hbm],...  7.99 us
    pallas_call x6, Pallas kernels, call(): pl.pallas_call(kernel, in_specs=[pl.BlockSpec(memory_space=space) for spa...  6.5 us
    all_gather x1, blocking collectives, local(): lax.all_gather(exchange(total, DP), 'c')  6.36 us
    ppermute x1, starting transfers between devices, local(): near = lax.ppermute(ends, CTX, one)  4.65 us
  transfers between devices with their start and end apart: 4, of which 1 were waited for; matrix products, arithmetic and copies ran while one was open for 0% of the time, Pallas kernels for 6%

profile of v8, /device:TPU:1, one launch (start us, length us, event | category | flops | bytes accessed | tf_op | source)
XLA Modules:
  0.0 129.1 jit_solution(674697895967924205)
XLA Ops:
  0.6 0.8 dynamic-slice_bitcast_fusion
  1.4 8.8 %collective-permute-start = (bf16[768,1024]{1,0:T(8,128)(2,1)}, bf16[768,1024]{1,0:T(8,128)(2,1)S(1)}, u32[]{:S(2)}, u32[]{:S(2)}) collective-permute-start(bf16[768,1024]{1,0:T(8,128)(2,1)} %bitcast.19), channel_id=1, source_target_pairs={{0,1},{1,0},{2,3},{3,2},{4,5},{5,4},{6,7},{7,6},{8,9},{9,8},{10,11... | collective-permute-start | bytes 4718600 | tf_op jit(solution)/shard_map/ppermute | solution.py:301
  10.2 1.9 %collective-permute-start.3 = (bf16[768,1024]{1,0:T(8,128)(2,1)}, bf16[768,1024]{1,0:T(8,128)(2,1)S(1)}, u32[]{:S(2)}, u32[]{:S(2)}) collective-permute-start(bf16[768,1024]{1,0:T(8,128)(2,1)} %bitcast.14), channel_id=1, source_target_pairs={{0,1},{1,0},{2,3},{3,2},{4,5},{5,4},{6,7},{7,6},{8,9},{9,8},{10,11... | collective-permute-start | bytes 4718600 | tf_op jit(solution)/shard_map/ppermute | solution.py:303
  12.1 1.3 %collective-permute-start.2 = (bf16[16,1024]{1,0:T(8,128)(2,1)S(1)}, bf16[16,1024]{1,0:T(8,128)(2,1)S(1)}, u32[]{:S(2)}, u32[]{:S(2)}) collective-permute-start(bf16[16,1024]{1,0:T(8,128)(2,1)S(1)} %dynamic-slice_bitcast_fusion), channel_id=1, source_target_pairs={{1,3},{2,0},{3,5},{4,2},{5,7},{6,4},{7,9},{8,6},{9,11},{10,8},{11,... | collective-permute-start | bytes 98312 | tf_op jit(solution)/shard_map/ppermute | solution.py:300
  13.4 4.7 %collective-permute-start.1 = (bf16[16,1024]{1,0:T(8,128)(2,1)S(1)}, bf16[16,1024]{1,0:T(8,128)(2,1)S(1)}, u32[]{:S(2)}, u32[]{:S(2)}) collective-permute-start(bf16[16,1024]{1,0:T(8,128)(2,1)S(1)} %dynamic-slice_bitcast_fusion), channel_id=1, source_target_pairs={{1,2},{2,1},{3,4},{4,3},{5,6},{6,5},{7,8},{8,7},{9,10},{10,9},{11,... | collective-permute-start | bytes 98312 | tf_op jit(solution)/shard_map/ppermute | solution.py:299
  18.1 0.1 pad_add_fusion.place_ref
  18.2 0.0 collective-permute-done.2.far_ref
  18.2 1.5 %collective-permute-done.1.near_ref = bf16[16,1024]{1,0:T(8,128)(2,1)S(1)} collective-permute-done((bf16[16,1024]{1,0:T(8,128)(2,1)S(1)}, bf16[16,1024]{1,0:T(8,128)(2,1)S(1)}, u32[]{:S(2)}, u32[]{:S(2)}) %collective-permute-start.1) | collective-permute-done | bytes 32800 | tf_op jit(solution)/shard_map/ppermute | solution.py:299
  19.7 0.0 collective-permute-done.other_ref
  19.7 8.0 %activation.1.act_ref = bf16[1536,512]{1,0:T(8,128)(2,1)S(1)} custom-call(s32[4]{0:T(128)S(1)} %pad_add_fusion.place_ref, bf16[768,1024]{1,0:T(8,128)(2,1)} %bitcast.20, bf16[768,1024]{1,0:T(8,128)(2,1)S(1)} %collective-permute-done.other_ref, bf16[16,1024]{1,0:T(8,128)(2,1)S(1)} %collective-permute-done.1.near_ref, ...), custom_call_target="tpu_custom_call" | custom-call | tf_op jit(solution)/shard_map/activation/pallas_call | solution.py:127
  27.7 0.0 collective-permute-done.3.other_ref
  27.7 0.0 copy-done
  27.7 2.4 %product_kernel.1 = bf16[4,2,4,16,1024]{4,3,2,1,0:T(8,128)(2,1)S(1)} custom-call(s32[4]{0:T(128)S(1)} %pad_add_fusion.place_ref, bf16[1536,512]{1,0:T(8,128)(2,1)S(1)} %activation.1.act_ref, bf16[768,1024]{1,0:T(8,128)(2,1)S(1)} %bitcast.15, bf16[768,1024]{1,0:T(8,128)(2,1)S(1)} %collective-permute-done.3.other_ref), custom_call_target="tpu_custom_call" | custom-call | tf_op jit(solution)/shard_map/product_kernel/pallas_call | solution.py:271
  30.1 0.0 copy-start.1
  30.1 0.0 copy-start.2
  30.1 36.8 %all_to_all.25.parts_ref = bf16[32,16,1024]{2,1,0:T(8,128)(2,1)S(1)} all-to-all(bf16[32,16,1024]{2,1,0:T(8,128)(2,1)S(1)} %bitcast.13), channel_id=1, replica_groups={{0,2,4,6,9,11,13,15,16,18,20,22,25,27,29,31,32,34,36,38,41,43,45,47,48,..., dimensions={0} | all-to-all | bytes 2097152 | tf_op jit(solution)/shard_map/all_to_all | solution.py:282
  66.9 0.5 merge_kernel.1
  67.4 18.5 %all_to_all.26.parts_ref = f32[16,24,128]{2,1,0:T(8,128)S(1)} all-to-all(f32[16,24,128]{2,1,0:T(8,128)S(1)} %get-tuple-element.14), channel_id=1, replica_groups=mesh['x'=4,'h'=2,'y'=4,'z'=8,'c'=2] {'x','h','c'}, dimensions={0} | all-to-all | bytes 393216 | tf_op jit(solution)/shard_map/all_to_all | solution.py:282
  85.9 0.9 term_kernel.1
  86.8 10.1 %all_to_all.27.parts_ref = f32[4,40,128]{2,1,0:T(8,128)S(1)} all-to-all(f32[4,40,128]{2,1,0:T(8,128)S(1)} %get-tuple-element.15), channel_id=1, replica_groups=mesh['x'=4,'h'=2,'y'=4,'z'=8,'c'=2] {'y'}, dimensions={0} | all-to-all | bytes 163840 | tf_op jit(solution)/shard_map/all_to_all | solution.py:282
  97.0 11.0 %all_to_all.28.parts_ref = f32[8,40,128]{2,1,0:T(8,128)S(1)} all-to-all(f32[8,40,128]{2,1,0:T(8,128)S(1)} %total_kernel.2), channel_id=1, replica_groups=mesh['x'=4,'h'=2,'y'=4,'z'=8,'c'=2] {'z'}, dimensions={0} | all-to-all | bytes 327680 | tf_op jit(solution)/shard_map/all_to_all | solution.py:282
  108.0 12.0 %all_to_all.29 = f32[8,40,128]{2,1,0:T(8,128)S(1)} all-to-all(f32[8,40,128]{2,1,0:T(8,128)S(1)} %total_kernel.3), channel_id=1, replica_groups=mesh['x'=4,'h'=2,'y'=4,'z'=8,'c'=2] {'x','h'}, dimensions={0} | all-to-all | bytes 327680 | tf_op jit(solution)/shard_map/all_to_all | solution.py:282
  120.0 6.4 %all-gather = f32[16,40,128]{2,1,0:T(8,128)S(1)} all-gather(f32[8,40,128]{2,1,0:T(8,128)S(1)} %all_to_all.29), channel_id=2, replica_groups=mesh['x'=4,'h'=2,'y'=4,'z'=8,'c'=2] {'c'}, dimensions={0}, use_global_device_ids=true | all-gather | bytes 491520 | tf_op jit(solution)/shard_map/all_gather | solution.py:346
  126.3 2.7 %finish_kernel.1 = (f32[64,1024]{1,0:T(8,128)}, f32[16,1024]{1,0:T(8,128)}, f32[16,1024]{1,0:T(8,128)}) custom-call(f32[2,8,40,128]{3,2,1,0:T(8,128)S(1)} %bitcast.16, f32[16,64]{1,0:T(8,128)S(1)} %get-tuple-element.16.left_ref, f32[16,1024]{1,0:T(8,128)S(1)} %get-tuple-element.17.merged_ref), custom_call_target="tpu_custom_call" | custom-call | tf_op jit(solution)/shard_map/finish_kernel/pallas_call | solution.py:271
  (5 shorter events, 0.0 us)
Async XLA Ops:
  1.4 18.3 %collective-permute-start = (bf16[768,1024]{1,0:T(8,128)(2,1)}, bf16[768,1024]{1,0:T(8,128)(2,1)S(1)}, u32[]{:S(2)}, u32[]{:S(2)}) collective-permute-start(bf16[768,1024]{1,0:T(8,128)(2,1)} %bitcast.19), channel_id=1, source_target_pairs={{0,1},{1,0},{2,3},{3,2},{4,5},{5,4},{6,7},{7,6},{8,9},{9,8},{10,11... | collective-permute-start | bytes 4718600 | tf_op jit(solution)/shard_map/ppermute | solution.py:301
  10.2 17.5 %collective-permute-start.3 = (bf16[768,1024]{1,0:T(8,128)(2,1)}, bf16[768,1024]{1,0:T(8,128)(2,1)S(1)}, u32[]{:S(2)}, u32[]{:S(2)}) collective-permute-start(bf16[768,1024]{1,0:T(8,128)(2,1)} %bitcast.14), channel_id=1, source_target_pairs={{0,1},{1,0},{2,3},{3,2},{4,5},{5,4},{6,7},{7,6},{8,9},{9,8},{10,11... | collective-permute-start | bytes 4718600 | tf_op jit(solution)/shard_map/ppermute | solution.py:303
  12.1 6.1 %collective-permute-start.2 = (bf16[16,1024]{1,0:T(8,128)(2,1)S(1)}, bf16[16,1024]{1,0:T(8,128)(2,1)S(1)}, u32[]{:S(2)}, u32[]{:S(2)}) collective-permute-start(bf16[16,1024]{1,0:T(8,128)(2,1)S(1)} %dynamic-slice_bitcast_fusion), channel_id=1, source_target_pairs={{1,3},{2,0},{3,5},{4,2},{5,7},{6,4},{7,9},{8,6},{9,11},{10,8},{11,... | collective-permute-start | bytes 98312 | tf_op jit(solution)/shard_map/ppermute | solution.py:300
  13.4 6.2 %collective-permute-start.1 = (bf16[16,1024]{1,0:T(8,128)(2,1)S(1)}, bf16[16,1024]{1,0:T(8,128)(2,1)S(1)}, u32[]{:S(2)}, u32[]{:S(2)}) collective-permute-start(bf16[16,1024]{1,0:T(8,128)(2,1)S(1)} %dynamic-slice_bitcast_fusion), channel_id=1, source_target_pairs={{1,2},{2,1},{3,4},{4,3},{5,6},{6,5},{7,8},{8,7},{9,10},{10,9},{11,... | collective-permute-start | bytes 98312 | tf_op jit(solution)/shard_map/ppermute | solution.py:299
  18.2 9.5 %copy-start = (bf16[1,768,1024]{2,1,0:T(8,128)(2,1)S(1)}, bf16[1,768,1024]{2,1,0:T(8,128)(2,1)}, u32[]{:S(2)}) copy-start(bf16[1,768,1024]{2,1,0:T(8,128)(2,1)} %param.6) | copy-start | bytes 4718596
  30.1 36.8 %copy-start.1 = (f32[1024,64]{0,1:T(8,128)S(1)}, f32[1024,64]{0,1:T(8,128)}, u32[]{:S(2)}) copy-start(f32[1024,64]{0,1:T(8,128)} %param.9) | copy-start | bytes 786436
  30.1 36.8 %copy-start.2 = (f32[1,16,1024]{2,1,0:T(8,128)S(1)}, f32[1,16,1024]{2,1,0:T(8,128)}, u32[]{:S(2)}) copy-start(f32[1,16,1024]{2,1,0:T(8,128)} %param.8) | copy-start | bytes 196612

commit v9 on v8

--- a/solution.py
+++ b/solution.py
@@ -247,11 +247,11 @@
     rank = left_ref.shape[1]
     features = merged_ref.shape[1]
     half = rank // 2
-    for index in range(rows_ref.shape[1]):
+    for index in range(rows_ref.shape[0] // 2):
         cols = slice(LANES * index, LANES * (index + 1))
-        wide_ref[:half, cols] = rows_ref[0, index, :half]
-        wide_ref[half:, cols] = rows_ref[1, index, :half]
-        wide_ref[TILE * index : TILE * (index + 1), features:] = rows_ref[0, index, half:]
+        wide_ref[:half, cols] = rows_ref[2 * index, :half]
+        wide_ref[half:, cols] = rows_ref[2 * index + 1, :half]
+        wide_ref[TILE * index : TILE * (index + 1), features:] = rows_ref[2 * index, half:]
     row = lax.broadcasted_iota(jnp.int32, (rank, 2 * rank), 0)
     lane = lax.broadcasted_iota(jnp.int32, (rank, 2 * rank), 1)
     work = eliminate(wide_ref[:, features:] + (row == lane).astype(F32), rank)
@@ -339,11 +339,11 @@
         scratch=[pltpu.VMEM((spread // replicas, owned, rank), F32), pltpu.VMEM((rank, LANES), F32)],
     )
     (total,) = call(total_kernel, [pltpu.VMEM((lax.axis_size("z"), *size), F32)], exchange(term, "y"))
-    (total,) = call(total_kernel, [pltpu.VMEM((replicas, *size), F32)], exchange(total, "z"))
+    (total,) = call(total_kernel, [pltpu.VMEM((spread, *size), F32)], exchange(total, "z"))
     right, estimate, error = call(
         functools.partial(finish_kernel, replicas),
         [(rank, features), row, row],
-        lax.all_gather(exchange(total, DP), "c"),
+        exchange(total, SPREAD),
         left,
         merged,
         scratch=[pltpu.VMEM((rank, features + 2 * rank), F32)],

time: 130 us -> 132 us (1.015)
  the two profiles are of different devices: /device:TPU:1 before, /device:TPU:9 now
where the time goes in v9:
time: 132 us; the launch traced here: 131 us
  blocking collectives  98.7 us (75%)
  Pallas kernels  14.5 us (11%)
  starting transfers between devices  10.8 us (8%)
  waiting for transfers between devices  5.43 us (4%)
    all_to_all x5, blocking collectives, exchange(): lax.all_to_all(block, axes, 0, 0, tiled=True, axis_index_groups=groups)  98.7 us
    pallas_call x1, Pallas kernels, activation(): pl.pallas_call(conv_kernel, in_specs=[smem, hbm, vmem, vmem, vmem, hbm],...  7.99 us
    pallas_call x6, Pallas kernels, call(): pl.pallas_call(kernel, in_specs=[pl.BlockSpec(memory_space=space) for spa...  6.49 us
    ppermute x1, waiting for transfers between devices, local(): far = lax.ppermute(ends, CTX, two)  5.42 us
    ppermute x1, starting transfers between devices, local(): far = lax.ppermute(ends, CTX, two)  4 us
  transfers between devices with their start and end apart: 4, of which 1 were waited for; matrix products, arithmetic and copies ran while one was open for 0% of the time, Pallas kernels for 6%

profile of v9, /device:TPU:9, one launch (start us, length us, event | category | flops | bytes accessed | tf_op | source)
XLA Modules:
  0.0 131.1 jit_solution(7917010477724680345)
XLA Ops:
  0.6 0.8 dynamic-slice_bitcast_fusion
  1.4 2.6 %collective-permute-start = (bf16[768,1024]{1,0:T(8,128)(2,1)}, bf16[768,1024]{1,0:T(8,128)(2,1)S(1)}, u32[]{:S(2)}, u32[]{:S(2)}) collective-permute-start(bf16[768,1024]{1,0:T(8,128)(2,1)} %bitcast.17), channel_id=1, source_target_pairs={{0,1},{1,0},{2,3},{3,2},{4,5},{5,4},{6,7},{7,6},{8,9},{9,8},{10,11... | collective-permute-start | bytes 4718600 | tf_op jit(solution)/shard_map/ppermute | solution.py:301
  4.0 1.9 %collective-permute-start.3 = (bf16[768,1024]{1,0:T(8,128)(2,1)}, bf16[768,1024]{1,0:T(8,128)(2,1)S(1)}, u32[]{:S(2)}, u32[]{:S(2)}) collective-permute-start(bf16[768,1024]{1,0:T(8,128)(2,1)} %bitcast.13), channel_id=1, source_target_pairs={{0,1},{1,0},{2,3},{3,2},{4,5},{5,4},{6,7},{7,6},{8,9},{9,8},{10,11... | collective-permute-start | bytes 4718600 | tf_op jit(solution)/shard_map/ppermute | solution.py:303
  5.9 4.0 %collective-permute-start.2 = (bf16[16,1024]{1,0:T(8,128)(2,1)S(1)}, bf16[16,1024]{1,0:T(8,128)(2,1)S(1)}, u32[]{:S(2)}, u32[]{:S(2)}) collective-permute-start(bf16[16,1024]{1,0:T(8,128)(2,1)S(1)} %dynamic-slice_bitcast_fusion), channel_id=1, source_target_pairs={{1,3},{2,0},{3,5},{4,2},{5,7},{6,4},{7,9},{8,6},{9,11},{10,8},{11,... | collective-permute-start | bytes 98312 | tf_op jit(solution)/shard_map/ppermute | solution.py:300
  9.9 2.3 %collective-permute-start.1 = (bf16[16,1024]{1,0:T(8,128)(2,1)S(1)}, bf16[16,1024]{1,0:T(8,128)(2,1)S(1)}, u32[]{:S(2)}, u32[]{:S(2)}) collective-permute-start(bf16[16,1024]{1,0:T(8,128)(2,1)S(1)} %dynamic-slice_bitcast_fusion), channel_id=1, source_target_pairs={{1,2},{2,1},{3,4},{4,3},{5,6},{6,5},{7,8},{8,7},{9,10},{10,9},{11,... | collective-permute-start | bytes 98312 | tf_op jit(solution)/shard_map/ppermute | solution.py:299
  12.3 0.1 pad_add_fusion.place_ref
  12.3 5.4 %collective-permute-done.2.far_ref = bf16[16,1024]{1,0:T(8,128)(2,1)S(1)} collective-permute-done((bf16[16,1024]{1,0:T(8,128)(2,1)S(1)}, bf16[16,1024]{1,0:T(8,128)(2,1)S(1)}, u32[]{:S(2)}, u32[]{:S(2)}) %collective-permute-start.2) | collective-permute-done | bytes 32800 | tf_op jit(solution)/shard_map/ppermute | solution.py:300
  17.8 0.0 collective-permute-done.1.near_ref
  17.8 0.0 collective-permute-done.other_ref
  17.8 8.0 %activation.1.act_ref = bf16[1536,512]{1,0:T(8,128)(2,1)S(1)} custom-call(s32[4]{0:T(128)S(1)} %pad_add_fusion.place_ref, bf16[768,1024]{1,0:T(8,128)(2,1)} %bitcast.18, bf16[768,1024]{1,0:T(8,128)(2,1)S(1)} %collective-permute-done.other_ref, bf16[16,1024]{1,0:T(8,128)(2,1)S(1)} %collective-permute-done.1.near_ref, ...), custom_call_target="tpu_custom_call" | custom-call | tf_op jit(solution)/shard_map/activation/pallas_call | solution.py:127
  25.8 0.0 collective-permute-done.3.other_ref
  25.8 0.0 copy-done
  25.8 2.4 %product_kernel.1 = bf16[4,2,4,16,1024]{4,3,2,1,0:T(8,128)(2,1)S(1)} custom-call(s32[4]{0:T(128)S(1)} %pad_add_fusion.place_ref, bf16[1536,512]{1,0:T(8,128)(2,1)S(1)} %activation.1.act_ref, bf16[768,1024]{1,0:T(8,128)(2,1)S(1)} %bitcast.14, bf16[768,1024]{1,0:T(8,128)(2,1)S(1)} %collective-permute-done.3.other_ref), custom_call_target="tpu_custom_call" | custom-call | tf_op jit(solution)/shard_map/product_kernel/pallas_call | solution.py:271
  28.2 0.0 copy-start.1
  28.2 0.0 copy-start.2
  28.2 35.8 %all_to_all.25.parts_ref = bf16[32,16,1024]{2,1,0:T(8,128)(2,1)S(1)} all-to-all(bf16[32,16,1024]{2,1,0:T(8,128)(2,1)S(1)} %bitcast.12), channel_id=1, replica_groups={{0,2,4,6,9,11,13,15,16,18,20,22,25,27,29,31,32,34,36,38,41,43,45,47,48,..., dimensions={0} | all-to-all | bytes 2097152 | tf_op jit(solution)/shard_map/all_to_all | solution.py:282
  64.0 0.0 copy-done.1
  64.0 0.5 merge_kernel.1
  64.5 21.2 %all_to_all.26.parts_ref = f32[16,24,128]{2,1,0:T(8,128)S(1)} all-to-all(f32[16,24,128]{2,1,0:T(8,128)S(1)} %get-tuple-element.14), channel_id=1, replica_groups=mesh['x'=4,'h'=2,'y'=4,'z'=8,'c'=2] {'x','h','c'}, dimensions={0} | all-to-all | bytes 393216 | tf_op jit(solution)/shard_map/all_to_all | solution.py:282
  85.8 0.9 term_kernel.1
  86.6 9.0 %all_to_all.27.parts_ref = f32[4,40,128]{2,1,0:T(8,128)S(1)} all-to-all(f32[4,40,128]{2,1,0:T(8,128)S(1)} %get-tuple-element.15), channel_id=1, replica_groups=mesh['x'=4,'h'=2,'y'=4,'z'=8,'c'=2] {'y'}, dimensions={0} | all-to-all | bytes 163840 | tf_op jit(solution)/shard_map/all_to_all | solution.py:282
  95.7 10.9 %all_to_all.28.parts_ref = f32[8,40,128]{2,1,0:T(8,128)S(1)} all-to-all(f32[8,40,128]{2,1,0:T(8,128)S(1)} %total_kernel.2), channel_id=1, replica_groups=mesh['x'=4,'h'=2,'y'=4,'z'=8,'c'=2] {'z'}, dimensions={0} | all-to-all | bytes 327680 | tf_op jit(solution)/shard_map/all_to_all | solution.py:282
  106.6 21.8 %all_to_all.29.rows_ref = f32[16,40,128]{2,1,0:T(8,128)S(1)} all-to-all(f32[16,40,128]{2,1,0:T(8,128)S(1)} %total_kernel.3), channel_id=1, replica_groups=mesh['x'=4,'h'=2,'y'=4,'z'=8,'c'=2] {'x','h','c'}, dimensions={0} | all-to-all | bytes 655360 | tf_op jit(solution)/shard_map/all_to_all | solution.py:282
  128.4 2.7 %finish_kernel.1 = (f32[64,1024]{1,0:T(8,128)}, f32[16,1024]{1,0:T(8,128)}, f32[16,1024]{1,0:T(8,128)}) custom-call(f32[16,40,128]{2,1,0:T(8,128)S(1)} %all_to_all.29.rows_ref, f32[16,64]{1,0:T(8,128)S(1)} %get-tuple-element.16.left_ref, f32[16,1024]{1,0:T(8,128)S(1)} %get-tuple-element.17.merged_ref), custom_call_target="tpu_custom_call" | custom-call | tf_op jit(solution)/shard_map/finish_kernel/pallas_call | solution.py:271
  (4 shorter events, 0.0 us)
Async XLA Ops:
  1.4 16.4 %collective-permute-start = (bf16[768,1024]{1,0:T(8,128)(2,1)}, bf16[768,1024]{1,0:T(8,128)(2,1)S(1)}, u32[]{:S(2)}, u32[]{:S(2)}) collective-permute-start(bf16[768,1024]{1,0:T(8,128)(2,1)} %bitcast.17), channel_id=1, source_target_pairs={{0,1},{1,0},{2,3},{3,2},{4,5},{5,4},{6,7},{7,6},{8,9},{9,8},{10,11... | collective-permute-start | bytes 4718600 | tf_op jit(solution)/shard_map/ppermute | solution.py:301
  4.0 21.8 %collective-permute-start.3 = (bf16[768,1024]{1,0:T(8,128)(2,1)}, bf16[768,1024]{1,0:T(8,128)(2,1)S(1)}, u32[]{:S(2)}, u32[]{:S(2)}) collective-permute-start(bf16[768,1024]{1,0:T(8,128)(2,1)} %bitcast.13), channel_id=1, source_target_pairs={{0,1},{1,0},{2,3},{3,2},{4,5},{5,4},{6,7},{7,6},{8,9},{9,8},{10,11... | collective-permute-start | bytes 4718600 | tf_op jit(solution)/shard_map/ppermute | solution.py:303
  5.9 11.9 %collective-permute-start.2 = (bf16[16,1024]{1,0:T(8,128)(2,1)S(1)}, bf16[16,1024]{1,0:T(8,128)(2,1)S(1)}, u32[]{:S(2)}, u32[]{:S(2)}) collective-permute-start(bf16[16,1024]{1,0:T(8,128)(2,1)S(1)} %dynamic-slice_bitcast_fusion), channel_id=1, source_target_pairs={{1,3},{2,0},{3,5},{4,2},{5,7},{6,4},{7,9},{8,6},{9,11},{10,8},{11,... | collective-permute-start | bytes 98312 | tf_op jit(solution)/shard_map/ppermute | solution.py:300
  9.9 7.8 %collective-permute-start.1 = (bf16[16,1024]{1,0:T(8,128)(2,1)S(1)}, bf16[16,1024]{1,0:T(8,128)(2,1)S(1)}, u32[]{:S(2)}, u32[]{:S(2)}) collective-permute-start(bf16[16,1024]{1,0:T(8,128)(2,1)S(1)} %dynamic-slice_bitcast_fusion), channel_id=1, source_target_pairs={{1,2},{2,1},{3,4},{4,3},{5,6},{6,5},{7,8},{8,7},{9,10},{10,9},{11,... | collective-permute-start | bytes 98312 | tf_op jit(solution)/shard_map/ppermute | solution.py:299
  12.3 13.4 %copy-start = (bf16[1,768,1024]{2,1,0:T(8,128)(2,1)S(1)}, bf16[1,768,1024]{2,1,0:T(8,128)(2,1)}, u32[]{:S(2)}) copy-start(bf16[1,768,1024]{2,1,0:T(8,128)(2,1)} %param.6) | copy-start | bytes 4718596
  28.2 35.9 %copy-start.1 = (f32[1024,64]{0,1:T(8,128)S(1)}, f32[1024,64]{0,1:T(8,128)}, u32[]{:S(2)}) copy-start(f32[1024,64]{0,1:T(8,128)} %param.9) | copy-start | bytes 786436
  28.2 35.8 %copy-start.2 = (f32[1,16,1024]{2,1,0:T(8,128)S(1)}, f32[1,16,1024]{2,1,0:T(8,128)}, u32[]{:S(2)}) copy-start(f32[1,16,1024]{2,1,0:T(8,128)} %param.8) | copy-start | bytes 196612

commit v10 on v9

--- a/solution.py
+++ b/solution.py
@@ -207,6 +207,14 @@
     for index in range(term_ref.shape[0]):
         term_ref[index, : rank // 2] = term
         term_ref[index, rank // 2 :] = gram
+
+
+def join_kernel(halves_ref, total_ref):
+    half = halves_ref.shape[1] - TILE
+    for index in range(total_ref.shape[0]):
+        total_ref[index, :half] = halves_ref[0, :half]
+        total_ref[index, half : 2 * half] = halves_ref[1, :half]
+        total_ref[index, 2 * half :] = halves_ref[0, half:]
 
 
 def total_kernel(parts_ref, total_ref):
@@ -246,12 +254,9 @@
 def finish_kernel(replicas, rows_ref, left_ref, merged_ref, right_ref, estimate_ref, error_ref, wide_ref):
     rank = left_ref.shape[1]
     features = merged_ref.shape[1]
-    half = rank // 2
-    for index in range(rows_ref.shape[0] // 2):
-        cols = slice(LANES * index, LANES * (index + 1))
-        wide_ref[:half, cols] = rows_ref[2 * index, :half]
-        wide_ref[half:, cols] = rows_ref[2 * index + 1, :half]
-        wide_ref[TILE * index : TILE * (index + 1), features:] = rows_ref[2 * index, half:]
+    for index in range(rows_ref.shape[0]):
+        wide_ref[:, LANES * index : LANES * (index + 1)] = rows_ref[index, :rank]
+        wide_ref[TILE * index : TILE * (index + 1), features:] = rows_ref[index, rank:]
     row = lax.broadcasted_iota(jnp.int32, (rank, 2 * rank), 0)
     lane = lax.broadcasted_iota(jnp.int32, (rank, 2 * rank), 1)
     work = eliminate(wide_ref[:, features:] + (row == lane).astype(F32), rank)
@@ -339,11 +344,13 @@
         scratch=[pltpu.VMEM((spread // replicas, owned, rank), F32), pltpu.VMEM((rank, LANES), F32)],
     )
     (total,) = call(total_kernel, [pltpu.VMEM((lax.axis_size("z"), *size), F32)], exchange(term, "y"))
-    (total,) = call(total_kernel, [pltpu.VMEM((spread, *size), F32)], exchange(total, "z"))
+    (total,) = call(total_kernel, [(1, *size)], exchange(total, "z"))
+    full = pltpu.VMEM((replicas, rank + TILE, LANES), F32)
+    (total,) = call(join_kernel, [full], lax.all_gather(total[0], "c"))
     right, estimate, error = call(
         functools.partial(finish_kernel, replicas),
         [(rank, features), row, row],
-        exchange(total, SPREAD),
+        exchange(total, DP),
         left,
         merged,
         scratch=[pltpu.VMEM((rank, features + 2 * rank), F32)],

time: 132 us -> 132 us (level)
    all_gather x0 -> x1, blocking collectives: none -> 5.04 us  [local(): total, = call(join_kernel, [full], lax.all_gather(total[0], 'c'))]
    all_to_all x5, blocking collectives: 98.7 us -> 94.4 us  [exchange(): lax.all_to_all(block, axes, 0, 0, tiled=True, axis_index_groups=groups)]
    pallas_call x6 -> x7, Pallas kernels: 6.49 us -> 6.5 us  [call(): pl.pallas_call(kernel, in_specs=[pl.BlockSpec(memory_space=space) for spa...]
where the time goes in v10:
time: 132 us
  blocking collectives  99.5 us (75%)
  Pallas kernels  14.5 us (11%)
  starting transfers between devices  10.8 us (8%)
  waiting for transfers between devices  5.43 us (4%)
    all_to_all x5, blocking collectives, exchange(): lax.all_to_all(block, axes, 0, 0, tiled=True, axis_index_groups=groups)  94.4 us
    pallas_call x1, Pallas kernels, activation(): pl.pallas_call(conv_kernel, in_specs=[smem, hbm, vmem, vmem, vmem, hbm],...  7.99 us
    pallas_call x7, Pallas kernels, call(): pl.pallas_call(kernel, in_specs=[pl.BlockSpec(memory_space=space) for spa...  6.5 us
    ppermute x1, waiting for transfers between devices, local(): far = lax.ppermute(ends, CTX, two)  5.42 us
    all_gather x1, blocking collectives, local(): total, = call(join_kernel, [full], lax.all_gather(total[0], 'c'))  5.04 us
    ppermute x1, starting transfers between devices, local(): far = lax.ppermute(ends, CTX, two)  4 us
  transfers between devices with their start and end apart: 4, of which 1 were waited for; matrix products, arithmetic and copies ran while one was open for 0% of the time, Pallas kernels for 6%

profile of v10, /device:TPU:9, one launch (start us, length us, event | category | flops | bytes accessed | tf_op | source)
XLA Modules:
  0.0 131.8 jit_solution(5861046293007128301)
XLA Ops:
  0.6 0.8 dynamic-slice_bitcast_fusion
  1.4 2.6 %collective-permute-start = (bf16[768,1024]{1,0:T(8,128)(2,1)}, bf16[768,1024]{1,0:T(8,128)(2,1)S(1)}, u32[]{:S(2)}, u32[]{:S(2)}) collective-permute-start(bf16[768,1024]{1,0:T(8,128)(2,1)} %bitcast.17), channel_id=1, source_target_pairs={{0,1},{1,0},{2,3},{3,2},{4,5},{5,4},{6,7},{7,6},{8,9},{9,8},{10,11... | collective-permute-start | bytes 4718600 | tf_op jit(solution)/shard_map/ppermute | solution.py:306
  4.0 1.9 %collective-permute-start.3 = (bf16[768,1024]{1,0:T(8,128)(2,1)}, bf16[768,1024]{1,0:T(8,128)(2,1)S(1)}, u32[]{:S(2)}, u32[]{:S(2)}) collective-permute-start(bf16[768,1024]{1,0:T(8,128)(2,1)} %bitcast.13), channel_id=1, source_target_pairs={{0,1},{1,0},{2,3},{3,2},{4,5},{5,4},{6,7},{7,6},{8,9},{9,8},{10,11... | collective-permute-start | bytes 4718600 | tf_op jit(solution)/shard_map/ppermute | solution.py:308
  5.9 4.0 %collective-permute-start.2 = (bf16[16,1024]{1,0:T(8,128)(2,1)S(1)}, bf16[16,1024]{1,0:T(8,128)(2,1)S(1)}, u32[]{:S(2)}, u32[]{:S(2)}) collective-permute-start(bf16[16,1024]{1,0:T(8,128)(2,1)S(1)} %dynamic-slice_bitcast_fusion), channel_id=1, source_target_pairs={{1,3},{2,0},{3,5},{4,2},{5,7},{6,4},{7,9},{8,6},{9,11},{10,8},{11,... | collective-permute-start | bytes 98312 | tf_op jit(solution)/shard_map/ppermute | solution.py:305
  9.9 2.3 %collective-permute-start.1 = (bf16[16,1024]{1,0:T(8,128)(2,1)S(1)}, bf16[16,1024]{1,0:T(8,128)(2,1)S(1)}, u32[]{:S(2)}, u32[]{:S(2)}) collective-permute-start(bf16[16,1024]{1,0:T(8,128)(2,1)S(1)} %dynamic-slice_bitcast_fusion), channel_id=1, source_target_pairs={{1,2},{2,1},{3,4},{4,3},{5,6},{6,5},{7,8},{8,7},{9,10},{10,9},{11,... | collective-permute-start | bytes 98312 | tf_op jit(solution)/shard_map/ppermute | solution.py:304
  12.3 0.1 pad_add_fusion.place_ref
  12.3 5.4 %collective-permute-done.2.far_ref = bf16[16,1024]{1,0:T(8,128)(2,1)S(1)} collective-permute-done((bf16[16,1024]{1,0:T(8,128)(2,1)S(1)}, bf16[16,1024]{1,0:T(8,128)(2,1)S(1)}, u32[]{:S(2)}, u32[]{:S(2)}) %collective-permute-start.2) | collective-permute-done | bytes 32800 | tf_op jit(solution)/shard_map/ppermute | solution.py:305
  17.8 0.0 collective-permute-done.1.near_ref
  17.8 0.0 collective-permute-done.other_ref
  17.8 8.0 %activation.1.act_ref = bf16[1536,512]{1,0:T(8,128)(2,1)S(1)} custom-call(s32[4]{0:T(128)S(1)} %pad_add_fusion.place_ref, bf16[768,1024]{1,0:T(8,128)(2,1)} %bitcast.18, bf16[768,1024]{1,0:T(8,128)(2,1)S(1)} %collective-permute-done.other_ref, bf16[16,1024]{1,0:T(8,128)(2,1)S(1)} %collective-permute-done.1.near_ref, ...), custom_call_target="tpu_custom_call" | custom-call | tf_op jit(solution)/shard_map/activation/pallas_call | solution.py:127
  25.8 0.0 collective-permute-done.3.other_ref
  25.8 0.0 copy-done
  25.8 2.4 %product_kernel.1 = bf16[4,2,4,16,1024]{4,3,2,1,0:T(8,128)(2,1)S(1)} custom-call(s32[4]{0:T(128)S(1)} %pad_add_fusion.place_ref, bf16[1536,512]{1,0:T(8,128)(2,1)S(1)} %activation.1.act_ref, bf16[768,1024]{1,0:T(8,128)(2,1)S(1)} %bitcast.14, bf16[768,1024]{1,0:T(8,128)(2,1)S(1)} %collective-permute-done.3.other_ref), custom_call_target="tpu_custom_call" | custom-call | tf_op jit(solution)/shard_map/product_kernel/pallas_call | solution.py:276
  28.2 0.0 copy-start.1
  28.2 0.0 copy-start.2
  28.2 35.8 %all_to_all.25.parts_ref = bf16[32,16,1024]{2,1,0:T(8,128)(2,1)S(1)} all-to-all(bf16[32,16,1024]{2,1,0:T(8,128)(2,1)S(1)} %bitcast.12), channel_id=1, replica_groups={{0,2,4,6,9,11,13,15,16,18,20,22,25,27,29,31,32,34,36,38,41,43,45,47,48,..., dimensions={0} | all-to-all | bytes 2097152 | tf_op jit(solution)/shard_map/all_to_all | solution.py:287
  64.0 0.5 merge_kernel.1
  64.5 21.2 %all_to_all.26.parts_ref = f32[16,24,128]{2,1,0:T(8,128)S(1)} all-to-all(f32[16,24,128]{2,1,0:T(8,128)S(1)} %get-tuple-element.14), channel_id=1, replica_groups=mesh['x'=4,'h'=2,'y'=4,'z'=8,'c'=2] {'x','h','c'}, dimensions={0} | all-to-all | bytes 393216 | tf_op jit(solution)/shard_map/all_to_all | solution.py:287
  85.8 0.9 term_kernel.1
  86.6 9.0 %all_to_all.27.parts_ref = f32[4,40,128]{2,1,0:T(8,128)S(1)} all-to-all(f32[4,40,128]{2,1,0:T(8,128)S(1)} %get-tuple-element.15), channel_id=1, replica_groups=mesh['x'=4,'h'=2,'y'=4,'z'=8,'c'=2] {'y'}, dimensions={0} | all-to-all | bytes 163840 | tf_op jit(solution)/shard_map/all_to_all | solution.py:287
  95.7 10.9 %all_to_all.28.parts_ref = f32[8,40,128]{2,1,0:T(8,128)S(1)} all-to-all(f32[8,40,128]{2,1,0:T(8,128)S(1)} %total_kernel.2), channel_id=1, replica_groups=mesh['x'=4,'h'=2,'y'=4,'z'=8,'c'=2] {'z'}, dimensions={0} | all-to-all | bytes 327680 | tf_op jit(solution)/shard_map/all_to_all | solution.py:287
  106.6 5.0 %all_gather.3.halves_ref = f32[2,40,128]{2,1,0:T(8,128)S(1)} all-gather(f32[1,40,128]{2,1,0:T(8,128)S(1)} %total_kernel.3), channel_id=1, replica_groups=mesh['x'=4,'h'=2,'y'=4,'z'=8,'c'=2] {'c'}, dimensions={0}, use_global_device_ids=true | all-gather | bytes 61440 | tf_op jit(solution)/shard_map/all_gather | solution.py:349
  111.7 17.4 %all_to_all.29.rows_ref = f32[8,72,128]{2,1,0:T(8,128)S(1)} all-to-all(f32[8,72,128]{2,1,0:T(8,128)S(1)} %join_kernel.1), channel_id=1, replica_groups=mesh['x'=4,'h'=2,'y'=4,'z'=8,'c'=2] {'x','h'}, dimensions={0} | all-to-all | bytes 589824 | tf_op jit(solution)/shard_map/all_to_all | solution.py:287
  129.1 2.7 %finish_kernel.1 = (f32[64,1024]{1,0:T(8,128)}, f32[16,1024]{1,0:T(8,128)}, f32[16,1024]{1,0:T(8,128)}) custom-call(f32[8,72,128]{2,1,0:T(8,128)S(1)} %all_to_all.29.rows_ref, f32[16,64]{1,0:T(8,128)S(1)} %get-tuple-element.16.left_ref, f32[16,1024]{1,0:T(8,128)S(1)} %get-tuple-element.17.merged_ref), custom_call_target="tpu_custom_call" | custom-call | tf_op jit(solution)/shard_map/finish_kernel/pallas_call | solution.py:276
  (6 shorter events, 0.1 us)
Async XLA Ops:
  1.4 16.4 %collective-permute-start = (bf16[768,1024]{1,0:T(8,128)(2,1)}, bf16[768,1024]{1,0:T(8,128)(2,1)S(1)}, u32[]{:S(2)}, u32[]{:S(2)}) collective-permute-start(bf16[768,1024]{1,0:T(8,128)(2,1)} %bitcast.17), channel_id=1, source_target_pairs={{0,1},{1,0},{2,3},{3,2},{4,5},{5,4},{6,7},{7,6},{8,9},{9,8},{10,11... | collective-permute-start | bytes 4718600 | tf_op jit(solution)/shard_map/ppermute | solution.py:306
  4.0 21.8 %collective-permute-start.3 = (bf16[768,1024]{1,0:T(8,128)(2,1)}, bf16[768,1024]{1,0:T(8,128)(2,1)S(1)}, u32[]{:S(2)}, u32[]{:S(2)}) collective-permute-start(bf16[768,1024]{1,0:T(8,128)(2,1)} %bitcast.13), channel_id=1, source_target_pairs={{0,1},{1,0},{2,3},{3,2},{4,5},{5,4},{6,7},{7,6},{8,9},{9,8},{10,11... | collective-permute-start | bytes 4718600 | tf_op jit(solution)/shard_map/ppermute | solution.py:308
  5.9 11.9 %collective-permute-start.2 = (bf16[16,1024]{1,0:T(8,128)(2,1)S(1)}, bf16[16,1024]{1,0:T(8,128)(2,1)S(1)}, u32[]{:S(2)}, u32[]{:S(2)}) collective-permute-start(bf16[16,1024]{1,0:T(8,128)(2,1)S(1)} %dynamic-slice_bitcast_fusion), channel_id=1, source_target_pairs={{1,3},{2,0},{3,5},{4,2},{5,7},{6,4},{7,9},{8,6},{9,11},{10,8},{11,... | collective-permute-start | bytes 98312 | tf_op jit(solution)/shard_map/ppermute | solution.py:305
  9.9 7.8 %collective-permute-start.1 = (bf16[16,1024]{1,0:T(8,128)(2,1)S(1)}, bf16[16,1024]{1,0:T(8,128)(2,1)S(1)}, u32[]{:S(2)}, u32[]{:S(2)}) collective-permute-start(bf16[16,1024]{1,0:T(8,128)(2,1)S(1)} %dynamic-slice_bitcast_fusion), channel_id=1, source_target_pairs={{1,2},{2,1},{3,4},{4,3},{5,6},{6,5},{7,8},{8,7},{9,10},{10,9},{11,... | collective-permute-start | bytes 98312 | tf_op jit(solution)/shard_map/ppermute | solution.py:304
  12.3 13.4 %copy-start = (bf16[1,768,1024]{2,1,0:T(8,128)(2,1)S(1)}, bf16[1,768,1024]{2,1,0:T(8,128)(2,1)}, u32[]{:S(2)}) copy-start(bf16[1,768,1024]{2,1,0:T(8,128)(2,1)} %param.6) | copy-start | bytes 4718596
  28.2 35.9 %copy-start.1 = (f32[1024,64]{0,1:T(8,128)S(1)}, f32[1024,64]{0,1:T(8,128)}, u32[]{:S(2)}) copy-start(f32[1024,64]{0,1:T(8,128)} %param.9) | copy-start | bytes 786436
  28.2 35.8 %copy-start.2 = (f32[1,16,1024]{2,1,0:T(8,128)S(1)}, f32[1,16,1024]{2,1,0:T(8,128)}, u32[]{:S(2)}) copy-start(f32[1,16,1024]{2,1,0:T(8,128)} %param.8) | copy-start | bytes 196612
